TPU v7x, 512 devices: a whole 4x8x8 slice. The times are simulated.
512 devices in a mesh: group: 16 (over y, core), dev: 32 (over z, x).
Axes of the slice: x: 4, y: 8, z: 8, core: 2. Of those that a mesh axis runs over, the one named last changes fastest.
Arguments:
- prompt_cache: bfloat16 [16, 6144, 576], P('group', 'dev'), may hold values from -6 to 6
- prompt_of_group: int32 [16], replicated, may hold values from 0 to 15, each once
- queries: bfloat16 [16, 16, 4, 64, 576], P('group', None, None, 'dev'), may hold values from -12 to 12
- new_latents: bfloat16 [16, 16, 4, 576], P('group'), may hold values from -6 to 6
- value_up: bfloat16 [64, 512, 128], P('dev'), may hold values from -0.25 to 0.25
- out_weight: bfloat16 [8192, 7168], P('dev'), may hold values from -0.0625 to 0.0625
- norm_gain: bfloat16 [7168], replicated, may hold values from 0.099609375 to 1.8984375
- routes: int32 [1024, 8], P('group'), may hold values from 0 to 383, all different within a row; in each aligned block of 64 rows (0 to 63, 64 to 127, ...) at most 2 rows name the same one
- gates: float32 [1024, 8], P('group'), may hold values from 0.05 to 1
Outputs:
- slot_rows: float32 [16, 384, 2, 7168], P('group', 'dev')
- slot_gates: float32 [16, 384, 2], P('group', 'dev')
Inputs may be any that keep to these rules, and one draw needn't show every extreme that they name: `routes`: within each aligned block of 64 rows (one decode group) every expert is named by at most 2 rows, a bound that some block reaches; a row names 8 different experts. `prompt_of_group`: each prompt is served by exactly one decode group.
All inputs are finite; a program needn't handle non-finite values.
Results may differ from a plain program's by a relative error of at most 0.015.
Values may be sent and summed in bfloat16 or wider, within the bound.
No kernel may reach another device: no remote copies, remote signals or barrier semaphores. Data moves between devices by JAX's collectives and lax.ppermute only.
A program may use at most 64 MiB of HBM per device.

v0:
```python
import jax
import jax.numpy as jnp
from jax import lax
from jax.sharding import PartitionSpec as P

LAT_KV = 512
QK_DIM = 192
EXPERTS = 384
CAP = 2


EPSILON = 1e-06


def fold_keys(query_rows, partial_value, key_rows):
    best, totals, accum = partial_value
    scores = jnp.einsum(
        "rhc,nc->rhn", query_rows, key_rows, preferred_element_type=jnp.float32
    ) * QK_DIM ** (-0.5)
    new_best = jnp.maximum(best, jnp.max(scores, axis=-1))
    factor = jnp.exp(best - new_best)
    weights = jnp.exp(scores - new_best[..., None])
    totals = totals * factor + jnp.sum(weights, axis=-1)
    accum = accum * factor[..., None] + jnp.einsum(
        "rhn,nc->rhc",
        weights.astype(jnp.bfloat16),
        key_rows[:, :LAT_KV],
        preferred_element_type=jnp.float32,
    )
    return (new_best, totals, accum)


def own_partial(query_block, own_rows):
    samples, steps, heads, width = query_block.shape
    scores = jnp.einsum(
        "sthc,suc->sthu", query_block, own_rows, preferred_element_type=jnp.float32
    ) * QK_DIM ** (-0.5)
    steps_index = jnp.arange(steps, dtype=jnp.int32)
    visible = steps_index[None, :] <= steps_index[:, None]
    scores = jnp.where(visible[None, :, None, :], scores, -1e30)
    best = jnp.max(scores, axis=-1)
    weights = jnp.exp(scores - best[..., None])
    totals = jnp.sum(weights, axis=-1)
    accum = jnp.einsum(
        "sthu,suc->sthc",
        weights.astype(jnp.bfloat16),
        own_rows[..., :LAT_KV],
        preferred_element_type=jnp.float32,
    )
    row_count = samples * steps
    return (
        best.reshape(row_count, heads),
        totals.reshape(row_count, heads),
        accum.reshape(row_count, heads, LAT_KV),
    )


def rms_scale(rows, norm_gain):
    mean_square = jnp.mean(rows * rows, axis=-1, keepdims=True)
    return rows * lax.rsqrt(mean_square + EPSILON) * norm_gain.astype(jnp.float32)


def local(
    prompt_cache,
    prompt_of_group,
    queries,
    new_latents,
    value_up,
    out_weight,
    norm_gain,
    routes,
    gates,
):
    group_index = lax.axis_index("group")
    dev_index = lax.axis_index("dev")
    dev_count = lax.axis_size("dev")
    wanted = (prompt_of_group == group_index)[:, None, None]
    outgoing = jnp.where(wanted, prompt_cache, jnp.zeros_like(prompt_cache))
    arrived = lax.all_to_all(outgoing, "group", split_axis=0, concat_axis=0, tiled=True)
    cache_rows = lax.dynamic_index_in_dim(arrived, prompt_of_group[group_index], 0, keepdims=False)
    samples, steps, local_heads, width = queries.shape[1:]
    row_count = samples * steps
    local_queries = queries[0].reshape(row_count, local_heads, width)
    own_best, own_totals, own_accum = own_partial(queries[0], new_latents[0])
    best, totals, accum = fold_keys(
        local_queries,
        (own_best, own_totals, own_accum),
        lax.all_gather(cache_rows, "dev", axis=0, tiled=True),
    )
    latent_out = (accum / totals[..., None]).astype(jnp.bfloat16)
    head_values = jnp.einsum(
        "rhc,hcv->rhv", latent_out, value_up, preferred_element_type=jnp.float32
    ).astype(jnp.bfloat16)
    head_values = head_values.reshape(row_count, local_heads * value_up.shape[2])
    summed = lax.psum(jnp.dot(head_values, out_weight, preferred_element_type=jnp.float32), "dev")
    normed = rms_scale(summed, norm_gain)
    expert_count = EXPERTS // dev_count
    local_ids = routes - dev_index * expert_count
    matches = (
        local_ids[:, :, None] == jnp.arange(expert_count, dtype=jnp.int32)[None, None, :]
    ).astype(jnp.float32)
    chosen = jnp.sum(matches, axis=1)
    gating = jnp.sum(matches * gates[:, :, None], axis=1)
    position = jnp.cumsum(chosen, axis=0) - chosen
    slot_index = jnp.arange(CAP, dtype=jnp.float32)
    selected = chosen[:, :, None] * (position[:, :, None] == slot_index[None, None, :]).astype(
        jnp.float32
    )
    slot_rows = jnp.einsum("rec,rd->ecd", selected, normed, precision=lax.Precision.HIGHEST)
    slot_gates = jnp.einsum("rec,re->ec", selected, gating, precision=lax.Precision.HIGHEST)
    return (slot_rows[None], slot_gates[None])


def solution(mesh):
    return jax.shard_map(
        local,
        mesh=mesh,
        in_specs=(
            P("group", "dev", None),
            P(),
            P("group", None, None, "dev", None),
            P("group", None, None, None),
            P("dev", None, None),
            P("dev", None),
            P(),
            P("group", None),
            P("group", None),
        ),
        out_specs=(P("group", "dev", None, None), P("group", "dev", None)),
        check_vma=False,
    )
```

profile of v0, /device:TPU:8, one launch (start us, length us, event | category | flops | bytes accessed | tf_op | source)
XLA Modules:
  0.0 413.1 jit_solution(9053916580923141080)
XLA Ops:
  7.2 0.0 copy-start
  7.2 0.7 broadcast_compare_fusion
  7.9 3.3 broadcast_select_fusion
  11.2 0.0 copy-start.6
  11.2 0.0 copy-start.4
  11.2 10.2 %all-to-all-start = ((bf16[16,192,576]{2,1,0:T(8,128)(2,1)}), bf16[16,192,576]{2,1,0:T(8,128)(2,1)}, u32[]{:S(2)}, u32[]{:S(2)}) async-start(bf16[16,192,576]{2,1,0:T(8,128)(2,1)} %broadcast_select_fusion), calls=%async_computation | async-start | bytes 7864320 | tf_op jit(solution)/shard_map/all_to_all | solution.py:79
  21.4 0.0 all-gather.3.cloned.1.call-start
  21.4 0.0 copy-done.6
  21.4 0.6 dynamic_slice.7
  24.0 84.2 %all-to-all-done = bf16[16,192,576]{2,1,0:T(8,128)(2,1)} async-done(((bf16[16,192,576]{2,1,0:T(8,128)(2,1)}), bf16[16,192,576]{2,1,0:T(8,128)(2,1)}, u32[]{:S(2)}, u32[]{:S(2)}) %all-to-all-start) | async-done | bytes 3538976 | tf_op jit(solution)/shard_map/all_to_all | solution.py:79
  108.2 1.7 constant_dynamic-slice_fusion
  109.8 0.0 all-gather.3.cloned.1.call-update
  109.9 0.0 all-reduce.2.cloned.1.call-start
  109.9 0.0 copy-done.4
  109.9 0.0 copy-done.5
  109.9 0.3 fusion.31
  110.3 0.1 copy.72
  110.4 0.1 fusion.41
  110.5 0.1 copy.77
  110.6 0.1 reshape.84
  110.7 0.1 fusion.44
  110.8 0.1 copy.87
  110.9 0.1 copy.83
  111.0 0.1 reshape.85
  111.1 0.9 fusion.36
  112.0 101.4 %all-gather.3.cloned.1.call-done = bf16[1,6144,576]{2,1,0:T(8,128)(2,1)} async-done(((bf16[1,192,576]{2,1,0:T(8,128)(2,1)}), bf16[1,6144,576]{2,1,0:T(8,128)(2,1)}) %all-gather.3.cloned.1.call-update) | async-done | bytes 7077904 | tf_op jit(solution)/shard_map/all_gather | solution.py:88
  213.4 5.9 %fusion.48 = (f32[64,2]{0,1:T(2,128)S(1)}, f32[64,2,6144]{2,0,1:T(8,128)S(1)}) fusion(bf16[64,2,576]{2,1,0:T(2,128)(2,1)} %bitcast.67, bf16[1,6144,576]{2,1,0:T(8,128)(2,1)} %all-gather.3.cloned.1.call-done), kind=kOutput, calls=%fused_computation.55 | convolution fusion | flops 907542400 | bytes 10371584 | tf_op jit(solution)/shard_map/rhc,nc->rhn/dot_general | solution.py:17
  219.3 0.6 fusion.9
  219.9 10.3 %copy.78 = bf16[1,6144,576]{1,2,0:T(8,128)(2,1)} copy(bf16[1,6144,576]{2,1,0:T(8,128)(2,1)} %all-gather.3.cloned.1.call-done) | data formatting | bytes 14155776 | tf_op jit(solution)/shard_map/all_gather | solution.py:88
  230.2 0.0 copy-done
  230.2 5.1 %fusion.19 = bf16[2,8,8,128]{3,2,1,0:T(8,128)(2,1)S(1)} fusion(bf16[2,512,128]{2,1,0:T(8,128)(2,1)S(1)} %copy-done, bf16[6144,576]{0,1:T(8,128)(2,1)} %bitcast.63, f32[64,2,6144]{2,0,1:T(8,128)S(1)} %get-tuple-element.19, f32[64,2]{0,1:T(2,128)S(1)} %max.13, f32[64,2,512]{2,1,0:T(2,128)} %bitcast.69, f32[64,2]{0,1:T(2,128)S(1)} %get-tuple-element.14, ...), kind=kOutput, calls=%fused_computation.18 | convolution fusion | flops 823934976 | bytes 9995776 | tf_op jit(solution)/shard_map/rhc,hcv->rhv/dot_general | solution.py:91
  235.4 0.0 copy-start.1
  235.4 0.0 copy-start.2
  235.4 0.0 copy-start.3
  235.4 4.0 fusion.37
  239.4 0.0 all-reduce.2.cloned.1.call-update
  239.5 0.0 copy-done.1
  239.5 0.0 copy-done.2
  239.5 0.0 copy-done.3
  239.6 0.1 copy.69
  239.7 0.1 reduce_window_sum.11
  239.8 0.1 copy.71
  239.9 0.2 fusion.42
  240.1 0.7 copy.93
  240.7 159.7 %all-reduce.2.cloned.1.call-done = f32[64,7168]{1,0:T(8,128)} async-done(((f32[64,7168]{1,0:T(8,128)}), f32[64,7168]{1,0:T(8,128)}) %all-reduce.2.cloned.1.call-update) | async-done | bytes 1835024 | tf_op jit(solution)/shard_map/psum | solution.py:95
  400.4 1.7 multiply_reduce_fusion
  402.2 2.7 convolution_bitcast_fusion
  404.9 1.4 copy.85
  (10 shorter events, 0.1 us)
Async XLA Ops:
  7.2 223.1 %copy-start = (bf16[2,512,128]{2,1,0:T(8,128)(2,1)S(1)}, bf16[2,512,128]{2,1,0:T(8,128)(2,1)}, u32[]{:S(2)}) copy-start(bf16[2,512,128]{2,1,0:T(8,128)(2,1)} %param.13) | copy-start | bytes 786436
  11.2 10.3 %copy-start.6 = (s32[16]{0:T(128)S(1)}, s32[16]{0:T(128)}, u32[]{:S(2)}) copy-start(s32[16]{0:T(128)} %param.10) | copy-start | bytes 196
  11.2 98.8 %copy-start.4 = (bf16[1,16,4,2,576]{4,3,2,1,0:T(2,128)(2,1)S(1)}, bf16[1,16,4,2,576]{4,3,2,1,0:T(2,128)(2,1)}, u32[]{:S(2)}) copy-start(bf16[1,16,4,2,576]{4,3,2,1,0:T(2,128)(2,1)} %param.11) | copy-start | bytes 442372
  11.2 98.8 %copy-start.5 = (bf16[1,16,4,576]{3,2,1,0:T(4,128)(2,1)S(1)}, bf16[1,16,4,576]{3,2,1,0:T(4,128)(2,1)}, u32[]{:S(2)}) copy-start(bf16[1,16,4,576]{3,2,1,0:T(4,128)(2,1)} %param.12) | copy-start | bytes 221188
  11.2 97.0 %all-to-all-start = ((bf16[16,192,576]{2,1,0:T(8,128)(2,1)}), bf16[16,192,576]{2,1,0:T(8,128)(2,1)}, u32[]{:S(2)}, u32[]{:S(2)}) async-start(bf16[16,192,576]{2,1,0:T(8,128)(2,1)} %broadcast_select_fusion), calls=%async_computation | async-start | bytes 7864320 | tf_op jit(solution)/shard_map/all_to_all | solution.py:79
  21.4 192.1 %all-gather.3.cloned.1.call-start = ((), (), s32[]{:S(2)}) async-start(), calls=%async_computation.2 | async-start | bytes 8110080 | tf_op jit(solution)/shard_map/all_gather | solution.py:88
  109.9 290.6 %all-reduce.2.cloned.1.call-start = ((), (), s32[]{:S(2)}) async-start(), calls=%async_computation.1 | async-start | bytes 3670016 | tf_op jit(solution)/shard_map/psum | solution.py:95
  235.4 4.1 copy-start.1
  235.4 4.1 copy-start.2
  235.4 4.1 copy-start.3
Sparse Core Ops, SparseCore 0:
  110.0 103.4 all-gather.2
  239.6 160.8 all-reduce.1
where the time goes:
time: 414 us; the launch traced here: 413 us
  waiting for transfers between devices  345 us (83%)
  matrix products  19.2 us (5%)
  between operations  16.1 us (4%)
  local copies, waits for them, and re-layouts  15.4 us (4%)
  starting transfers between devices  10.3 us (2%)
  other arithmetic  6.66 us (2%)
    psum x1, waiting for transfers between devices, local(): lax.psum(jnp.dot(head_values, out_weight, preferred_element_type=jnp.floa...  160 us
    all_gather x1, waiting for transfers between devices, local(): lax.all_gather(cache_rows, 'dev', axis=0, tiled=True)  101 us
    all_to_all x1, waiting for transfers between devices, local(): lax.all_to_all(outgoing, 'group', split_axis=0, concat_axis=0, tiled=True)  84.2 us
    all_gather x1, local copies, waits for them, and re-layouts, local(): lax.all_gather(cache_rows, 'dev', axis=0, tiled=True)  10.3 us
    all_to_all x1, starting transfers between devices, local(): lax.all_to_all(outgoing, 'group', split_axis=0, concat_axis=0, tiled=True)  10.2 us
  transfers between devices with their start and end apart: 3, of which 3 were waited for; matrix products, arithmetic and copies ran while one was open for 1% of the time, Pallas kernels for 0%

commit v1 on v0

v1 whole, which is shorter than its diff:
```python
import jax
import jax.numpy as jnp
from jax import lax
from jax.experimental import pallas as pl
from jax.experimental.pallas import tpu as pltpu
from jax.sharding import Mesh
from jax.sharding import PartitionSpec as P

D = 7168
LAT = 576
LAT_KV = 512
HEAD_V = 128
QK_DIM = 192
EXPERTS = 384
CAP = 2
ROWS = 64
EPSILON = 1e-06
SCALE = QK_DIM ** (-0.5)

NY, NZ, NX = 8, 8, 4
DEVS = NZ * NX
PIECE = 192 // NY
KEYS = 192 * NX
MINE = 2 * ROWS
SENT = MINE + 16
SLOTS = EXPERTS * CAP
OWN_SLOTS = SLOTS // DEVS
QUARTER = D // NX
BLOCK = 256
BLOCKS = QUARTER // BLOCK

bf16 = jnp.bfloat16
f32 = jnp.float32
VMEM = pl.BlockSpec(memory_space=pltpu.VMEM)
SMEM = pl.BlockSpec(memory_space=pltpu.SMEM)


def params():
    return pltpu.CompilerParams(vmem_limit_bytes=48 * 1024 * 1024)


def dot(a, b, dims=((1,), (0,))):
    return lax.dot_general(a, b, (dims, ((), ())), preferred_element_type=f32)


def columns_to_lanes(column):
    return jnp.transpose(jnp.broadcast_to(column, (MINE, 128)))[:1]


def pick_kernel(wanted, mine, other, out):
    core = wanted[8]
    for y in range(NY):
        prompt = wanted[y]
        row = lax.shift_right_logical(prompt, 1)

        @pl.when((prompt & 1) == core)
        def _():
            out[y] = mine[row]

        @pl.when((prompt & 1) != core)
        def _():
            out[y] = other[row]


def pick(wanted, mine, other):
    return pl.pallas_call(
        pick_kernel,
        out_shape=jax.ShapeDtypeStruct(mine.shape, mine.dtype),
        in_specs=[SMEM, VMEM, VMEM],
        out_specs=VMEM,
        compiler_params=params(),
        name="pick",
    )(wanted, mine, other)


def attend(query, keys, visible=None):
    scores = dot(query, keys, ((1,), (1,))) * SCALE
    if visible is not None:
        scores = jnp.where(visible, scores, -1e30)
    best = jnp.max(scores, axis=1, keepdims=True)
    weights = jnp.exp(scores - best)
    total = jnp.sum(weights, axis=1, keepdims=True)
    latent = dot(weights.astype(bf16), keys[:, :LAT_KV]) / total
    return best, total, latent.astype(bf16)


def three(value):
    high = value.astype(bf16).astype(f32)
    rest = value - high
    mid = rest.astype(bf16).astype(f32)
    return high, mid, rest - mid


def attention_kernel(query, keys, value_up, out):
    best, total, latent = attend(query[0], keys[...])
    for head in range(2):
        values = dot(latent[head * ROWS : (head + 1) * ROWS], value_up[0, head])
        out[0, head * ROWS : (head + 1) * ROWS, :] = values.astype(bf16)
    parts = three(columns_to_lanes(best)) + three(columns_to_lanes(total))
    index = lax.broadcasted_iota(jnp.int32, (16, 128), 0)
    stats = jnp.zeros((16, 128), f32)
    for i, part in enumerate(parts):
        stats = jnp.where(index == i, jnp.broadcast_to(part, (16, 128)), stats)
    out[0, MINE:, :] = stats.astype(bf16)


def prompt_attention(queries, keys, value_up):
    return pl.pallas_call(
        attention_kernel,
        grid=(NZ,),
        out_shape=jax.ShapeDtypeStruct((NZ, SENT, 128), bf16),
        in_specs=[
            pl.BlockSpec((1, MINE, LAT), lambda z: (z, 0, 0)),
            pl.BlockSpec((KEYS, LAT), lambda z: (0, 0)),
            pl.BlockSpec((1, 2, LAT_KV, HEAD_V), lambda z: (z, 0, 0, 0)),
        ],
        out_specs=pl.BlockSpec((1, SENT, 128), lambda z: (z, 0, 0)),
        compiler_params=params(),
        name="prompt_attention",
    )(queries, keys, value_up)


def own_kernel(query, keys, value_up, values, stats):
    row = lax.broadcasted_iota(jnp.int32, (MINE, ROWS), 0) & (ROWS - 1)
    key = lax.broadcasted_iota(jnp.int32, (MINE, ROWS), 1)
    same = lax.shift_right_logical(row, 2) == lax.shift_right_logical(key, 2)
    best, total, latent = attend(query[...], keys[...], same & (key <= row))
    for head in range(2):
        part = slice(head * ROWS, (head + 1) * ROWS)
        values[part, :] = dot(latent[part], value_up[head])
    index = lax.broadcasted_iota(jnp.int32, (8, 128), 0)
    stats[...] = jnp.where(
        index == 0,
        jnp.broadcast_to(columns_to_lanes(best), (8, 128)),
        jnp.broadcast_to(columns_to_lanes(total), (8, 128)),
    )


def own_attention(query, keys, value_up):
    return pl.pallas_call(
        own_kernel,
        out_shape=(
            jax.ShapeDtypeStruct((MINE, HEAD_V), f32),
            jax.ShapeDtypeStruct((8, 128), f32),
        ),
        in_specs=[VMEM] * 3,
        out_specs=(VMEM, VMEM),
        compiler_params=params(),
        name="own_attention",
    )(query, keys, value_up)


def combine_kernel(arrived, own_values, own_stats, out):
    bests, totals = [own_stats[0:1, :]], [own_stats[1:2, :]]
    for z in range(NZ):
        stats = arrived[z, MINE:, :].astype(f32)
        bests.append(stats[0:1] + stats[1:2] + stats[2:3])
        totals.append(stats[3:4] + stats[4:5] + stats[5:6])
    top = bests[0]
    for best in bests[1:]:
        top = jnp.maximum(top, best)
    shares = [total * jnp.exp(best - top) for best, total in zip(bests, totals)]
    whole = shares[0]
    for share in shares[1:]:
        whole = whole + share
    index = lax.broadcasted_iota(jnp.int32, (128, 128), 0)
    table = jnp.zeros((128, 128), f32)
    for i, share in enumerate(shares):
        table = jnp.where(index == i, jnp.broadcast_to(share / whole, (128, 128)), table)
    table = jnp.transpose(table)
    values = table[:, 0:1] * own_values[...]
    for z in range(NZ):
        values = values + table[:, z + 1 : z + 2] * arrived[z, :MINE, :].astype(f32)
    values = values.astype(bf16)
    for x in range(NX):
        out[x, :, :HEAD_V] = values[:ROWS]
        out[x, :, HEAD_V:] = values[ROWS:]


def combine(arrived, own_values, own_stats):
    return pl.pallas_call(
        combine_kernel,
        out_shape=jax.ShapeDtypeStruct((NX, ROWS, 2 * HEAD_V), bf16),
        in_specs=[VMEM] * 3,
        out_specs=VMEM,
        compiler_params=params(),
        name="combine",
    )(arrived, own_values, own_stats)


def project_kernel(head_values, weight, out):
    @pl.when(pl.program_id(0) < BLOCKS)
    def _():
        total = dot(head_values[0], weight[0])
        for x in range(1, NX):
            total = total + dot(head_values[x], weight[x])
        out[0] = total.astype(bf16)

    @pl.when(pl.program_id(0) >= BLOCKS)
    def _():
        out[0] = jnp.zeros((ROWS, BLOCK), bf16)


def project(head_values, weight):
    return pl.pallas_call(
        project_kernel,
        grid=(NZ,),
        out_shape=jax.ShapeDtypeStruct((NZ, ROWS, BLOCK), bf16),
        in_specs=[
            pl.BlockSpec((NX, ROWS, 2 * HEAD_V), lambda z: (0, 0, 0)),
            pl.BlockSpec((NX, 2 * HEAD_V, BLOCK), lambda z: (0, 0, jnp.minimum(z, BLOCKS - 1))),
        ],
        out_specs=pl.BlockSpec((1, ROWS, BLOCK), lambda z: (z, 0, 0)),
        compiler_params=params(),
        name="project",
    )(head_values, weight)


def slots_kernel(routes, gates, picks, slot_gates):
    slot = lax.broadcasted_iota(jnp.int32, (SLOTS, ROWS), 0)
    expert = lax.shift_right_logical(slot, 1)
    chosen = jnp.zeros((SLOTS, ROWS), f32)
    gating = jnp.zeros((SLOTS, ROWS), f32)
    for k in range(8):
        match = expert == routes[k : k + 1, :]
        chosen = jnp.where(match, 1.0, chosen)
        gating = jnp.where(match, gates[k : k + 1, :], gating)
    earlier = lax.broadcasted_iota(jnp.int32, (ROWS, ROWS), 0) < lax.broadcasted_iota(
        jnp.int32, (ROWS, ROWS), 1
    )
    position = dot(chosen.astype(bf16), jnp.where(earlier, 1.0, 0.0).astype(bf16))
    place = (slot & 1).astype(f32)
    selected = jnp.where(position == place, chosen, 0.0)
    picks[...] = selected.astype(bf16)
    slot_gates[...] = jnp.sum(selected * gating, axis=1, keepdims=True)


def slots(routes, gates):
    return pl.pallas_call(
        slots_kernel,
        out_shape=(
            jax.ShapeDtypeStruct((SLOTS, ROWS), bf16),
            jax.ShapeDtypeStruct((SLOTS, 1), f32),
        ),
        in_specs=[VMEM] * 2,
        out_specs=(VMEM, VMEM),
        compiler_params=params(),
        name="slots",
    )(routes, gates)


def dispatch_kernel(arrived, picks, out):
    total = arrived[0].astype(f32)
    for z in range(1, NZ):
        total = total + arrived[z].astype(f32)
    out[...] = dot(picks[...], total.astype(bf16)).astype(bf16)


def dispatch(arrived, picks):
    return pl.pallas_call(
        dispatch_kernel,
        out_shape=jax.ShapeDtypeStruct((SLOTS, BLOCK), bf16),
        in_specs=[VMEM] * 2,
        out_specs=VMEM,
        compiler_params=params(),
        name="dispatch",
    )(arrived, picks)


def norm_kernel(arrived, gain, out):
    blocks = []
    for x in range(NX):
        for z in range(BLOCKS):
            blocks.append(arrived[z * NX + x].astype(f32))
    square = blocks[0] * blocks[0]
    for block in blocks[1:]:
        square = square + block * block
    scale = lax.rsqrt(jnp.sum(square, axis=1, keepdims=True) * (1.0 / D) + EPSILON)
    for i, block in enumerate(blocks):
        part = slice(i * BLOCK, (i + 1) * BLOCK)
        normed = block * scale * gain[:, part].astype(f32)
        for expert in range(OWN_SLOTS // CAP):
            out[expert, :, part] = normed[expert * CAP : (expert + 1) * CAP]


def norm(arrived, gain):
    return pl.pallas_call(
        norm_kernel,
        out_shape=jax.ShapeDtypeStruct((OWN_SLOTS // CAP, CAP, D), f32),
        in_specs=[VMEM] * 2,
        out_specs=VMEM,
        compiler_params=params(),
        name="norm",
    )(arrived, gain)


def exchange(value, axes):
    return lax.all_to_all(value, axes, split_axis=0, concat_axis=0, tiled=True)


def local(
    prompt_cache,
    prompt_of_group,
    queries,
    new_latents,
    value_up,
    out_weight,
    norm_gain,
    routes,
    gates,
):
    core = lax.axis_index("core")
    dev = lax.axis_index("z") * NX + lax.axis_index("x")

    pieces = exchange(prompt_cache.reshape(NY, PIECE, LAT), "y")
    other = lax.ppermute(pieces, "core", [(0, 1), (1, 0)])
    own_prompts = jnp.where(core == 0, prompt_of_group[0::2], prompt_of_group[1::2])
    wanted = jnp.concatenate([own_prompts, core[None].astype(jnp.int32)])
    served = exchange(pick(wanted, pieces, other), "y").reshape(NY * PIECE, LAT)
    keys = lax.all_gather(served, "x", axis=0, tiled=True)

    query = queries.reshape(ROWS, 2, LAT).transpose(1, 0, 2).reshape(MINE, LAT)
    all_queries = exchange(jnp.broadcast_to(query, (NZ, MINE, LAT)), "z")
    all_value_up = lax.all_gather(
        value_up.reshape(2 * LAT_KV, HEAD_V), "z", axis=0, tiled=True
    ).reshape(NZ, 2, LAT_KV, HEAD_V)
    weight = exchange(out_weight.reshape(2 * HEAD_V, NX, QUARTER).transpose(1, 0, 2), "x")
    own_values, own_stats = own_attention(query, new_latents.reshape(ROWS, LAT), value_up)
    picks, all_gates = slots(routes.T, gates.T)
    slot_gates = lax.dynamic_slice_in_dim(all_gates, dev * OWN_SLOTS, OWN_SLOTS, 0)

    partial = exchange(prompt_attention(all_queries, keys, all_value_up), "z")
    head_values = exchange(combine(partial, own_values, own_stats), "x")
    sums = exchange(project(head_values, weight), "z")
    rows = dispatch(sums, picks).reshape(DEVS, OWN_SLOTS, BLOCK)
    slot_rows = norm(exchange(rows, ("z", "x")), norm_gain.reshape(1, D))
    return (slot_rows[None], slot_gates.reshape(1, OWN_SLOTS // CAP, CAP))


def solution(mesh):
    fine = Mesh(mesh.devices.reshape(NY, 2, NZ, NX), ("y", "core", "z", "x"))
    group, dev = ("y", "core"), ("z", "x")
    return jax.shard_map(
        local,
        mesh=fine,
        in_specs=(
            P(group, dev, None),
            P(),
            P(group, None, None, dev, None),
            P(group, None, None, None),
            P(dev, None, None),
            P(dev, None),
            P(),
            P(group, None),
            P(group, None),
        ),
        out_specs=(P(group, dev, None, None), P(group, dev, None)),
        check_vma=False,
    )
```

time: 414 us -> 223 us (0.54)
  the two profiles are of different devices: /device:TPU:8 before, /device:TPU:2 now
where the time goes in v1:
time: 223 us; the launch traced here: 222 us
  waiting for transfers between devices  102 us (46%)
  starting transfers between devices  42.3 us (19%)
  blocking collectives  23.4 us (10%)
  Pallas kernels  20 us (9%)
  local copies, waits for them, and re-layouts  19.8 us (9%)
  between operations  14.2 us (6%)
    all_to_all x7, waiting for transfers between devices, exchange(): return lax.all_to_all(value, axes, split_axis=0, concat_axis=0, tiled=True)  100 us
    all_to_all x7, starting transfers between devices, exchange(): return lax.all_to_all(value, axes, split_axis=0, concat_axis=0, tiled=True)  40.4 us
    all_gather x1, blocking collectives, local(): keys = lax.all_gather(served, 'x', axis=0, tiled=True)  15 us
    pallas_call x1, Pallas kernels, prompt_attention(): pl.pallas_call(attention_kernel, grid=(NZ,), out_shape=jax.ShapeDtypeStru...  9.1 us
    all_to_all x1, blocking collectives, exchange(): return lax.all_to_all(value, axes, split_axis=0, concat_axis=0, tiled=True)  8.35 us
    unnamed x14, local copies, waits for them, and re-layouts  8.18 us
    reshape x1, local copies, waits for them, and re-layouts, local(): out_weight.reshape(2 * HEAD_V, NX, QUARTER).transpose(1, 0, 2)  5.92 us
    pallas_call x1, Pallas kernels, project(): pl.pallas_call(project_kernel, grid=(NZ,), out_shape=jax.ShapeDtypeStruct...  5.8 us
  transfers between devices with their start and end apart: 9, of which 8 were waited for; matrix products, arithmetic and copies ran while one was open for 8% of the time, Pallas kernels for 1%

profile of v1, /device:TPU:2, one launch (start us, length us, event | category | flops | bytes accessed | tf_op | source)
XLA Modules:
  0.0 222.2 jit_solution(1769969980364045141)
XLA Ops:
  7.2 0.0 all-gather.2.cloned.1.call-start
  7.2 0.7 all-gather.2.cloned.1.call-update
  7.9 7.1 %all-to-all-start.1 = ((bf16[8,24,576]{2,1,0:T(8,128)(2,1)}), bf16[8,24,576]{2,1,0:T(8,128)(2,1)S(1)}, u32[]{:S(2)}, u32[]{:S(2)}) async-start(bf16[8,24,576]{2,1,0:T(8,128)(2,1)} %bitcast.25), calls=%async_computation.1 | async-start | bytes 491520 | tf_op jit(solution)/shard_map/all_to_all | solution.py:298
  15.0 0.7 slice.6
  15.8 0.7 slice.7
  16.5 10.0 %all-to-all-done.1.mine = bf16[8,24,576]{2,1,0:T(8,128)(2,1)S(1)} async-done(((bf16[8,24,576]{2,1,0:T(8,128)(2,1)}), bf16[8,24,576]{2,1,0:T(8,128)(2,1)S(1)}, u32[]{:S(2)}, u32[]{:S(2)}) %all-to-all-start.1) | async-done | bytes 221216 | tf_op jit(solution)/shard_map/all_to_all | solution.py:298
  26.5 1.9 collective-permute-start
  28.5 0.1 pad_add_fusion.wanted
  28.5 1.4 collective-permute-done.other
  29.9 1.4 pick.1
  31.3 3.4 %all-to-all-start.2 = ((bf16[8,24,576]{2,1,0:T(8,128)(2,1)}), bf16[8,24,576]{2,1,0:T(8,128)(2,1)S(1)}, u32[]{:S(2)}, u32[]{:S(2)}) async-start(bf16[8,24,576]{2,1,0:T(8,128)(2,1)} %pick.1), calls=%async_computation.2 | async-start | bytes 491520 | tf_op jit(solution)/shard_map/all_to_all | solution.py:298
  34.7 0.9 copy.17
  35.6 0.1 copy.18
  35.8 10.9 %all-to-all-done.2 = bf16[8,24,576]{2,1,0:T(8,128)(2,1)S(1)} async-done(((bf16[8,24,576]{2,1,0:T(8,128)(2,1)}), bf16[8,24,576]{2,1,0:T(8,128)(2,1)S(1)}, u32[]{:S(2)}, u32[]{:S(2)}) %all-to-all-start.2) | async-done | bytes 221216 | tf_op jit(solution)/shard_map/all_to_all | solution.py:298
  46.7 1.2 broadcast_in_dim.9
  47.9 10.3 %all-to-all-start = ((bf16[8,128,576]{1,2,0:T(8,128)(2,1)}), bf16[8,128,576]{1,2,0:T(8,128)(2,1)}, u32[]{:S(2)}, u32[]{:S(2)}) async-start(bf16[8,128,576]{1,2,0:T(8,128)(2,1)} %broadcast_in_dim.9), calls=%async_computation | async-start | bytes 2359296 | tf_op jit(solution)/shard_map/all_to_all | solution.py:298
  58.2 15.0 %all_gather.6.keys = bf16[768,576]{1,0:T(8,128)(2,1)S(1)} all-gather(bf16[192,576]{1,0:T(8,128)(2,1)S(1)} %bitcast.23), channel_id=1, replica_groups=mesh['y'=8,'core'=2,'z'=8,'x'=4] {'x'}, dimensions={0}, use_global_device_ids=true | all-gather | bytes 1105920 | tf_op jit(solution)/shard_map/all_gather | solution.py:320
  73.2 16.8 %all-to-all-done = bf16[8,128,576]{1,2,0:T(8,128)(2,1)} async-done(((bf16[8,128,576]{1,2,0:T(8,128)(2,1)}), bf16[8,128,576]{1,2,0:T(8,128)(2,1)}, u32[]{:S(2)}, u32[]{:S(2)}) %all-to-all-start) | async-done | bytes 1179680 | tf_op jit(solution)/shard_map/all_to_all | solution.py:298
  90.1 1.7 copy.19.query
  91.8 0.0 all-gather.2.cloned.1.call-done
  91.8 0.0 copy-start
  91.8 1.6 copy-done
  93.4 9.1 %prompt_attention.1 = bf16[8,144,128]{2,1,0:T(8,128)(2,1)} custom-call(bf16[8,128,576]{2,1,0:T(8,128)(2,1)S(1)} %copy.19.query, bf16[768,576]{1,0:T(8,128)(2,1)S(1)} %all_gather.6.keys, bf16[8,2,512,128]{3,2,1,0:T(8,128)(2,1)S(1)} %bitcast.15), custom_call_target="tpu_custom_call" | custom-call | tf_op jit(solution)/shard_map/prompt_attention/pallas_call | solution.py:108
  102.5 3.4 %all-to-all-start.3 = ((bf16[8,144,128]{2,1,0:T(8,128)(2,1)}), bf16[8,144,128]{2,1,0:T(8,128)(2,1)S(1)}, u32[]{:S(2)}, u32[]{:S(2)}) async-start(bf16[8,144,128]{2,1,0:T(8,128)(2,1)} %prompt_attention.1), calls=%async_computation.3 | async-start | bytes 589824 | tf_op jit(solution)/shard_map/all_to_all | solution.py:298
  105.9 5.9 %copy.20 = bf16[256,7168]{0,1:T(8,128)(2,1)} copy(bf16[256,7168]{1,0:T(8,128)(2,1)} %param.14) | data formatting | bytes 7340032 | tf_op args[5]
  111.8 5.9 %copy.21 = bf16[256,4,1792]{2,0,1:T(8,128)(2,1)} copy(bf16[256,4,1792]{0,2,1:T(8,128)(2,1)} %bitcast.22) | data formatting | bytes 7340032 | tf_op jit(solution)/shard_map/reshape | solution.py:327
  117.7 1.1 all-to-all-done.3.arrived
  118.9 5.4 %all-to-all-start.5 = ((bf16[4,256,1792]{2,1,0:T(8,128)(2,1)}), bf16[4,256,1792]{2,1,0:T(8,128)(2,1)}, u32[]{:S(2)}, u32[]{:S(2)}) async-start(bf16[4,256,1792]{2,1,0:T(8,128)(2,1)} %bitcast.21), calls=%async_computation.5 | async-start | bytes 7340032 | tf_op jit(solution)/shard_map/all_to_all | solution.py:298
  124.2 0.0 copy-done.4
  124.3 0.0 copy-done.1
  124.3 0.0 copy-start.5
  124.3 0.6 own_attention.1
  124.9 0.4 combine.1
  125.3 41.2 %all-to-all-done.5.weight = bf16[4,256,1792]{2,1,0:T(8,128)(2,1)} async-done(((bf16[4,256,1792]{2,1,0:T(8,128)(2,1)}), bf16[4,256,1792]{2,1,0:T(8,128)(2,1)}, u32[]{:S(2)}, u32[]{:S(2)}) %all-to-all-start.5) | async-done | bytes 3670048 | tf_op jit(solution)/shard_map/all_to_all | solution.py:298
  166.5 8.3 %all_to_all.40.head_values = bf16[4,64,256]{2,1,0:T(8,128)(2,1)S(1)} all-to-all(bf16[4,64,256]{2,1,0:T(8,128)(2,1)S(1)} %combine.1), channel_id=1, replica_groups=mesh['y'=8,'core'=2,'z'=8,'x'=4] {'x'}, dimensions={0} | all-to-all | bytes 262144 | tf_op jit(solution)/shard_map/all_to_all | solution.py:298
  174.9 5.8 %project.1 = bf16[8,64,256]{2,1,0:T(8,128)(2,1)} custom-call(bf16[4,64,256]{2,1,0:T(8,128)(2,1)S(1)} %all_to_all.40.head_values, bf16[4,256,1792]{2,1,0:T(8,128)(2,1)} %all-to-all-done.5.weight), custom_call_target="tpu_custom_call" | custom-call | tf_op jit(solution)/shard_map/project/pallas_call | solution.py:205
  180.7 5.8 %all-to-all-start.6 = ((bf16[8,64,256]{2,1,0:T(8,128)(2,1)}), bf16[8,64,256]{2,1,0:T(8,128)(2,1)S(1)}, u32[]{:S(2)}, u32[]{:S(2)}) async-start(bf16[8,64,256]{2,1,0:T(8,128)(2,1)} %project.1), calls=%async_computation.6 | async-start | bytes 524288 | tf_op jit(solution)/shard_map/all_to_all | solution.py:298
  186.4 0.0 copy-done.2
  186.4 0.6 slots.1
  187.1 9.8 %all-to-all-done.6.arrived = bf16[8,64,256]{2,1,0:T(8,128)(2,1)S(1)} async-done(((bf16[8,64,256]{2,1,0:T(8,128)(2,1)}), bf16[8,64,256]{2,1,0:T(8,128)(2,1)S(1)}, u32[]{:S(2)}, u32[]{:S(2)}) %all-to-all-start.6) | async-done | bytes 262176 | tf_op jit(solution)/shard_map/all_to_all | solution.py:298
  196.9 1.0 dispatch.1
  197.9 5.0 %all-to-all-start.7 = ((bf16[32,24,256]{2,1,0:T(8,128)(2,1)}), bf16[32,24,256]{2,1,0:T(8,128)(2,1)S(1)}, u32[]{:S(2)}, u32[]{:S(2)}) async-start(bf16[32,24,256]{2,1,0:T(8,128)(2,1)} %bitcast.13), calls=%async_computation.7 | async-start | bytes 786432 | tf_op jit(solution)/shard_map/all_to_all | solution.py:298
  202.9 0.0 copy-done.5
  202.9 0.1 dynamic-slice_reduce_fusion
  203.1 0.1 reshape.47
  203.1 0.7 copy.22
  203.8 10.4 %all-to-all-done.7.arrived = bf16[32,24,256]{2,1,0:T(8,128)(2,1)S(1)} async-done(((bf16[32,24,256]{2,1,0:T(8,128)(2,1)}), bf16[32,24,256]{2,1,0:T(8,128)(2,1)S(1)}, u32[]{:S(2)}, u32[]{:S(2)}) %all-to-all-start.7) | async-done | bytes 393248 | tf_op jit(solution)/shard_map/all_to_all | solution.py:298
  214.2 1.1 norm.1
  (8 shorter events, 0.1 us)
Async XLA Ops:
  7.2 84.6 %all-gather.2.cloned.1.call-start = ((), (), s32[]{:S(2)}) async-start(), calls=%async_computation.8 | async-start | bytes 2359296 | tf_op jit(solution)/shard_map/all_gather | solution.py:324
  7.9 18.6 %all-to-all-start.1 = ((bf16[8,24,576]{2,1,0:T(8,128)(2,1)}), bf16[8,24,576]{2,1,0:T(8,128)(2,1)S(1)}, u32[]{:S(2)}, u32[]{:S(2)}) async-start(bf16[8,24,576]{2,1,0:T(8,128)(2,1)} %bitcast.25), calls=%async_computation.1 | async-start | bytes 491520 | tf_op jit(solution)/shard_map/all_to_all | solution.py:298
  26.5 3.4 %collective-permute-start = (bf16[8,24,576]{2,1,0:T(8,128)(2,1)S(1)}, bf16[8,24,576]{2,1,0:T(8,128)(2,1)S(1)}, u32[]{:S(2)}, u32[]{:S(2)}) collective-permute-start(bf16[8,24,576]{2,1,0:T(8,128)(2,1)S(1)} %all-to-all-done.1.mine), channel_id=1, source_target_pairs={{0,32},{32,0},{1,33},{33,1},{2,34},{34,2},{3,35},{35,3},{4,36},{36... | collective-permute-start | bytes 663560 | tf_op jit(solution)/shard_map/ppermute | solution.py:316
  31.3 15.4 %all-to-all-start.2 = ((bf16[8,24,576]{2,1,0:T(8,128)(2,1)}), bf16[8,24,576]{2,1,0:T(8,128)(2,1)S(1)}, u32[]{:S(2)}, u32[]{:S(2)}) async-start(bf16[8,24,576]{2,1,0:T(8,128)(2,1)} %pick.1), calls=%async_computation.2 | async-start | bytes 491520 | tf_op jit(solution)/shard_map/all_to_all | solution.py:298
  47.9 42.2 %all-to-all-start = ((bf16[8,128,576]{1,2,0:T(8,128)(2,1)}), bf16[8,128,576]{1,2,0:T(8,128)(2,1)}, u32[]{:S(2)}, u32[]{:S(2)}) async-start(bf16[8,128,576]{1,2,0:T(8,128)(2,1)} %broadcast_in_dim.9), calls=%async_computation | async-start | bytes 2359296 | tf_op jit(solution)/shard_map/all_to_all | solution.py:298
  91.8 1.6 copy-start
  102.5 16.4 %all-to-all-start.3 = ((bf16[8,144,128]{2,1,0:T(8,128)(2,1)}), bf16[8,144,128]{2,1,0:T(8,128)(2,1)S(1)}, u32[]{:S(2)}, u32[]{:S(2)}) async-start(bf16[8,144,128]{2,1,0:T(8,128)(2,1)} %prompt_attention.1), calls=%async_computation.3 | async-start | bytes 589824 | tf_op jit(solution)/shard_map/all_to_all | solution.py:298
  118.9 5.4 %copy-start.4 = (bf16[1,16,4,576]{3,2,1,0:T(4,128)(2,1)S(1)}, bf16[1,16,4,576]{3,2,1,0:T(4,128)(2,1)}, u32[]{:S(2)}) copy-start(bf16[1,16,4,576]{3,2,1,0:T(4,128)(2,1)} %param.12) | copy-start | bytes 221188
  118.9 5.4 %copy-start.1 = (bf16[2,512,128]{2,1,0:T(8,128)(2,1)S(1)}, bf16[2,512,128]{2,1,0:T(8,128)(2,1)}, u32[]{:S(2)}) copy-start(bf16[2,512,128]{2,1,0:T(8,128)(2,1)} %value_up.1) | copy-start | bytes 786436
  118.9 47.6 %all-to-all-start.5 = ((bf16[4,256,1792]{2,1,0:T(8,128)(2,1)}), bf16[4,256,1792]{2,1,0:T(8,128)(2,1)}, u32[]{:S(2)}, u32[]{:S(2)}) async-start(bf16[4,256,1792]{2,1,0:T(8,128)(2,1)} %bitcast.21), calls=%async_computation.5 | async-start | bytes 7340032 | tf_op jit(solution)/shard_map/all_to_all | solution.py:298
  124.2 62.2 %copy-start.2 = (s32[64,8]{0,1:T(8,128)S(1)}, s32[64,8]{0,1:T(8,128)}, u32[]{:S(2)}) copy-start(s32[64,8]{0,1:T(8,128)} %param.16) | copy-start | bytes 6148
  124.2 62.2 %copy-start.3 = (f32[64,8]{0,1:T(8,128)S(1)}, f32[64,8]{0,1:T(8,128)}, u32[]{:S(2)}) copy-start(f32[64,8]{0,1:T(8,128)} %param.17) | copy-start | bytes 6148
  124.3 78.6 %copy-start.5 = (bf16[7168]{0:T(1024)(128)(2,1)S(1)}, bf16[7168]{0:T(1024)(128)(2,1)}, u32[]{:S(2)}) copy-start(bf16[7168]{0:T(1024)(128)(2,1)} %param.15) | copy-start | bytes 43012
  180.7 16.2 %all-to-all-start.6 = ((bf16[8,64,256]{2,1,0:T(8,128)(2,1)}), bf16[8,64,256]{2,1,0:T(8,128)(2,1)S(1)}, u32[]{:S(2)}, u32[]{:S(2)}) async-start(bf16[8,64,256]{2,1,0:T(8,128)(2,1)} %project.1), calls=%async_computation.6 | async-start | bytes 524288 | tf_op jit(solution)/shard_map/all_to_all | solution.py:298
  197.9 16.3 %all-to-all-start.7 = ((bf16[32,24,256]{2,1,0:T(8,128)(2,1)}), bf16[32,24,256]{2,1,0:T(8,128)(2,1)S(1)}, u32[]{:S(2)}, u32[]{:S(2)}) async-start(bf16[32,24,256]{2,1,0:T(8,128)(2,1)} %bitcast.13), calls=%async_computation.7 | async-start | bytes 786432 | tf_op jit(solution)/shard_map/all_to_all | solution.py:298
Sparse Core Ops, SparseCore 0:
  10.1 49.2 all-gather.1

commit v2 on v1

--- a/solution.py
+++ b/solution.py
@@ -28,6 +28,9 @@
 QUARTER = D // NX
 BLOCK = 256
 BLOCKS = QUARTER // BLOCK
+TILES = -(-LAT // 128)
+PACKED = TILES * MINE + LAT_KV
+STEP = 4
 
 bf16 = jnp.bfloat16
 f32 = jnp.float32
@@ -36,7 +39,7 @@
 
 
 def params():
-    return pltpu.CompilerParams(vmem_limit_bytes=48 * 1024 * 1024)
+    return pltpu.CompilerParams(vmem_limit_bytes=24 * 1024 * 1024)
 
 
 def dot(a, b, dims=((1,), (0,))):
@@ -91,33 +94,118 @@
     return high, mid, rest - mid
 
 
-def attention_kernel(query, keys, value_up, out):
-    best, total, latent = attend(query[0], keys[...])
-    for head in range(2):
-        values = dot(latent[head * ROWS : (head + 1) * ROWS], value_up[0, head])
-        out[0, head * ROWS : (head + 1) * ROWS, :] = values.astype(bf16)
-    parts = three(columns_to_lanes(best)) + three(columns_to_lanes(total))
+def pack_kernel(core, query, value_up, out):
+    for tile in range(TILES):
+        width = min(128, LAT - tile * 128)
+        part = query[:, tile * 128 : tile * 128 + width]
+        if width < 128:
+            part = jnp.concatenate([part, jnp.zeros((MINE, 128 - width), bf16)], axis=1)
+        out[tile * MINE : (tile + 1) * MINE, :] = part
+    out[TILES * MINE :, :] = value_up[core[0]]
+
+
+def pack(core, query, value_up):
+    return pl.pallas_call(
+        pack_kernel,
+        out_shape=jax.ShapeDtypeStruct((PACKED, 128), bf16),
+        in_specs=[SMEM, VMEM, VMEM],
+        out_specs=VMEM,
+        compiler_params=params(),
+        name="pack",
+    )(core, query, value_up)
+
+
+def attention_kernel(packed, keys, latents, stats):
     index = lax.broadcasted_iota(jnp.int32, (16, 128), 0)
-    stats = jnp.zeros((16, 128), f32)
-    for i, part in enumerate(parts):
-        stats = jnp.where(index == i, jnp.broadcast_to(part, (16, 128)), stats)
-    out[0, MINE:, :] = stats.astype(bf16)
-
-
-def prompt_attention(queries, keys, value_up):
+    for step in range(NZ // STEP):
+        zs = range(step * STEP, (step + 1) * STEP)
+        query = jnp.concatenate(
+            [
+                jnp.concatenate(
+                    [packed[z, tile * MINE : (tile + 1) * MINE, :] for tile in range(TILES)], axis=1
+                )
+                for z in zs
+            ],
+            axis=0,
+        )[:, :LAT]
+        best, total, latent = attend(query, keys[...])
+        for i, z in enumerate(zs):
+            part = slice(i * MINE, (i + 1) * MINE)
+            latents[z] = latent[part]
+            rows = three(columns_to_lanes(best[part])) + three(columns_to_lanes(total[part]))
+            table = jnp.zeros((16, 128), f32)
+            for j, row in enumerate(rows):
+                table = jnp.where(index == j, jnp.broadcast_to(row, (16, 128)), table)
+            stats[z] = table.astype(bf16)
+
+
+def prompt_attention(packed, keys):
     return pl.pallas_call(
         attention_kernel,
-        grid=(NZ,),
+        out_shape=(
+            jax.ShapeDtypeStruct((NZ, MINE, LAT_KV), bf16),
+            jax.ShapeDtypeStruct((NZ, 16, 128), bf16),
+        ),
+        in_specs=[VMEM] * 2,
+        out_specs=(VMEM, VMEM),
+        compiler_params=params(),
+        name="prompt_attention",
+    )(packed, keys)
+
+
+def up_kernel(core, latents, stats, mine, other, out):
+    for z in range(NZ):
+        out[z, MINE:, :] = stats[z]
+
+    def apply(first, second):
+        for z in range(NZ):
+            out[z, :ROWS, :] = dot(latents[z, :ROWS], first(z)).astype(bf16)
+            out[z, ROWS:MINE, :] = dot(latents[z, ROWS:], second(z)).astype(bf16)
+
+    @pl.when(core[0] == 0)
+    def _():
+        apply(lambda z: mine[z, TILES * MINE :, :], lambda z: other[z])
+
+    @pl.when(core[0] != 0)
+    def _():
+        apply(lambda z: other[z], lambda z: mine[z, TILES * MINE :, :])
+
+
+def up_project(core, latents, stats, mine, other):
+    return pl.pallas_call(
+        up_kernel,
         out_shape=jax.ShapeDtypeStruct((NZ, SENT, 128), bf16),
-        in_specs=[
-            pl.BlockSpec((1, MINE, LAT), lambda z: (z, 0, 0)),
-            pl.BlockSpec((KEYS, LAT), lambda z: (0, 0)),
-            pl.BlockSpec((1, 2, LAT_KV, HEAD_V), lambda z: (z, 0, 0, 0)),
-        ],
-        out_specs=pl.BlockSpec((1, SENT, 128), lambda z: (z, 0, 0)),
-        compiler_params=params(),
-        name="prompt_attention",
-    )(queries, keys, value_up)
+        in_specs=[SMEM] + [VMEM] * 4,
+        out_specs=VMEM,
+        compiler_params=params(),
+        name="up_project",
+    )(core, latents, stats, mine, other)
+
+
+def turn_kernel(x, weight, *refs):
+    outs, sems = refs[:NX], refs[NX]
+    copies = []
+    for k in range(NX):
+        start = pl.multiple_of(((x[0] + k) & (NX - 1)) * QUARTER, 128)
+        copies.append(
+            pltpu.make_async_copy(weight.at[:, pl.ds(start, QUARTER)], outs[k], sems.at[k])
+        )
+    for copy in copies:
+        copy.start()
+    for copy in copies:
+        copy.wait()
+
+
+def turn(x, weight):
+    return pl.pallas_call(
+        turn_kernel,
+        out_shape=[jax.ShapeDtypeStruct((2 * HEAD_V, QUARTER), bf16)] * NX,
+        in_specs=[SMEM, pl.BlockSpec(memory_space=pl.ANY)],
+        out_specs=[pl.BlockSpec(memory_space=pl.ANY)] * NX,
+        scratch_shapes=[pltpu.SemaphoreType.DMA((NX,))],
+        compiler_params=params(),
+        name="turn",
+    )(x, weight)
 
 
 def own_kernel(query, keys, value_up, values, stats):
@@ -188,32 +276,28 @@
     )(arrived, own_values, own_stats)
 
 
-def project_kernel(head_values, weight, out):
-    @pl.when(pl.program_id(0) < BLOCKS)
-    def _():
-        total = dot(head_values[0], weight[0])
-        for x in range(1, NX):
-            total = total + dot(head_values[x], weight[x])
-        out[0] = total.astype(bf16)
-
-    @pl.when(pl.program_id(0) >= BLOCKS)
-    def _():
-        out[0] = jnp.zeros((ROWS, BLOCK), bf16)
-
-
-def project(head_values, weight):
+def project_kernel(x, head_values, *refs):
+    weights, out = refs[:NX], refs[NX]
+    rows = [head_values[(x[0] + NX - k) & (NX - 1)] for k in range(NX)]
+    for block in range(BLOCKS):
+        part = slice(block * BLOCK, (block + 1) * BLOCK)
+        total = dot(rows[0], weights[0][:, part])
+        for k in range(1, NX):
+            total = total + dot(rows[k], weights[k][:, part])
+        out[block] = total.astype(bf16)
+    for block in range(BLOCKS, NZ):
+        out[block] = jnp.zeros((ROWS, BLOCK), bf16)
+
+
+def project(x, head_values, weights):
     return pl.pallas_call(
         project_kernel,
-        grid=(NZ,),
         out_shape=jax.ShapeDtypeStruct((NZ, ROWS, BLOCK), bf16),
-        in_specs=[
-            pl.BlockSpec((NX, ROWS, 2 * HEAD_V), lambda z: (0, 0, 0)),
-            pl.BlockSpec((NX, 2 * HEAD_V, BLOCK), lambda z: (0, 0, jnp.minimum(z, BLOCKS - 1))),
-        ],
-        out_specs=pl.BlockSpec((1, ROWS, BLOCK), lambda z: (z, 0, 0)),
+        in_specs=[SMEM] + [VMEM] * (1 + NX),
+        out_specs=VMEM,
         compiler_params=params(),
         name="project",
-    )(head_values, weight)
+    )(x, head_values, *weights)
 
 
 def slots_kernel(routes, gates, picks, slot_gates):
@@ -320,18 +404,23 @@
     keys = lax.all_gather(served, "x", axis=0, tiled=True)
 
     query = queries.reshape(ROWS, 2, LAT).transpose(1, 0, 2).reshape(MINE, LAT)
-    all_queries = exchange(jnp.broadcast_to(query, (NZ, MINE, LAT)), "z")
-    all_value_up = lax.all_gather(
-        value_up.reshape(2 * LAT_KV, HEAD_V), "z", axis=0, tiled=True
-    ).reshape(NZ, 2, LAT_KV, HEAD_V)
-    weight = exchange(out_weight.reshape(2 * HEAD_V, NX, QUARTER).transpose(1, 0, 2), "x")
+    core = core[None].astype(jnp.int32)
+    x = lax.axis_index("x")[None].astype(jnp.int32)
+    packed = lax.all_gather(pack(core, query, value_up), "z", axis=0, tiled=True)
+    packed = packed.reshape(NZ, PACKED, 128)
+    other_up = lax.ppermute(packed[:, TILES * MINE :, :], "core", [(0, 1), (1, 0)])
+    weights = turn(x, out_weight)
+    weights = [weights[0]] + [
+        lax.ppermute(weights[k], "x", [(i, (i + k) % NX) for i in range(NX)]) for k in range(1, NX)
+    ]
     own_values, own_stats = own_attention(query, new_latents.reshape(ROWS, LAT), value_up)
     picks, all_gates = slots(routes.T, gates.T)
     slot_gates = lax.dynamic_slice_in_dim(all_gates, dev * OWN_SLOTS, OWN_SLOTS, 0)
 
-    partial = exchange(prompt_attention(all_queries, keys, all_value_up), "z")
+    latents, stats = prompt_attention(packed, keys)
+    partial = exchange(up_project(core, latents, stats, packed, other_up), "z")
     head_values = exchange(combine(partial, own_values, own_stats), "x")
-    sums = exchange(project(head_values, weight), "z")
+    sums = exchange(project(x, head_values, weights), "z")
     rows = dispatch(sums, picks).reshape(DEVS, OWN_SLOTS, BLOCK)
     slot_rows = norm(exchange(rows, ("z", "x")), norm_gain.reshape(1, D))
     return (slot_rows[None], slot_gates.reshape(1, OWN_SLOTS // CAP, CAP))

time: 223 us -> 213 us (0.955)
  the two profiles are of different devices: /device:TPU:2 before, /device:TPU:8 now
where the time goes in v2:
time: 213 us; the launch traced here: 212 us
  waiting for transfers between devices  75.6 us (35%)
  starting transfers between devices  47.7 us (22%)
  blocking collectives  46.6 us (22%)
  Pallas kernels  17 us (8%)
  between operations  14.2 us (7%)
  local copies, waits for them, and re-layouts  10.9 us (5%)
    all_gather x1, blocking collectives, local(): keys = lax.all_gather(served, 'x', axis=0, tiled=True)  46.6 us
    all_to_all x6, waiting for transfers between devices, exchange(): return lax.all_to_all(value, axes, split_axis=0, concat_axis=0, tiled=True)  45 us
    all_to_all x6, starting transfers between devices, exchange(): return lax.all_to_all(value, axes, split_axis=0, concat_axis=0, tiled=True)  32.5 us
    all_gather x1, waiting for transfers between devices, local(): lax.all_gather(pack(core, query, value_up), 'z', axis=0, tiled=True)  30.5 us
    ppermute x3, starting transfers between devices, local(): lax.ppermute(weights[k], 'x', [(i, (i + k) % NX) for i in range(NX)])  11.3 us
    unnamed x21, local copies, waits for them, and re-layouts  5.82 us
  transfers between devices with their start and end apart: 12, of which 6 were waited for; matrix products, arithmetic and copies ran while one was open for 2% of the time, Pallas kernels for 5%

profile of v2, /device:TPU:8, one launch (start us, length us, event | category | flops | bytes accessed | tf_op | source)
XLA Modules:
  0.0 212.1 jit_solution(7024389225790591793)
XLA Ops:
  7.2 0.0 all-gather.2.cloned.1.call-start
  7.2 0.9 copy.13
  8.2 0.0 copy-start.2
  8.2 0.9 copy-done.2
  9.1 0.8 pack.1
  9.9 0.0 all-gather.2.cloned.1.call-update
  9.9 9.1 %all-to-all-start = ((bf16[8,24,576]{2,1,0:T(8,128)(2,1)}), bf16[8,24,576]{2,1,0:T(8,128)(2,1)S(1)}, u32[]{:S(2)}, u32[]{:S(2)}) async-start(bf16[8,24,576]{2,1,0:T(8,128)(2,1)} %bitcast.22), calls=%async_computation | async-start | bytes 491520 | tf_op jit(solution)/shard_map/all_to_all | solution.py:382
  19.0 0.7 slice.10
  19.8 0.7 slice.9
  20.5 7.4 %all-to-all-done.mine = bf16[8,24,576]{2,1,0:T(8,128)(2,1)S(1)} async-done(((bf16[8,24,576]{2,1,0:T(8,128)(2,1)}), bf16[8,24,576]{2,1,0:T(8,128)(2,1)S(1)}, u32[]{:S(2)}, u32[]{:S(2)}) %all-to-all-start) | async-done | bytes 221216 | tf_op jit(solution)/shard_map/all_to_all | solution.py:382
  27.9 1.9 collective-permute-start
  29.8 30.5 %all-gather.2.cloned.1.call-done = bf16[9216,128]{1,0:T(8,128)(2,1)} async-done(((bf16[1152,128]{1,0:T(8,128)(2,1)}), bf16[9216,128]{1,0:T(8,128)(2,1)}) %all-gather.2.cloned.1.call-update) | async-done | bytes 2359312 | tf_op jit(solution)/shard_map/all_gather | solution.py:409
  60.4 2.4 %slice.12 = bf16[8,512,128]{2,1,0:T(8,128)(2,1)} slice(bf16[8,1152,128]{2,1,0:T(8,128)(2,1)} %bitcast.13), slice={[0:8], [640:1152], [0:128]} | slice | bytes 2097152 | tf_op jit(solution)/shard_map/slice | solution.py:411
  62.8 1.9 collective-permute-start.1
  64.7 0.1 pad_add_fusion.wanted
  64.8 0.0 collective-permute-done.other
  64.8 1.4 pick.1
  66.2 7.3 %all-to-all-start.1 = ((bf16[8,24,576]{2,1,0:T(8,128)(2,1)}), bf16[8,24,576]{2,1,0:T(8,128)(2,1)S(1)}, u32[]{:S(2)}, u32[]{:S(2)}) async-start(bf16[8,24,576]{2,1,0:T(8,128)(2,1)} %pick.1), calls=%async_computation.1 | async-start | bytes 491520 | tf_op jit(solution)/shard_map/all_to_all | solution.py:382
  73.4 2.0 copy-done.1
  75.5 1.7 turn.1
  77.2 1.0 copy-done.4
  78.1 3.4 %collective-permute-start.2 = (bf16[256,1792]{1,0:T(8,128)(2,1)}, bf16[256,1792]{1,0:T(8,128)(2,1)}, u32[]{:S(2)}, u32[]{:S(2)}) collective-permute-start(bf16[256,1792]{1,0:T(8,128)(2,1)} %get-tuple-element.17), channel_id=1, source_target_pairs={{0,1},{1,2},{2,3},{3,0},{4,5},{5,6},{6,7},{7,4},{8,9},{9,10},{10,1... | collective-permute-start | bytes 2752520 | tf_op jit(solution)/shard_map/ppermute | solution.py:414
  81.5 4.6 %collective-permute-start.3 = (bf16[256,1792]{1,0:T(8,128)(2,1)}, bf16[256,1792]{1,0:T(8,128)(2,1)}, u32[]{:S(2)}, u32[]{:S(2)}) collective-permute-start(bf16[256,1792]{1,0:T(8,128)(2,1)} %get-tuple-element.18), channel_id=1, source_target_pairs={{0,2},{1,3},{2,0},{3,1},{4,6},{5,7},{6,4},{7,5},{8,10},{9,11},{10,... | collective-permute-start | bytes 2752520 | tf_op jit(solution)/shard_map/ppermute | solution.py:414
  86.1 3.4 %collective-permute-start.4 = (bf16[256,1792]{1,0:T(8,128)(2,1)}, bf16[256,1792]{1,0:T(8,128)(2,1)}, u32[]{:S(2)}, u32[]{:S(2)}) collective-permute-start(bf16[256,1792]{1,0:T(8,128)(2,1)} %get-tuple-element.19), channel_id=1, source_target_pairs={{0,3},{1,0},{2,1},{3,2},{4,7},{5,4},{6,5},{7,6},{8,11},{9,8},{10,9... | collective-permute-start | bytes 2752520 | tf_op jit(solution)/shard_map/ppermute | solution.py:414
  89.5 46.6 %all_gather.7.keys = bf16[768,576]{1,0:T(8,128)(2,1)S(1)} all-gather(bf16[192,576]{1,0:T(8,128)(2,1)S(1)} %bitcast.20), channel_id=1, replica_groups=mesh['y'=8,'core'=2,'z'=8,'x'=4] {'x'}, dimensions={0}, use_global_device_ids=true | all-gather | bytes 1105920 | tf_op jit(solution)/shard_map/all_gather | solution.py:404
  136.1 3.2 %prompt_attention.1 = (bf16[8,128,512]{2,1,0:T(8,128)(2,1)S(1)}, bf16[8,16,128]{2,1,0:T(8,128)(2,1)S(1)}) custom-call(bf16[8,1152,128]{2,1,0:T(8,128)(2,1)S(1)} %bitcast.14, bf16[768,576]{1,0:T(8,128)(2,1)S(1)} %all_gather.7.keys), custom_call_target="tpu_custom_call" | custom-call | tf_op jit(solution)/shard_map/prompt_attention/pallas_call | solution.py:143
  139.3 2.4 %up_project.1 = bf16[8,144,128]{2,1,0:T(8,128)(2,1)} custom-call(s32[1]{0:T(128)} %bitcast.1.core, bf16[8,128,512]{2,1,0:T(8,128)(2,1)S(1)} %get-tuple-element.12.latents, bf16[8,16,128]{2,1,0:T(8,128)(2,1)S(1)} %get-tuple-element.13.stats, bf16[8,1152,128]{2,1,0:T(8,128)(2,1)S(1)} %bitcast.15, bf16[8,512,128]{2,1,0:T(8,128)(2,1)} %collective-permute-done.1.other), custom_call_target="tpu_custom_call" | custom-call | tf_op jit(solution)/shard_map/up_project/pallas_call | solution.py:175
  141.7 4.6 %all-to-all-start.2 = ((bf16[8,144,128]{2,1,0:T(8,128)(2,1)}), bf16[8,144,128]{2,1,0:T(8,128)(2,1)S(1)}, u32[]{:S(2)}, u32[]{:S(2)}) async-start(bf16[8,144,128]{2,1,0:T(8,128)(2,1)} %up_project.1), calls=%async_computation.2 | async-start | bytes 589824 | tf_op jit(solution)/shard_map/all_to_all | solution.py:382
  146.3 0.0 copy-start.9
  146.3 0.6 own_attention.1
  146.9 10.2 %all-to-all-done.2.arrived = bf16[8,144,128]{2,1,0:T(8,128)(2,1)S(1)} async-done(((bf16[8,144,128]{2,1,0:T(8,128)(2,1)}), bf16[8,144,128]{2,1,0:T(8,128)(2,1)S(1)}, u32[]{:S(2)}, u32[]{:S(2)}) %all-to-all-start.2) | async-done | bytes 294944 | tf_op jit(solution)/shard_map/all_to_all | solution.py:382
  157.1 1.1 combine.1
  158.2 4.3 %all-to-all-start.3 = ((bf16[4,64,256]{2,1,0:T(8,128)(2,1)}), bf16[4,64,256]{2,1,0:T(8,128)(2,1)S(1)}, u32[]{:S(2)}, u32[]{:S(2)}) async-start(bf16[4,64,256]{2,1,0:T(8,128)(2,1)} %combine.1), calls=%async_computation.3 | async-start | bytes 262144 | tf_op jit(solution)/shard_map/all_to_all | solution.py:382
  162.4 0.0 collective-permute-done.2.refs_1_
  162.4 0.0 collective-permute-done.3.refs_2_
  162.4 6.0 %all-to-all-done.3.head_values = bf16[4,64,256]{2,1,0:T(8,128)(2,1)S(1)} async-done(((bf16[4,64,256]{2,1,0:T(8,128)(2,1)}), bf16[4,64,256]{2,1,0:T(8,128)(2,1)S(1)}, u32[]{:S(2)}, u32[]{:S(2)}) %all-to-all-start.3) | async-done | bytes 131104 | tf_op jit(solution)/shard_map/all_to_all | solution.py:382
  168.4 1.2 copy-done.5
  169.6 3.2 %project.1 = bf16[8,64,256]{2,1,0:T(8,128)(2,1)} custom-call(s32[1]{0:T(128)} %bitcast.x, bf16[4,64,256]{2,1,0:T(8,128)(2,1)S(1)} %all-to-all-done.3.head_values, bf16[256,1792]{1,0:T(8,128)(2,1)S(1)} %copy-done.5, bf16[256,1792]{1,0:T(8,128)(2,1)} %collective-permute-done.2.refs_1_, bf16[256,1792]{1,0:T(8,128)(2,1)} %collective-permute-done.3.refs_2_, ...), custom_call_target="tpu_custom_call" | custom-call | tf_op jit(solution)/shard_map/project/pallas_call | solution.py:293
  172.8 3.4 %all-to-all-start.4 = ((bf16[8,64,256]{2,1,0:T(8,128)(2,1)}), bf16[8,64,256]{2,1,0:T(8,128)(2,1)S(1)}, u32[]{:S(2)}, u32[]{:S(2)}) async-start(bf16[8,64,256]{2,1,0:T(8,128)(2,1)} %project.1), calls=%async_computation.4 | async-start | bytes 524288 | tf_op jit(solution)/shard_map/all_to_all | solution.py:382
  176.2 0.6 slots.1
  176.8 9.7 %all-to-all-done.4.arrived = bf16[8,64,256]{2,1,0:T(8,128)(2,1)S(1)} async-done(((bf16[8,64,256]{2,1,0:T(8,128)(2,1)}), bf16[8,64,256]{2,1,0:T(8,128)(2,1)S(1)}, u32[]{:S(2)}, u32[]{:S(2)}) %all-to-all-start.4) | async-done | bytes 262176 | tf_op jit(solution)/shard_map/all_to_all | solution.py:382
  186.6 1.0 dispatch.1
  187.6 3.9 %all-to-all-start.5 = ((bf16[32,24,256]{2,1,0:T(8,128)(2,1)}), bf16[32,24,256]{2,1,0:T(8,128)(2,1)S(1)}, u32[]{:S(2)}, u32[]{:S(2)}) async-start(bf16[32,24,256]{2,1,0:T(8,128)(2,1)} %bitcast.11), calls=%async_computation.5 | async-start | bytes 786432 | tf_op jit(solution)/shard_map/all_to_all | solution.py:382
  191.5 0.1 dynamic-slice_reduce_fusion
  191.6 0.1 reshape.39
  191.7 0.7 copy.14
  192.4 11.7 %all-to-all-done.5.arrived = bf16[32,24,256]{2,1,0:T(8,128)(2,1)S(1)} async-done(((bf16[32,24,256]{2,1,0:T(8,128)(2,1)}), bf16[32,24,256]{2,1,0:T(8,128)(2,1)S(1)}, u32[]{:S(2)}, u32[]{:S(2)}) %all-to-all-start.5) | async-done | bytes 393248 | tf_op jit(solution)/shard_map/all_to_all | solution.py:382
  204.1 1.1 norm.1
  (20 shorter events, 0.1 us)
Async XLA Ops:
  7.2 53.2 %all-gather.2.cloned.1.call-start = ((), (), s32[]{:S(2)}) async-start(), calls=%async_computation.6 | async-start | bytes 2654208 | tf_op jit(solution)/shard_map/all_gather | solution.py:409
  8.2 1.0 copy-start.2
  9.9 18.0 %all-to-all-start = ((bf16[8,24,576]{2,1,0:T(8,128)(2,1)}), bf16[8,24,576]{2,1,0:T(8,128)(2,1)S(1)}, u32[]{:S(2)}, u32[]{:S(2)}) async-start(bf16[8,24,576]{2,1,0:T(8,128)(2,1)} %bitcast.22), calls=%async_computation | async-start | bytes 491520 | tf_op jit(solution)/shard_map/all_to_all | solution.py:382
  27.9 36.9 %collective-permute-start = (bf16[8,24,576]{2,1,0:T(8,128)(2,1)S(1)}, bf16[8,24,576]{2,1,0:T(8,128)(2,1)S(1)}, u32[]{:S(2)}, u32[]{:S(2)}) collective-permute-start(bf16[8,24,576]{2,1,0:T(8,128)(2,1)S(1)} %all-to-all-done.mine), channel_id=1, source_target_pairs={{0,32},{32,0},{1,33},{33,1},{2,34},{34,2},{3,35},{35,3},{4,36},{36... | collective-permute-start | bytes 663560 | tf_op jit(solution)/shard_map/ppermute | solution.py:400
  60.4 75.7 %copy-start = (bf16[9216,128]{1,0:T(8,128)(2,1)S(1)}, bf16[9216,128]{1,0:T(8,128)(2,1)}, u32[]{:S(2)}) copy-start(bf16[9216,128]{1,0:T(8,128)(2,1)} %all-gather.2.cloned.1.call-done) | copy-start | bytes 7077892
  62.8 76.5 %collective-permute-start.1 = (bf16[8,512,128]{2,1,0:T(8,128)(2,1)}, bf16[8,512,128]{2,1,0:T(8,128)(2,1)}, u32[]{:S(2)}, u32[]{:S(2)}) collective-permute-start(bf16[8,512,128]{2,1,0:T(8,128)(2,1)} %slice.12), channel_id=1, source_target_pairs={{0,32},{32,0},{1,33},{33,1},{2,34},{34,2},{3,35},{35,3},{4,36},{36... | collective-permute-start | bytes 3145736 | tf_op jit(solution)/shard_map/ppermute | solution.py:411
  66.2 23.3 %all-to-all-start.1 = ((bf16[8,24,576]{2,1,0:T(8,128)(2,1)}), bf16[8,24,576]{2,1,0:T(8,128)(2,1)S(1)}, u32[]{:S(2)}, u32[]{:S(2)}) async-start(bf16[8,24,576]{2,1,0:T(8,128)(2,1)} %pick.1), calls=%async_computation.1 | async-start | bytes 491520 | tf_op jit(solution)/shard_map/all_to_all | solution.py:382
  73.4 2.0 copy-start.1
  77.2 1.0 copy-start.4
  78.1 84.3 %collective-permute-start.2 = (bf16[256,1792]{1,0:T(8,128)(2,1)}, bf16[256,1792]{1,0:T(8,128)(2,1)}, u32[]{:S(2)}, u32[]{:S(2)}) collective-permute-start(bf16[256,1792]{1,0:T(8,128)(2,1)} %get-tuple-element.17), channel_id=1, source_target_pairs={{0,1},{1,2},{2,3},{3,0},{4,5},{5,6},{6,7},{7,4},{8,9},{9,10},{10,1... | collective-permute-start | bytes 2752520 | tf_op jit(solution)/shard_map/ppermute | solution.py:414
  81.5 80.9 %collective-permute-start.3 = (bf16[256,1792]{1,0:T(8,128)(2,1)}, bf16[256,1792]{1,0:T(8,128)(2,1)}, u32[]{:S(2)}, u32[]{:S(2)}) collective-permute-start(bf16[256,1792]{1,0:T(8,128)(2,1)} %get-tuple-element.18), channel_id=1, source_target_pairs={{0,2},{1,3},{2,0},{3,1},{4,6},{5,7},{6,4},{7,5},{8,10},{9,11},{10,... | collective-permute-start | bytes 2752520 | tf_op jit(solution)/shard_map/ppermute | solution.py:414
  86.1 76.3 %collective-permute-start.4 = (bf16[256,1792]{1,0:T(8,128)(2,1)}, bf16[256,1792]{1,0:T(8,128)(2,1)}, u32[]{:S(2)}, u32[]{:S(2)}) collective-permute-start(bf16[256,1792]{1,0:T(8,128)(2,1)} %get-tuple-element.19), channel_id=1, source_target_pairs={{0,3},{1,0},{2,1},{3,2},{4,7},{5,4},{6,5},{7,6},{8,11},{9,8},{10,9... | collective-permute-start | bytes 2752520 | tf_op jit(solution)/shard_map/ppermute | solution.py:414
  136.1 10.2 %copy-start.8 = (bf16[1,16,4,576]{3,2,1,0:T(4,128)(2,1)S(1)}, bf16[1,16,4,576]{3,2,1,0:T(4,128)(2,1)}, u32[]{:S(2)}) copy-start(bf16[1,16,4,576]{3,2,1,0:T(4,128)(2,1)} %param.12) | copy-start | bytes 221188
  136.1 10.2 %copy-start.3 = (bf16[2,512,128]{2,1,0:T(8,128)(2,1)S(1)}, bf16[2,512,128]{2,1,0:T(8,128)(2,1)}, u32[]{:S(2)}) copy-start(bf16[2,512,128]{2,1,0:T(8,128)(2,1)} %value_up.3) | copy-start | bytes 786436
  141.7 34.5 %copy-start.6 = (s32[64,8]{0,1:T(8,128)S(1)}, s32[64,8]{0,1:T(8,128)}, u32[]{:S(2)}) copy-start(s32[64,8]{0,1:T(8,128)} %param.16) | copy-start | bytes 6148
  141.7 34.5 %copy-start.7 = (f32[64,8]{0,1:T(8,128)S(1)}, f32[64,8]{0,1:T(8,128)}, u32[]{:S(2)}) copy-start(f32[64,8]{0,1:T(8,128)} %param.17) | copy-start | bytes 6148
  141.7 15.4 %all-to-all-start.2 = ((bf16[8,144,128]{2,1,0:T(8,128)(2,1)}), bf16[8,144,128]{2,1,0:T(8,128)(2,1)S(1)}, u32[]{:S(2)}, u32[]{:S(2)}) async-start(bf16[8,144,128]{2,1,0:T(8,128)(2,1)} %up_project.1), calls=%async_computation.2 | async-start | bytes 589824 | tf_op jit(solution)/shard_map/all_to_all | solution.py:382
  146.3 45.1 %copy-start.9 = (bf16[7168]{0:T(1024)(128)(2,1)S(1)}, bf16[7168]{0:T(1024)(128)(2,1)}, u32[]{:S(2)}) copy-start(bf16[7168]{0:T(1024)(128)(2,1)} %param.15) | copy-start | bytes 43012
  158.2 10.2 %all-to-all-start.3 = ((bf16[4,64,256]{2,1,0:T(8,128)(2,1)}), bf16[4,64,256]{2,1,0:T(8,128)(2,1)S(1)}, u32[]{:S(2)}, u32[]{:S(2)}) async-start(bf16[4,64,256]{2,1,0:T(8,128)(2,1)} %combine.1), calls=%async_computation.3 | async-start | bytes 262144 | tf_op jit(solution)/shard_map/all_to_all | solution.py:382
  168.4 1.2 copy-start.5
  172.8 13.8 %all-to-all-start.4 = ((bf16[8,64,256]{2,1,0:T(8,128)(2,1)}), bf16[8,64,256]{2,1,0:T(8,128)(2,1)S(1)}, u32[]{:S(2)}, u32[]{:S(2)}) async-start(bf16[8,64,256]{2,1,0:T(8,128)(2,1)} %project.1), calls=%async_computation.4 | async-start | bytes 524288 | tf_op jit(solution)/shard_map/all_to_all | solution.py:382
  187.6 16.5 %all-to-all-start.5 = ((bf16[32,24,256]{2,1,0:T(8,128)(2,1)}), bf16[32,24,256]{2,1,0:T(8,128)(2,1)S(1)}, u32[]{:S(2)}, u32[]{:S(2)}) async-start(bf16[32,24,256]{2,1,0:T(8,128)(2,1)} %bitcast.11), calls=%async_computation.5 | async-start | bytes 786432 | tf_op jit(solution)/shard_map/all_to_all | solution.py:382
Sparse Core Ops, SparseCore 0:
  10.7 49.6 all-gather.1

commit v3 on v2

--- a/solution.py
+++ b/solution.py
@@ -25,9 +25,8 @@
 SENT = MINE + 16
 SLOTS = EXPERTS * CAP
 OWN_SLOTS = SLOTS // DEVS
-QUARTER = D // NX
 BLOCK = 256
-BLOCKS = QUARTER // BLOCK
+BLOCKS = D // BLOCK
 TILES = -(-LAT // 128)
 PACKED = TILES * MINE + LAT_KV
 STEP = 4
@@ -164,11 +163,11 @@
 
     @pl.when(core[0] == 0)
     def _():
-        apply(lambda z: mine[z, TILES * MINE :, :], lambda z: other[z])
+        apply(lambda z: mine[z, TILES * MINE :, :], lambda z: other[z, TILES * MINE :, :])
 
     @pl.when(core[0] != 0)
     def _():
-        apply(lambda z: other[z], lambda z: mine[z, TILES * MINE :, :])
+        apply(lambda z: other[z, TILES * MINE :, :], lambda z: mine[z, TILES * MINE :, :])
 
 
 def up_project(core, latents, stats, mine, other):
@@ -180,32 +179,6 @@
         compiler_params=params(),
         name="up_project",
     )(core, latents, stats, mine, other)
-
-
-def turn_kernel(x, weight, *refs):
-    outs, sems = refs[:NX], refs[NX]
-    copies = []
-    for k in range(NX):
-        start = pl.multiple_of(((x[0] + k) & (NX - 1)) * QUARTER, 128)
-        copies.append(
-            pltpu.make_async_copy(weight.at[:, pl.ds(start, QUARTER)], outs[k], sems.at[k])
-        )
-    for copy in copies:
-        copy.start()
-    for copy in copies:
-        copy.wait()
-
-
-def turn(x, weight):
-    return pl.pallas_call(
-        turn_kernel,
-        out_shape=[jax.ShapeDtypeStruct((2 * HEAD_V, QUARTER), bf16)] * NX,
-        in_specs=[SMEM, pl.BlockSpec(memory_space=pl.ANY)],
-        out_specs=[pl.BlockSpec(memory_space=pl.ANY)] * NX,
-        scratch_shapes=[pltpu.SemaphoreType.DMA((NX,))],
-        compiler_params=params(),
-        name="turn",
-    )(x, weight)
 
 
 def own_kernel(query, keys, value_up, values, stats):
@@ -260,15 +233,14 @@
     for z in range(NZ):
         values = values + table[:, z + 1 : z + 2] * arrived[z, :MINE, :].astype(f32)
     values = values.astype(bf16)
-    for x in range(NX):
-        out[x, :, :HEAD_V] = values[:ROWS]
-        out[x, :, HEAD_V:] = values[ROWS:]
+    out[:, :HEAD_V] = values[:ROWS]
+    out[:, HEAD_V:] = values[ROWS:]
 
 
 def combine(arrived, own_values, own_stats):
     return pl.pallas_call(
         combine_kernel,
-        out_shape=jax.ShapeDtypeStruct((NX, ROWS, 2 * HEAD_V), bf16),
+        out_shape=jax.ShapeDtypeStruct((ROWS, 2 * HEAD_V), bf16),
         in_specs=[VMEM] * 3,
         out_specs=VMEM,
         compiler_params=params(),
@@ -276,28 +248,23 @@
     )(arrived, own_values, own_stats)
 
 
-def project_kernel(x, head_values, *refs):
-    weights, out = refs[:NX], refs[NX]
-    rows = [head_values[(x[0] + NX - k) & (NX - 1)] for k in range(NX)]
+def project_kernel(head_values, weight, out):
     for block in range(BLOCKS):
         part = slice(block * BLOCK, (block + 1) * BLOCK)
-        total = dot(rows[0], weights[0][:, part])
-        for k in range(1, NX):
-            total = total + dot(rows[k], weights[k][:, part])
-        out[block] = total.astype(bf16)
-    for block in range(BLOCKS, NZ):
+        out[block] = dot(head_values[...], weight[:, part]).astype(bf16)
+    for block in range(BLOCKS, DEVS):
         out[block] = jnp.zeros((ROWS, BLOCK), bf16)
 
 
-def project(x, head_values, weights):
+def project(head_values, weight):
     return pl.pallas_call(
         project_kernel,
-        out_shape=jax.ShapeDtypeStruct((NZ, ROWS, BLOCK), bf16),
-        in_specs=[SMEM] + [VMEM] * (1 + NX),
+        out_shape=jax.ShapeDtypeStruct((DEVS, ROWS, BLOCK), bf16),
+        in_specs=[VMEM] * 2,
         out_specs=VMEM,
         compiler_params=params(),
         name="project",
-    )(x, head_values, *weights)
+    )(head_values, weight)
 
 
 def slots_kernel(routes, gates, picks, slot_gates):
@@ -335,8 +302,8 @@
 
 def dispatch_kernel(arrived, picks, out):
     total = arrived[0].astype(f32)
-    for z in range(1, NZ):
-        total = total + arrived[z].astype(f32)
+    for dev in range(1, DEVS):
+        total = total + arrived[dev].astype(f32)
     out[...] = dot(picks[...], total.astype(bf16)).astype(bf16)
 
 
@@ -352,10 +319,7 @@
 
 
 def norm_kernel(arrived, gain, out):
-    blocks = []
-    for x in range(NX):
-        for z in range(BLOCKS):
-            blocks.append(arrived[z * NX + x].astype(f32))
+    blocks = [arrived[block].astype(f32) for block in range(BLOCKS)]
     square = blocks[0] * blocks[0]
     for block in blocks[1:]:
         square = square + block * block
@@ -405,22 +369,18 @@
 
     query = queries.reshape(ROWS, 2, LAT).transpose(1, 0, 2).reshape(MINE, LAT)
     core = core[None].astype(jnp.int32)
-    x = lax.axis_index("x")[None].astype(jnp.int32)
     packed = lax.all_gather(pack(core, query, value_up), "z", axis=0, tiled=True)
     packed = packed.reshape(NZ, PACKED, 128)
-    other_up = lax.ppermute(packed[:, TILES * MINE :, :], "core", [(0, 1), (1, 0)])
-    weights = turn(x, out_weight)
-    weights = [weights[0]] + [
-        lax.ppermute(weights[k], "x", [(i, (i + k) % NX) for i in range(NX)]) for k in range(1, NX)
-    ]
+    packed, keys = lax.optimization_barrier((packed, keys))
+    other_packed = lax.ppermute(packed, "core", [(0, 1), (1, 0)])
     own_values, own_stats = own_attention(query, new_latents.reshape(ROWS, LAT), value_up)
     picks, all_gates = slots(routes.T, gates.T)
     slot_gates = lax.dynamic_slice_in_dim(all_gates, dev * OWN_SLOTS, OWN_SLOTS, 0)
 
     latents, stats = prompt_attention(packed, keys)
-    partial = exchange(up_project(core, latents, stats, packed, other_up), "z")
-    head_values = exchange(combine(partial, own_values, own_stats), "x")
-    sums = exchange(project(x, head_values, weights), "z")
+    partial = exchange(up_project(core, latents, stats, packed, other_packed), "z")
+    head_values = combine(partial, own_values, own_stats)
+    sums = exchange(project(head_values, out_weight), ("z", "x"))
     rows = dispatch(sums, picks).reshape(DEVS, OWN_SLOTS, BLOCK)
     slot_rows = norm(exchange(rows, ("z", "x")), norm_gain.reshape(1, D))
     return (slot_rows[None], slot_gates.reshape(1, OWN_SLOTS // CAP, CAP))

time: 213 us -> 160 us (0.75)
  blocking collectives: 46.6 us -> 29.1 us
  starting transfers between devices: 47.7 us -> 33 us
  waiting for transfers between devices: 75.6 us -> 63.4 us
  Pallas kernels: 17 us -> 11.4 us
  local copies, waits for them, and re-layouts: 10.9 us -> 8.01 us
    all_gather x1, blocking collectives: 46.6 us -> 14.6 us  [local(): keys = lax.all_gather(served, 'x', axis=0, tiled=True)]
    all_gather x1, waiting for transfers between devices: 30.5 us -> 0.01 us  [local(): lax.all_gather(pack(core, query, value_up), 'z', axis=0, tiled=True)]
    all_to_all x6 -> x4, waiting for transfers between devices: 45 us -> 62 us  [exchange(): return lax.all_to_all(value, axes, split_axis=0, concat_axis=0, tiled=True)]
    all_to_all x0 -> x1, blocking collectives: none -> 14.5 us  [exchange(): return lax.all_to_all(value, axes, split_axis=0, concat_axis=0, tiled=True)]
    ppermute x4 -> x1, starting transfers between devices: 13.2 us -> 1.91 us  [local(): other_packed = lax.ppermute(packed, 'core', [(0, 1), (1, 0)])]
    pallas_call x3 -> x2, Pallas kernels: 5.91 us -> 2.15 us  [the longest x1 1.75 us: project(): pl.pallas_call(project_kernel, out_shape=jax.ShapeDtypeStruct((DEVS, ROWS...]
    all_to_all x6 -> x4, starting transfers between devices: 32.5 us -> 29.2 us  [exchange(): return lax.all_to_all(value, axes, split_axis=0, concat_axis=0, tiled=True)]
    slice x1 -> x0, local copies, waits for them, and re-layouts: 2.43 us -> none  [local(): packed[:, TILES * MINE:, :]]
  transfers between devices with their start and end apart: 12 -> 7, of which waited for: 6 -> 5; matrix products, arithmetic and copies ran while one was open for 2% -> 2% of each run, Pallas kernels for 5% -> 3%
where the time goes in v3:
time: 160 us; the launch traced here: 159 us
  waiting for transfers between devices  63.4 us (40%)
  starting transfers between devices  33 us (21%)
  blocking collectives  29.1 us (18%)
  between operations  14.2 us (9%)
  Pallas kernels  11.4 us (7%)
  local copies, waits for them, and re-layouts  8.01 us (5%)
    all_to_all x4, waiting for transfers between devices, exchange(): return lax.all_to_all(value, axes, split_axis=0, concat_axis=0, tiled=True)  62 us
    all_to_all x4, starting transfers between devices, exchange(): return lax.all_to_all(value, axes, split_axis=0, concat_axis=0, tiled=True)  29.2 us
    all_gather x1, blocking collectives, local(): keys = lax.all_gather(served, 'x', axis=0, tiled=True)  14.6 us
    all_to_all x1, blocking collectives, exchange(): return lax.all_to_all(value, axes, split_axis=0, concat_axis=0, tiled=True)  14.5 us
    unnamed x19, local copies, waits for them, and re-layouts  5.33 us
  transfers between devices with their start and end apart: 7, of which 5 were waited for; matrix products, arithmetic and copies ran while one was open for 2% of the time, Pallas kernels for 3%

profile of v3, /device:TPU:8, one launch (start us, length us, event | category | flops | bytes accessed | tf_op | source)
XLA Modules:
  0.0 159.1 jit_solution(14050040121253026256)
XLA Ops:
  7.2 0.0 all-gather.2.cloned.1.call-start
  7.2 0.9 copy.13
  8.2 0.0 copy-start.3
  8.2 0.9 copy-done.3
  9.1 0.8 pack.1
  9.9 0.0 all-gather.2.cloned.1.call-update
  9.9 9.1 %all-to-all-start = ((bf16[8,24,576]{2,1,0:T(8,128)(2,1)}), bf16[8,24,576]{2,1,0:T(8,128)(2,1)S(1)}, u32[]{:S(2)}, u32[]{:S(2)}) async-start(bf16[8,24,576]{2,1,0:T(8,128)(2,1)} %bitcast.21), calls=%async_computation | async-start | bytes 491520 | tf_op jit(solution)/shard_map/all_to_all | solution.py:346
  19.0 0.7 slice.6
  19.8 0.7 slice.7
  20.5 7.4 %all-to-all-done.mine = bf16[8,24,576]{2,1,0:T(8,128)(2,1)S(1)} async-done(((bf16[8,24,576]{2,1,0:T(8,128)(2,1)}), bf16[8,24,576]{2,1,0:T(8,128)(2,1)S(1)}, u32[]{:S(2)}, u32[]{:S(2)}) %all-to-all-start) | async-done | bytes 221216 | tf_op jit(solution)/shard_map/all_to_all | solution.py:346
  27.9 1.9 %collective-permute-start = (bf16[8,24,576]{2,1,0:T(8,128)(2,1)S(1)}, bf16[8,24,576]{2,1,0:T(8,128)(2,1)S(1)}, u32[]{:S(2)}, u32[]{:S(2)}) collective-permute-start(bf16[8,24,576]{2,1,0:T(8,128)(2,1)S(1)} %all-to-all-done.mine), channel_id=1, source_target_pairs={{0,32},{32,0},{1,33},{33,1},{2,34},{34,2},{3,35},{35,3},{4,36},{36... | collective-permute-start | bytes 663560 | tf_op jit(solution)/shard_map/ppermute | solution.py:364
  29.8 0.1 pad_add_fusion.wanted
  29.9 1.4 collective-permute-done.other
  31.3 0.7 pick.1
  32.0 14.5 %all_to_all.25 = bf16[8,24,576]{2,1,0:T(8,128)(2,1)S(1)} all-to-all(bf16[8,24,576]{2,1,0:T(8,128)(2,1)S(1)} %pick.1), channel_id=1, replica_groups=mesh['y'=8,'core'=2,'z'=8,'x'=4] {'y'}, dimensions={0} | all-to-all | bytes 442368 | tf_op jit(solution)/shard_map/all_to_all | solution.py:346
  46.5 14.6 %all_gather.7.keys = bf16[768,576]{1,0:T(8,128)(2,1)S(1)} all-gather(bf16[192,576]{1,0:T(8,128)(2,1)S(1)} %bitcast.19), channel_id=1, replica_groups=mesh['y'=8,'core'=2,'z'=8,'x'=4] {'x'}, dimensions={0}, use_global_device_ids=true | all-gather | bytes 1105920 | tf_op jit(solution)/shard_map/all_gather | solution.py:368
  61.0 0.0 all-gather.2.cloned.1.call-done
  61.0 1.9 %collective-permute-start.1 = (bf16[8,1152,128]{2,1,0:T(8,128)(2,1)}, bf16[8,1152,128]{2,1,0:T(8,128)(2,1)S(1)}, u32[]{:S(2)}, u32[]{:S(2)}) collective-permute-start(bf16[8,1152,128]{2,1,0:T(8,128)(2,1)} %bitcast.12), channel_id=1, source_target_pairs={{0,32},{32,0},{1,33},{33,1},{2,34},{34,2},{3,35},{35,3},{4,36},{36... | collective-permute-start | bytes 7077896 | tf_op jit(solution)/shard_map/ppermute | solution.py:375
  62.9 0.0 copy-start
  63.0 1.7 %copy-done = bf16[9216,128]{1,0:T(8,128)(2,1)S(1)} copy-done((bf16[9216,128]{1,0:T(8,128)(2,1)S(1)}, bf16[9216,128]{1,0:T(8,128)(2,1)}, u32[]{:S(2)}) %copy-start) | copy-done | bytes 2359320
  64.6 3.2 %prompt_attention.1 = (bf16[8,128,512]{2,1,0:T(8,128)(2,1)S(1)}, bf16[8,16,128]{2,1,0:T(8,128)(2,1)S(1)}) custom-call(bf16[8,1152,128]{2,1,0:T(8,128)(2,1)S(1)} %bitcast.13, bf16[768,576]{1,0:T(8,128)(2,1)S(1)} %all_gather.7.keys), custom_call_target="tpu_custom_call" | custom-call | tf_op jit(solution)/shard_map/prompt_attention/pallas_call | solution.py:142
  67.8 0.0 collective-permute-done.1.other
  67.8 0.0 copy-done.1
  67.8 0.0 copy-start.7
  67.8 0.0 copy-start.4
  67.8 1.2 up_project.1
  69.0 10.7 %all-to-all-start.2 = ((bf16[8,144,128]{2,1,0:T(8,128)(2,1)}), bf16[8,144,128]{2,1,0:T(8,128)(2,1)S(1)}, u32[]{:S(2)}, u32[]{:S(2)}) async-start(bf16[8,144,128]{2,1,0:T(8,128)(2,1)} %up_project.1), calls=%async_computation.2 | async-start | bytes 589824 | tf_op jit(solution)/shard_map/all_to_all | solution.py:346
  79.7 0.0 copy-done.7
  79.8 0.0 copy-done.4
  79.8 0.6 own_attention.1
  80.4 12.6 %all-to-all-done.2.arrived = bf16[8,144,128]{2,1,0:T(8,128)(2,1)S(1)} async-done(((bf16[8,144,128]{2,1,0:T(8,128)(2,1)}), bf16[8,144,128]{2,1,0:T(8,128)(2,1)S(1)}, u32[]{:S(2)}, u32[]{:S(2)}) %all-to-all-start.2) | async-done | bytes 294944 | tf_op jit(solution)/shard_map/all_to_all | solution.py:346
  93.0 0.4 combine.1.head_values
  93.4 0.0 copy-start.2
  93.4 2.0 %copy-done.2 = bf16[256,7168]{1,0:T(8,128)(2,1)S(1)} copy-done((bf16[256,7168]{1,0:T(8,128)(2,1)S(1)}, bf16[256,7168]{1,0:T(8,128)(2,1)}, u32[]{:S(2)}) %copy-start.2) | copy-done | bytes 3670040
  95.4 1.8 %project.1 = bf16[32,64,256]{2,1,0:T(8,128)(2,1)} custom-call(bf16[64,256]{1,0:T(8,128)(2,1)S(1)} %combine.1.head_values, bf16[256,7168]{1,0:T(8,128)(2,1)S(1)} %copy-done.2), custom_call_target="tpu_custom_call" | custom-call | tf_op jit(solution)/shard_map/project/pallas_call | solution.py:260
  97.2 4.1 %all-to-all-start.3 = ((bf16[32,64,256]{2,1,0:T(8,128)(2,1)}), bf16[32,64,256]{2,1,0:T(8,128)(2,1)S(1)}, u32[]{:S(2)}, u32[]{:S(2)}) async-start(bf16[32,64,256]{2,1,0:T(8,128)(2,1)} %project.1), calls=%async_computation.3 | async-start | bytes 2097152 | tf_op jit(solution)/shard_map/all_to_all | solution.py:346
  101.3 0.0 copy-done.5
  101.3 0.0 copy-done.6
  101.3 0.6 slots.1
  101.9 28.2 %all-to-all-done.3.arrived = bf16[32,64,256]{2,1,0:T(8,128)(2,1)S(1)} async-done(((bf16[32,64,256]{2,1,0:T(8,128)(2,1)}), bf16[32,64,256]{2,1,0:T(8,128)(2,1)S(1)}, u32[]{:S(2)}, u32[]{:S(2)}) %all-to-all-start.3) | async-done | bytes 1048608 | tf_op jit(solution)/shard_map/all_to_all | solution.py:346
  130.1 1.1 dispatch.1
  131.2 5.2 %all-to-all-start.4 = ((bf16[32,24,256]{2,1,0:T(8,128)(2,1)}), bf16[32,24,256]{2,1,0:T(8,128)(2,1)S(1)}, u32[]{:S(2)}, u32[]{:S(2)}) async-start(bf16[32,24,256]{2,1,0:T(8,128)(2,1)} %bitcast.10), calls=%async_computation.4 | async-start | bytes 786432 | tf_op jit(solution)/shard_map/all_to_all | solution.py:346
  136.5 0.0 copy-done.8
  136.5 0.1 dynamic-slice_reduce_fusion
  136.6 0.1 reshape.39
  136.7 0.7 copy.14
  137.4 13.8 %all-to-all-done.4.arrived = bf16[32,24,256]{2,1,0:T(8,128)(2,1)S(1)} async-done(((bf16[32,24,256]{2,1,0:T(8,128)(2,1)}), bf16[32,24,256]{2,1,0:T(8,128)(2,1)S(1)}, u32[]{:S(2)}, u32[]{:S(2)}) %all-to-all-start.4) | async-done | bytes 393248 | tf_op jit(solution)/shard_map/all_to_all | solution.py:346
  151.2 1.1 norm.1
  (7 shorter events, 0.1 us)
Async XLA Ops:
  7.2 53.9 %all-gather.2.cloned.1.call-start = ((), (), s32[]{:S(2)}) async-start(), calls=%async_computation.5 | async-start | bytes 2654208 | tf_op jit(solution)/shard_map/all_gather | solution.py:372
  8.2 1.0 copy-start.3
  9.9 18.0 %all-to-all-start = ((bf16[8,24,576]{2,1,0:T(8,128)(2,1)}), bf16[8,24,576]{2,1,0:T(8,128)(2,1)S(1)}, u32[]{:S(2)}, u32[]{:S(2)}) async-start(bf16[8,24,576]{2,1,0:T(8,128)(2,1)} %bitcast.21), calls=%async_computation | async-start | bytes 491520 | tf_op jit(solution)/shard_map/all_to_all | solution.py:346
  27.9 3.4 %collective-permute-start = (bf16[8,24,576]{2,1,0:T(8,128)(2,1)S(1)}, bf16[8,24,576]{2,1,0:T(8,128)(2,1)S(1)}, u32[]{:S(2)}, u32[]{:S(2)}) collective-permute-start(bf16[8,24,576]{2,1,0:T(8,128)(2,1)S(1)} %all-to-all-done.mine), channel_id=1, source_target_pairs={{0,32},{32,0},{1,33},{33,1},{2,34},{34,2},{3,35},{35,3},{4,36},{36... | collective-permute-start | bytes 663560 | tf_op jit(solution)/shard_map/ppermute | solution.py:364
  61.0 6.8 %collective-permute-start.1 = (bf16[8,1152,128]{2,1,0:T(8,128)(2,1)}, bf16[8,1152,128]{2,1,0:T(8,128)(2,1)S(1)}, u32[]{:S(2)}, u32[]{:S(2)}) collective-permute-start(bf16[8,1152,128]{2,1,0:T(8,128)(2,1)} %bitcast.12), channel_id=1, source_target_pairs={{0,32},{32,0},{1,33},{33,1},{2,34},{34,2},{3,35},{35,3},{4,36},{36... | collective-permute-start | bytes 7077896 | tf_op jit(solution)/shard_map/ppermute | solution.py:375
  62.9 1.7 %copy-start = (bf16[9216,128]{1,0:T(8,128)(2,1)S(1)}, bf16[9216,128]{1,0:T(8,128)(2,1)}, u32[]{:S(2)}) copy-start(bf16[9216,128]{1,0:T(8,128)(2,1)} %all-gather.2.cloned.1.call-done) | copy-start | bytes 7077892
  64.6 3.2 %copy-start.1 = (bf16[9216,128]{1,0:T(8,128)(2,1)S(1)}, bf16[9216,128]{1,0:T(8,128)(2,1)}, u32[]{:S(2)}) copy-start(bf16[9216,128]{1,0:T(8,128)(2,1)} %all-gather.2.cloned.1.call-done) | copy-start | bytes 7077892
  67.8 11.9 %copy-start.7 = (bf16[1,16,4,576]{3,2,1,0:T(4,128)(2,1)S(1)}, bf16[1,16,4,576]{3,2,1,0:T(4,128)(2,1)}, u32[]{:S(2)}) copy-start(bf16[1,16,4,576]{3,2,1,0:T(4,128)(2,1)} %param.12) | copy-start | bytes 221188
  67.8 12.0 %copy-start.4 = (bf16[2,512,128]{2,1,0:T(8,128)(2,1)S(1)}, bf16[2,512,128]{2,1,0:T(8,128)(2,1)}, u32[]{:S(2)}) copy-start(bf16[2,512,128]{2,1,0:T(8,128)(2,1)} %value_up.3) | copy-start | bytes 786436
  69.0 23.9 %all-to-all-start.2 = ((bf16[8,144,128]{2,1,0:T(8,128)(2,1)}), bf16[8,144,128]{2,1,0:T(8,128)(2,1)S(1)}, u32[]{:S(2)}, u32[]{:S(2)}) async-start(bf16[8,144,128]{2,1,0:T(8,128)(2,1)} %up_project.1), calls=%async_computation.2 | async-start | bytes 589824 | tf_op jit(solution)/shard_map/all_to_all | solution.py:346
  93.4 2.0 %copy-start.2 = (bf16[256,7168]{1,0:T(8,128)(2,1)S(1)}, bf16[256,7168]{1,0:T(8,128)(2,1)}, u32[]{:S(2)}) copy-start(bf16[256,7168]{1,0:T(8,128)(2,1)} %weight.1) | copy-start | bytes 11010052
  95.4 5.8 %copy-start.5 = (s32[64,8]{0,1:T(8,128)S(1)}, s32[64,8]{0,1:T(8,128)}, u32[]{:S(2)}) copy-start(s32[64,8]{0,1:T(8,128)} %param.16) | copy-start | bytes 6148
  95.4 5.8 %copy-start.6 = (f32[64,8]{0,1:T(8,128)S(1)}, f32[64,8]{0,1:T(8,128)}, u32[]{:S(2)}) copy-start(f32[64,8]{0,1:T(8,128)} %param.17) | copy-start | bytes 6148
  97.2 39.3 %copy-start.8 = (bf16[7168]{0:T(1024)(128)(2,1)S(1)}, bf16[7168]{0:T(1024)(128)(2,1)}, u32[]{:S(2)}) copy-start(bf16[7168]{0:T(1024)(128)(2,1)} %param.15) | copy-start | bytes 43012
  97.2 32.9 %all-to-all-start.3 = ((bf16[32,64,256]{2,1,0:T(8,128)(2,1)}), bf16[32,64,256]{2,1,0:T(8,128)(2,1)S(1)}, u32[]{:S(2)}, u32[]{:S(2)}) async-start(bf16[32,64,256]{2,1,0:T(8,128)(2,1)} %project.1), calls=%async_computation.3 | async-start | bytes 2097152 | tf_op jit(solution)/shard_map/all_to_all | solution.py:346
  131.2 19.9 %all-to-all-start.4 = ((bf16[32,24,256]{2,1,0:T(8,128)(2,1)}), bf16[32,24,256]{2,1,0:T(8,128)(2,1)S(1)}, u32[]{:S(2)}, u32[]{:S(2)}) async-start(bf16[32,24,256]{2,1,0:T(8,128)(2,1)} %bitcast.10), calls=%async_computation.4 | async-start | bytes 786432 | tf_op jit(solution)/shard_map/all_to_all | solution.py:346
Sparse Core Ops, SparseCore 0:
  10.7 49.4 all-gather.1

commit v4 on v3

--- a/solution.py
+++ b/solution.py
@@ -27,8 +27,6 @@
 OWN_SLOTS = SLOTS // DEVS
 BLOCK = 256
 BLOCKS = D // BLOCK
-TILES = -(-LAT // 128)
-PACKED = TILES * MINE + LAT_KV
 STEP = 4
 
 bf16 = jnp.bfloat16
@@ -49,30 +47,29 @@
     return jnp.transpose(jnp.broadcast_to(column, (MINE, 128)))[:1]
 
 
-def pick_kernel(wanted, mine, other, out):
-    core = wanted[8]
+def pick_kernel(core, prompt_of_group, mine, other, out):
     for y in range(NY):
-        prompt = wanted[y]
+        prompt = prompt_of_group[2 * y + core[0]]
         row = lax.shift_right_logical(prompt, 1)
 
-        @pl.when((prompt & 1) == core)
+        @pl.when((prompt & 1) == core[0])
         def _():
             out[y] = mine[row]
 
-        @pl.when((prompt & 1) != core)
+        @pl.when((prompt & 1) != core[0])
         def _():
             out[y] = other[row]
 
 
-def pick(wanted, mine, other):
+def pick(core, prompt_of_group, mine, other):
     return pl.pallas_call(
         pick_kernel,
         out_shape=jax.ShapeDtypeStruct(mine.shape, mine.dtype),
-        in_specs=[SMEM, VMEM, VMEM],
+        in_specs=[SMEM, SMEM, VMEM, VMEM],
         out_specs=VMEM,
         compiler_params=params(),
         name="pick",
-    )(wanted, mine, other)
+    )(core, prompt_of_group, mine, other)
 
 
 def attend(query, keys, visible=None):
@@ -93,102 +90,42 @@
     return high, mid, rest - mid
 
 
-def pack_kernel(core, query, value_up, out):
-    for tile in range(TILES):
-        width = min(128, LAT - tile * 128)
-        part = query[:, tile * 128 : tile * 128 + width]
-        if width < 128:
-            part = jnp.concatenate([part, jnp.zeros((MINE, 128 - width), bf16)], axis=1)
-        out[tile * MINE : (tile + 1) * MINE, :] = part
-    out[TILES * MINE :, :] = value_up[core[0]]
-
-
-def pack(core, query, value_up):
-    return pl.pallas_call(
-        pack_kernel,
-        out_shape=jax.ShapeDtypeStruct((PACKED, 128), bf16),
-        in_specs=[SMEM, VMEM, VMEM],
-        out_specs=VMEM,
-        compiler_params=params(),
-        name="pack",
-    )(core, query, value_up)
-
-
-def attention_kernel(packed, keys, latents, stats):
+def attention_kernel(z, keys, *refs):
+    queries, out = refs[:NZ], refs[NZ]
     index = lax.broadcasted_iota(jnp.int32, (16, 128), 0)
     for step in range(NZ // STEP):
-        zs = range(step * STEP, (step + 1) * STEP)
-        query = jnp.concatenate(
-            [
-                jnp.concatenate(
-                    [packed[z, tile * MINE : (tile + 1) * MINE, :] for tile in range(TILES)], axis=1
-                )
-                for z in zs
-            ],
-            axis=0,
-        )[:, :LAT]
+        shifts = range(step * STEP, (step + 1) * STEP)
+        query = jnp.concatenate([queries[k][...] for k in shifts], axis=0)
         best, total, latent = attend(query, keys[...])
-        for i, z in enumerate(zs):
+        for i, k in enumerate(shifts):
             part = slice(i * MINE, (i + 1) * MINE)
-            latents[z] = latent[part]
+            owner = (z[0] + NZ - k) & (NZ - 1)
+            out[owner, :MINE, :] = latent[part]
             rows = three(columns_to_lanes(best[part])) + three(columns_to_lanes(total[part]))
             table = jnp.zeros((16, 128), f32)
             for j, row in enumerate(rows):
                 table = jnp.where(index == j, jnp.broadcast_to(row, (16, 128)), table)
-            stats[z] = table.astype(bf16)
-
-
-def prompt_attention(packed, keys):
+            out[owner, MINE:, :128] = table.astype(bf16)
+            out[owner, MINE:, 128:] = jnp.zeros((16, LAT_KV - 128), bf16)
+
+
+def prompt_attention(z, keys, queries):
     return pl.pallas_call(
         attention_kernel,
-        out_shape=(
-            jax.ShapeDtypeStruct((NZ, MINE, LAT_KV), bf16),
-            jax.ShapeDtypeStruct((NZ, 16, 128), bf16),
-        ),
-        in_specs=[VMEM] * 2,
-        out_specs=(VMEM, VMEM),
+        out_shape=jax.ShapeDtypeStruct((NZ, SENT, LAT_KV), bf16),
+        in_specs=[SMEM] + [VMEM] * (1 + NZ),
+        out_specs=VMEM,
         compiler_params=params(),
         name="prompt_attention",
-    )(packed, keys)
-
-
-def up_kernel(core, latents, stats, mine, other, out):
-    for z in range(NZ):
-        out[z, MINE:, :] = stats[z]
-
-    def apply(first, second):
-        for z in range(NZ):
-            out[z, :ROWS, :] = dot(latents[z, :ROWS], first(z)).astype(bf16)
-            out[z, ROWS:MINE, :] = dot(latents[z, ROWS:], second(z)).astype(bf16)
-
-    @pl.when(core[0] == 0)
-    def _():
-        apply(lambda z: mine[z, TILES * MINE :, :], lambda z: other[z, TILES * MINE :, :])
-
-    @pl.when(core[0] != 0)
-    def _():
-        apply(lambda z: other[z, TILES * MINE :, :], lambda z: mine[z, TILES * MINE :, :])
-
-
-def up_project(core, latents, stats, mine, other):
-    return pl.pallas_call(
-        up_kernel,
-        out_shape=jax.ShapeDtypeStruct((NZ, SENT, 128), bf16),
-        in_specs=[SMEM] + [VMEM] * 4,
-        out_specs=VMEM,
-        compiler_params=params(),
-        name="up_project",
-    )(core, latents, stats, mine, other)
-
-
-def own_kernel(query, keys, value_up, values, stats):
+    )(z, keys, *queries)
+
+
+def own_kernel(query, keys, latents, stats):
     row = lax.broadcasted_iota(jnp.int32, (MINE, ROWS), 0) & (ROWS - 1)
     key = lax.broadcasted_iota(jnp.int32, (MINE, ROWS), 1)
     same = lax.shift_right_logical(row, 2) == lax.shift_right_logical(key, 2)
     best, total, latent = attend(query[...], keys[...], same & (key <= row))
-    for head in range(2):
-        part = slice(head * ROWS, (head + 1) * ROWS)
-        values[part, :] = dot(latent[part], value_up[head])
+    latents[...] = latent
     index = lax.broadcasted_iota(jnp.int32, (8, 128), 0)
     stats[...] = jnp.where(
         index == 0,
@@ -197,24 +134,24 @@
     )
 
 
-def own_attention(query, keys, value_up):
+def own_attention(query, keys):
     return pl.pallas_call(
         own_kernel,
         out_shape=(
-            jax.ShapeDtypeStruct((MINE, HEAD_V), f32),
+            jax.ShapeDtypeStruct((MINE, LAT_KV), bf16),
             jax.ShapeDtypeStruct((8, 128), f32),
         ),
-        in_specs=[VMEM] * 3,
+        in_specs=[VMEM] * 2,
         out_specs=(VMEM, VMEM),
         compiler_params=params(),
         name="own_attention",
-    )(query, keys, value_up)
-
-
-def combine_kernel(arrived, own_values, own_stats, out):
+    )(query, keys)
+
+
+def combine_kernel(arrived, own_latents, own_stats, value_up, out):
     bests, totals = [own_stats[0:1, :]], [own_stats[1:2, :]]
     for z in range(NZ):
-        stats = arrived[z, MINE:, :].astype(f32)
+        stats = arrived[z, MINE:, :128].astype(f32)
         bests.append(stats[0:1] + stats[1:2] + stats[2:3])
         totals.append(stats[3:4] + stats[4:5] + stats[5:6])
     top = bests[0]
@@ -229,23 +166,24 @@
     for i, share in enumerate(shares):
         table = jnp.where(index == i, jnp.broadcast_to(share / whole, (128, 128)), table)
     table = jnp.transpose(table)
-    values = table[:, 0:1] * own_values[...]
+    latent = table[:, 0:1] * own_latents[...].astype(f32)
     for z in range(NZ):
-        values = values + table[:, z + 1 : z + 2] * arrived[z, :MINE, :].astype(f32)
-    values = values.astype(bf16)
-    out[:, :HEAD_V] = values[:ROWS]
-    out[:, HEAD_V:] = values[ROWS:]
-
-
-def combine(arrived, own_values, own_stats):
+        latent = latent + table[:, z + 1 : z + 2] * arrived[z, :MINE, :].astype(f32)
+    latent = latent.astype(bf16)
+    for head in range(2):
+        values = dot(latent[head * ROWS : (head + 1) * ROWS], value_up[head])
+        out[:, head * HEAD_V : (head + 1) * HEAD_V] = values.astype(bf16)
+
+
+def combine(arrived, own_latents, own_stats, value_up):
     return pl.pallas_call(
         combine_kernel,
         out_shape=jax.ShapeDtypeStruct((ROWS, 2 * HEAD_V), bf16),
-        in_specs=[VMEM] * 3,
+        in_specs=[VMEM] * 4,
         out_specs=VMEM,
         compiler_params=params(),
         name="combine",
-    )(arrived, own_values, own_stats)
+    )(arrived, own_latents, own_stats, value_up)
 
 
 def project_kernel(head_values, weight, out):
@@ -357,29 +295,30 @@
     routes,
     gates,
 ):
-    core = lax.axis_index("core")
+    core = lax.axis_index("core")[None].astype(jnp.int32)
+    z = lax.axis_index("z")[None].astype(jnp.int32)
     dev = lax.axis_index("z") * NX + lax.axis_index("x")
 
+    query = queries.reshape(ROWS, 2, LAT).transpose(1, 0, 2).reshape(MINE, LAT)
+
+    def shifted(k):
+        return lax.ppermute(query, "z", [(i, (i + k) % NZ) for i in range(NZ)])
+
     pieces = exchange(prompt_cache.reshape(NY, PIECE, LAT), "y")
+    near = [1, NZ - 1, 2, NZ - 2]
+    pieces, *arrived = lax.optimization_barrier((pieces, *[shifted(k) for k in near]))
     other = lax.ppermute(pieces, "core", [(0, 1), (1, 0)])
-    own_prompts = jnp.where(core == 0, prompt_of_group[0::2], prompt_of_group[1::2])
-    wanted = jnp.concatenate([own_prompts, core[None].astype(jnp.int32)])
-    served = exchange(pick(wanted, pieces, other), "y").reshape(NY * PIECE, LAT)
+    served = exchange(pick(core, prompt_of_group, pieces, other), "y").reshape(NY * PIECE, LAT)
     keys = lax.all_gather(served, "x", axis=0, tiled=True)
-
-    query = queries.reshape(ROWS, 2, LAT).transpose(1, 0, 2).reshape(MINE, LAT)
-    core = core[None].astype(jnp.int32)
-    packed = lax.all_gather(pack(core, query, value_up), "z", axis=0, tiled=True)
-    packed = packed.reshape(NZ, PACKED, 128)
-    packed, keys = lax.optimization_barrier((packed, keys))
-    other_packed = lax.ppermute(packed, "core", [(0, 1), (1, 0)])
-    own_values, own_stats = own_attention(query, new_latents.reshape(ROWS, LAT), value_up)
+    far = [k for k in range(1, NZ) if k not in near]
+    by_shift = dict(zip(near + far, arrived + [shifted(k) for k in far]))
+    all_queries = [query] + [by_shift[k] for k in range(1, NZ)]
+    own_latents, own_stats = own_attention(query, new_latents.reshape(ROWS, LAT))
     picks, all_gates = slots(routes.T, gates.T)
     slot_gates = lax.dynamic_slice_in_dim(all_gates, dev * OWN_SLOTS, OWN_SLOTS, 0)
 
-    latents, stats = prompt_attention(packed, keys)
-    partial = exchange(up_project(core, latents, stats, packed, other_packed), "z")
-    head_values = combine(partial, own_values, own_stats)
+    partial = exchange(prompt_attention(z, keys, all_queries), "z")
+    head_values = combine(partial, own_latents, own_stats, value_up)
     sums = exchange(project(head_values, out_weight), ("z", "x"))
     rows = dispatch(sums, picks).reshape(DEVS, OWN_SLOTS, BLOCK)
     slot_rows = norm(exchange(rows, ("z", "x")), norm_gain.reshape(1, D))

time: 160 us -> 180 us (1.12)
  starting transfers between devices: 33 us -> 66.3 us
  waiting for transfers between devices: 63.4 us -> 81.3 us
  blocking collectives: 29.1 us -> 14.5 us
  between operations: 14.2 us -> 0.82 us
  local copies, waits for them, and re-layouts: 8.01 us -> 4.57 us
    ppermute x1 -> x7, starting transfers between devices: 1.91 us -> 33.5 us  [shifted(): return lax.ppermute(query, 'z', [(i, (i + k) % NZ) for i in range(NZ)])]
    all_to_all x1 -> x0, blocking collectives: 14.5 us -> none  [exchange(): return lax.all_to_all(value, axes, split_axis=0, concat_axis=0, tiled=True)]
    all_to_all x4 -> x5, waiting for transfers between devices: 62 us -> 72.2 us  [exchange(): return lax.all_to_all(value, axes, split_axis=0, concat_axis=0, tiled=True)]
    ppermute x1 -> x7, waiting for transfers between devices: 0.01 us -> 7.58 us  [shifted(): return lax.ppermute(query, 'z', [(i, (i + k) % NZ) for i in range(NZ)])]
    unnamed x19 -> x15, local copies, waits for them, and re-layouts: 5.33 us -> 3.38 us
    all_to_all x4 -> x5, starting transfers between devices: 29.2 us -> 30.9 us  [exchange(): return lax.all_to_all(value, axes, split_axis=0, concat_axis=0, tiled=True)]
    pallas_call x4 -> x2, Pallas kernels: 5.7 us -> 4.75 us  [the longest x1 4.27 us: prompt_attention(): pl.pallas_call(attention_kernel, out_shape=jax.ShapeDtypeStruct((NZ, SENT...]
  transfers between devices with their start and end apart: 7 -> 13, of which waited for: 5 -> 7; matrix products, arithmetic and copies ran while one was open for 2% -> 1% of each run, Pallas kernels for 3% -> 1%
where the time goes in v4:
time: 180 us; the launch traced here: 179 us
  waiting for transfers between devices  81.3 us (45%)
  starting transfers between devices  66.3 us (37%)
  blocking collectives  14.5 us (8%)
  Pallas kernels  11.4 us (6%)
  local copies, waits for them, and re-layouts  4.57 us (3%)
    all_to_all x5, waiting for transfers between devices, exchange(): return lax.all_to_all(value, axes, split_axis=0, concat_axis=0, tiled=True)  72.2 us
    ppermute x7, starting transfers between devices, shifted(): return lax.ppermute(query, 'z', [(i, (i + k) % NZ) for i in range(NZ)])  33.5 us
    all_to_all x5, starting transfers between devices, exchange(): return lax.all_to_all(value, axes, split_axis=0, concat_axis=0, tiled=True)  30.9 us
    all_gather x1, blocking collectives, local(): keys = lax.all_gather(served, 'x', axis=0, tiled=True)  14.5 us
    ppermute x7, waiting for transfers between devices, shifted(): return lax.ppermute(query, 'z', [(i, (i + k) % NZ) for i in range(NZ)])  7.58 us
    pallas_call x1, Pallas kernels, prompt_attention(): pl.pallas_call(attention_kernel, out_shape=jax.ShapeDtypeStruct((NZ, SENT...  4.27 us
  transfers between devices with their start and end apart: 13, of which 7 were waited for; matrix products, arithmetic and copies ran while one was open for 1% of the time, Pallas kernels for 1%

profile of v4, /device:TPU:8, one launch (start us, length us, event | category | flops | bytes accessed | tf_op | source)
XLA Modules:
  0.0 178.8 jit_solution(17857653959691936735)
XLA Ops:
  0.6 9.1 %all-to-all-start = ((bf16[8,24,576]{2,1,0:T(8,128)(2,1)}), bf16[8,24,576]{2,1,0:T(8,128)(2,1)S(1)}, u32[]{:S(2)}, u32[]{:S(2)}) async-start(bf16[8,24,576]{2,1,0:T(8,128)(2,1)} %bitcast.25), calls=%async_computation | async-start | bytes 491520 | tf_op jit(solution)/shard_map/all_to_all | solution.py:284
  9.8 0.9 copy.13
  10.7 2.7 %collective-permute-start = (bf16[128,576]{1,0:T(8,128)(2,1)S(1)}, bf16[128,576]{1,0:T(8,128)(2,1)S(1)}, u32[]{:S(2)}, u32[]{:S(2)}) collective-permute-start(bf16[128,576]{1,0:T(8,128)(2,1)S(1)} %bitcast.12), channel_id=1, source_target_pairs={{0,4},{4,8},{8,12},{12,16},{16,20},{20,24},{24,28},{28,0},{1,5},{5... | collective-permute-start | bytes 442376 | tf_op jit(solution)/shard_map/ppermute | solution.py:305
  13.4 8.6 %collective-permute-start.1 = (bf16[128,576]{1,0:T(8,128)(2,1)S(1)}, bf16[128,576]{1,0:T(8,128)(2,1)S(1)}, u32[]{:S(2)}, u32[]{:S(2)}) collective-permute-start(bf16[128,576]{1,0:T(8,128)(2,1)S(1)} %bitcast.13), channel_id=1, source_target_pairs={{0,28},{4,0},{8,4},{12,8},{16,12},{20,16},{24,20},{28,24},{1,29},{... | collective-permute-start | bytes 442376 | tf_op jit(solution)/shard_map/ppermute | solution.py:305
  22.0 1.9 %collective-permute-start.2 = (bf16[128,576]{1,0:T(8,128)(2,1)S(1)}, bf16[128,576]{1,0:T(8,128)(2,1)S(1)}, u32[]{:S(2)}, u32[]{:S(2)}) collective-permute-start(bf16[128,576]{1,0:T(8,128)(2,1)S(1)} %bitcast.14), channel_id=1, source_target_pairs={{0,8},{4,12},{8,16},{12,20},{16,24},{20,28},{24,0},{28,4},{1,9},{5... | collective-permute-start | bytes 442376 | tf_op jit(solution)/shard_map/ppermute | solution.py:305
  23.9 6.0 %collective-permute-start.3 = (bf16[128,576]{1,0:T(8,128)(2,1)S(1)}, bf16[128,576]{1,0:T(8,128)(2,1)S(1)}, u32[]{:S(2)}, u32[]{:S(2)}) collective-permute-start(bf16[128,576]{1,0:T(8,128)(2,1)S(1)} %bitcast.15), channel_id=1, source_target_pairs={{0,24},{4,28},{8,0},{12,4},{16,8},{20,12},{24,16},{28,20},{1,25},{... | collective-permute-start | bytes 442376 | tf_op jit(solution)/shard_map/ppermute | solution.py:305
  30.0 0.0 collective-permute-done.refs_1_
  30.0 0.0 collective-permute-done.1.refs_7_
  30.0 4.6 %collective-permute-done.2.refs_2_ = bf16[128,576]{1,0:T(8,128)(2,1)S(1)} collective-permute-done((bf16[128,576]{1,0:T(8,128)(2,1)S(1)}, bf16[128,576]{1,0:T(8,128)(2,1)S(1)}, u32[]{:S(2)}, u32[]{:S(2)}) %collective-permute-start.2) | collective-permute-done | bytes 147488 | tf_op jit(solution)/shard_map/ppermute | solution.py:305
  34.6 1.0 collective-permute-done.3.refs_6_
  35.6 0.0 all-to-all-done.mine
  35.6 1.9 %collective-permute-start.4 = (bf16[8,24,576]{2,1,0:T(8,128)(2,1)S(1)}, bf16[8,24,576]{2,1,0:T(8,128)(2,1)S(1)}, u32[]{:S(2)}, u32[]{:S(2)}) collective-permute-start(bf16[8,24,576]{2,1,0:T(8,128)(2,1)S(1)} %all-to-all-done.mine), channel_id=1, source_target_pairs={{0,32},{32,0},{1,33},{33,1},{2,34},{34,2},{3,35},{35,3},{4,36},{36... | collective-permute-start | bytes 663560 | tf_op jit(solution)/shard_map/ppermute | solution.py:310
  37.5 1.5 collective-permute-done.4.other
  39.0 0.0 copy-start.4
  39.0 0.7 copy-done.4
  39.7 1.4 pick.1
  41.1 7.2 %all-to-all-start.1 = ((bf16[8,24,576]{2,1,0:T(8,128)(2,1)}), bf16[8,24,576]{2,1,0:T(8,128)(2,1)S(1)}, u32[]{:S(2)}, u32[]{:S(2)}) async-start(bf16[8,24,576]{2,1,0:T(8,128)(2,1)} %pick.1), calls=%async_computation.1 | async-start | bytes 491520 | tf_op jit(solution)/shard_map/all_to_all | solution.py:284
  48.3 5.6 %collective-permute-start.5 = (bf16[128,576]{1,0:T(8,128)(2,1)S(1)}, bf16[128,576]{1,0:T(8,128)(2,1)S(1)}, u32[]{:S(2)}, u32[]{:S(2)}) collective-permute-start(bf16[128,576]{1,0:T(8,128)(2,1)S(1)} %bitcast.16), channel_id=1, source_target_pairs={{0,12},{4,16},{8,20},{12,24},{16,28},{20,0},{24,4},{28,8},{1,13},{... | collective-permute-start | bytes 442376 | tf_op jit(solution)/shard_map/ppermute | solution.py:305
  53.9 4.3 %collective-permute-start.6 = (bf16[128,576]{1,0:T(8,128)(2,1)S(1)}, bf16[128,576]{1,0:T(8,128)(2,1)S(1)}, u32[]{:S(2)}, u32[]{:S(2)}) collective-permute-start(bf16[128,576]{1,0:T(8,128)(2,1)S(1)} %bitcast.17), channel_id=1, source_target_pairs={{0,16},{4,20},{8,24},{12,28},{16,0},{20,4},{24,8},{28,12},{1,17},{... | collective-permute-start | bytes 442376 | tf_op jit(solution)/shard_map/ppermute | solution.py:305
  58.1 4.5 %collective-permute-start.7 = (bf16[128,576]{1,0:T(8,128)(2,1)S(1)}, bf16[128,576]{1,0:T(8,128)(2,1)S(1)}, u32[]{:S(2)}, u32[]{:S(2)}) collective-permute-start(bf16[128,576]{1,0:T(8,128)(2,1)S(1)} %bitcast.18), channel_id=1, source_target_pairs={{0,20},{4,24},{8,28},{12,0},{16,4},{20,8},{24,12},{28,16},{1,21},{... | collective-permute-start | bytes 442376 | tf_op jit(solution)/shard_map/ppermute | solution.py:305
  62.6 0.0 all-to-all-done.1
  62.6 14.5 %all_gather.3.keys = bf16[768,576]{1,0:T(8,128)(2,1)S(1)} all-gather(bf16[192,576]{1,0:T(8,128)(2,1)S(1)} %bitcast.23), channel_id=1, replica_groups=mesh['y'=8,'core'=2,'z'=8,'x'=4] {'x'}, dimensions={0}, use_global_device_ids=true | all-gather | bytes 1105920 | tf_op jit(solution)/shard_map/all_gather | solution.py:312
  77.1 0.0 collective-permute-done.5.refs_3_
  77.1 0.0 collective-permute-done.6.refs_4_
  77.1 2.0 %collective-permute-done.7.refs_5_ = bf16[128,576]{1,0:T(8,128)(2,1)S(1)} collective-permute-done((bf16[128,576]{1,0:T(8,128)(2,1)S(1)}, bf16[128,576]{1,0:T(8,128)(2,1)S(1)}, u32[]{:S(2)}, u32[]{:S(2)}) %collective-permute-start.7) | collective-permute-done | bytes 147488 | tf_op jit(solution)/shard_map/ppermute | solution.py:305
  79.1 4.3 %prompt_attention.1 = bf16[8,144,512]{2,1,0:T(8,128)(2,1)} custom-call(s32[1]{0:T(128)} %bitcast.z, bf16[768,576]{1,0:T(8,128)(2,1)S(1)} %all_gather.3.keys, bf16[128,576]{1,0:T(8,128)(2,1)S(1)} %bitcast.19, bf16[128,576]{1,0:T(8,128)(2,1)S(1)} %collective-permute-done.refs_1_, bf16[128,576]{1,0:T(8,128)(2,1)S(1)} %collective-permute-done.2.refs_2_, ...), custom_call_target="tpu_custom_call" | custom-call | tf_op jit(solution)/shard_map/prompt_attention/pallas_call | solution.py:113
  83.3 0.0 copy-start.5
  83.3 4.1 %all-to-all-start.2 = ((bf16[8,144,512]{2,1,0:T(8,128)(2,1)}), bf16[8,144,512]{2,1,0:T(8,128)(2,1)S(1)}, u32[]{:S(2)}, u32[]{:S(2)}) async-start(bf16[8,144,512]{2,1,0:T(8,128)(2,1)} %prompt_attention.1), calls=%async_computation.2 | async-start | bytes 2359296 | tf_op jit(solution)/shard_map/all_to_all | solution.py:284
  87.4 0.0 copy-done.5
  87.5 0.5 own_attention.1
  88.0 31.0 %all-to-all-done.2.arrived = bf16[8,144,512]{2,1,0:T(8,128)(2,1)S(1)} async-done(((bf16[8,144,512]{2,1,0:T(8,128)(2,1)}), bf16[8,144,512]{2,1,0:T(8,128)(2,1)S(1)}, u32[]{:S(2)}, u32[]{:S(2)}) %all-to-all-start.2) | async-done | bytes 1179680 | tf_op jit(solution)/shard_map/all_to_all | solution.py:284
  118.9 0.0 copy-done.1
  119.0 0.6 combine.1.head_values
  119.5 2.0 %copy-done = bf16[256,7168]{1,0:T(8,128)(2,1)S(1)} copy-done((bf16[256,7168]{1,0:T(8,128)(2,1)S(1)}, bf16[256,7168]{1,0:T(8,128)(2,1)}, u32[]{:S(2)}) %copy-start) | copy-done | bytes 3670040
  121.6 1.7 project.1
  123.3 4.8 %all-to-all-start.3 = ((bf16[32,64,256]{2,1,0:T(8,128)(2,1)}), bf16[32,64,256]{2,1,0:T(8,128)(2,1)S(1)}, u32[]{:S(2)}, u32[]{:S(2)}) async-start(bf16[32,64,256]{2,1,0:T(8,128)(2,1)} %project.1), calls=%async_computation.3 | async-start | bytes 2097152 | tf_op jit(solution)/shard_map/all_to_all | solution.py:284
  128.2 0.0 copy-done.2
  128.2 0.0 copy-done.3
  128.2 0.6 slots.1
  128.8 27.6 %all-to-all-done.3.arrived = bf16[32,64,256]{2,1,0:T(8,128)(2,1)S(1)} async-done(((bf16[32,64,256]{2,1,0:T(8,128)(2,1)}), bf16[32,64,256]{2,1,0:T(8,128)(2,1)S(1)}, u32[]{:S(2)}, u32[]{:S(2)}) %all-to-all-start.3) | async-done | bytes 1048608 | tf_op jit(solution)/shard_map/all_to_all | solution.py:284
  156.4 1.1 dispatch.1
  157.5 5.6 %all-to-all-start.4 = ((bf16[32,24,256]{2,1,0:T(8,128)(2,1)}), bf16[32,24,256]{2,1,0:T(8,128)(2,1)S(1)}, u32[]{:S(2)}, u32[]{:S(2)}) async-start(bf16[32,24,256]{2,1,0:T(8,128)(2,1)} %bitcast.10), calls=%async_computation.4 | async-start | bytes 786432 | tf_op jit(solution)/shard_map/all_to_all | solution.py:284
  163.1 0.0 copy-done.6
  163.2 0.1 dynamic-slice_reduce_fusion
  163.3 0.1 reshape.35
  163.4 0.7 copy.14
  164.0 13.7 %all-to-all-done.4.arrived = bf16[32,24,256]{2,1,0:T(8,128)(2,1)S(1)} async-done(((bf16[32,24,256]{2,1,0:T(8,128)(2,1)}), bf16[32,24,256]{2,1,0:T(8,128)(2,1)S(1)}, u32[]{:S(2)}, u32[]{:S(2)}) %all-to-all-start.4) | async-done | bytes 393248 | tf_op jit(solution)/shard_map/all_to_all | solution.py:284
  177.7 1.1 norm.1
  (7 shorter events, 0.1 us)
Async XLA Ops:
  0.6 35.0 %all-to-all-start = ((bf16[8,24,576]{2,1,0:T(8,128)(2,1)}), bf16[8,24,576]{2,1,0:T(8,128)(2,1)S(1)}, u32[]{:S(2)}, u32[]{:S(2)}) async-start(bf16[8,24,576]{2,1,0:T(8,128)(2,1)} %bitcast.25), calls=%async_computation | async-start | bytes 491520 | tf_op jit(solution)/shard_map/all_to_all | solution.py:284
  10.7 19.3 %collective-permute-start = (bf16[128,576]{1,0:T(8,128)(2,1)S(1)}, bf16[128,576]{1,0:T(8,128)(2,1)S(1)}, u32[]{:S(2)}, u32[]{:S(2)}) collective-permute-start(bf16[128,576]{1,0:T(8,128)(2,1)S(1)} %bitcast.12), channel_id=1, source_target_pairs={{0,4},{4,8},{8,12},{12,16},{16,20},{20,24},{24,28},{28,0},{1,5},{5... | collective-permute-start | bytes 442376 | tf_op jit(solution)/shard_map/ppermute | solution.py:305
  13.4 16.6 %collective-permute-start.1 = (bf16[128,576]{1,0:T(8,128)(2,1)S(1)}, bf16[128,576]{1,0:T(8,128)(2,1)S(1)}, u32[]{:S(2)}, u32[]{:S(2)}) collective-permute-start(bf16[128,576]{1,0:T(8,128)(2,1)S(1)} %bitcast.13), channel_id=1, source_target_pairs={{0,28},{4,0},{8,4},{12,8},{16,12},{20,16},{24,20},{28,24},{1,29},{... | collective-permute-start | bytes 442376 | tf_op jit(solution)/shard_map/ppermute | solution.py:305
  22.0 12.6 %collective-permute-start.2 = (bf16[128,576]{1,0:T(8,128)(2,1)S(1)}, bf16[128,576]{1,0:T(8,128)(2,1)S(1)}, u32[]{:S(2)}, u32[]{:S(2)}) collective-permute-start(bf16[128,576]{1,0:T(8,128)(2,1)S(1)} %bitcast.14), channel_id=1, source_target_pairs={{0,8},{4,12},{8,16},{12,20},{16,24},{20,28},{24,0},{28,4},{1,9},{5... | collective-permute-start | bytes 442376 | tf_op jit(solution)/shard_map/ppermute | solution.py:305
  23.9 11.7 %collective-permute-start.3 = (bf16[128,576]{1,0:T(8,128)(2,1)S(1)}, bf16[128,576]{1,0:T(8,128)(2,1)S(1)}, u32[]{:S(2)}, u32[]{:S(2)}) collective-permute-start(bf16[128,576]{1,0:T(8,128)(2,1)S(1)} %bitcast.15), channel_id=1, source_target_pairs={{0,24},{4,28},{8,0},{12,4},{16,8},{20,12},{24,16},{28,20},{1,25},{... | collective-permute-start | bytes 442376 | tf_op jit(solution)/shard_map/ppermute | solution.py:305
  35.6 3.4 %collective-permute-start.4 = (bf16[8,24,576]{2,1,0:T(8,128)(2,1)S(1)}, bf16[8,24,576]{2,1,0:T(8,128)(2,1)S(1)}, u32[]{:S(2)}, u32[]{:S(2)}) collective-permute-start(bf16[8,24,576]{2,1,0:T(8,128)(2,1)S(1)} %all-to-all-done.mine), channel_id=1, source_target_pairs={{0,32},{32,0},{1,33},{33,1},{2,34},{34,2},{3,35},{35,3},{4,36},{36... | collective-permute-start | bytes 663560 | tf_op jit(solution)/shard_map/ppermute | solution.py:310
  39.0 0.7 copy-start.4
  41.1 21.5 %all-to-all-start.1 = ((bf16[8,24,576]{2,1,0:T(8,128)(2,1)}), bf16[8,24,576]{2,1,0:T(8,128)(2,1)S(1)}, u32[]{:S(2)}, u32[]{:S(2)}) async-start(bf16[8,24,576]{2,1,0:T(8,128)(2,1)} %pick.1), calls=%async_computation.1 | async-start | bytes 491520 | tf_op jit(solution)/shard_map/all_to_all | solution.py:284
  48.3 28.8 %collective-permute-start.5 = (bf16[128,576]{1,0:T(8,128)(2,1)S(1)}, bf16[128,576]{1,0:T(8,128)(2,1)S(1)}, u32[]{:S(2)}, u32[]{:S(2)}) collective-permute-start(bf16[128,576]{1,0:T(8,128)(2,1)S(1)} %bitcast.16), channel_id=1, source_target_pairs={{0,12},{4,16},{8,20},{12,24},{16,28},{20,0},{24,4},{28,8},{1,13},{... | collective-permute-start | bytes 442376 | tf_op jit(solution)/shard_map/ppermute | solution.py:305
  53.9 23.2 %collective-permute-start.6 = (bf16[128,576]{1,0:T(8,128)(2,1)S(1)}, bf16[128,576]{1,0:T(8,128)(2,1)S(1)}, u32[]{:S(2)}, u32[]{:S(2)}) collective-permute-start(bf16[128,576]{1,0:T(8,128)(2,1)S(1)} %bitcast.17), channel_id=1, source_target_pairs={{0,16},{4,20},{8,24},{12,28},{16,0},{20,4},{24,8},{28,12},{1,17},{... | collective-permute-start | bytes 442376 | tf_op jit(solution)/shard_map/ppermute | solution.py:305
  58.1 20.9 %collective-permute-start.7 = (bf16[128,576]{1,0:T(8,128)(2,1)S(1)}, bf16[128,576]{1,0:T(8,128)(2,1)S(1)}, u32[]{:S(2)}, u32[]{:S(2)}) collective-permute-start(bf16[128,576]{1,0:T(8,128)(2,1)S(1)} %bitcast.18), channel_id=1, source_target_pairs={{0,20},{4,24},{8,28},{12,0},{16,4},{20,8},{24,12},{28,16},{1,21},{... | collective-permute-start | bytes 442376 | tf_op jit(solution)/shard_map/ppermute | solution.py:305
  83.3 4.1 %copy-start.5 = (bf16[1,16,4,576]{3,2,1,0:T(4,128)(2,1)S(1)}, bf16[1,16,4,576]{3,2,1,0:T(4,128)(2,1)}, u32[]{:S(2)}) copy-start(bf16[1,16,4,576]{3,2,1,0:T(4,128)(2,1)} %param.12) | copy-start | bytes 221188
  83.3 35.6 %copy-start.1 = (bf16[2,512,128]{2,1,0:T(8,128)(2,1)S(1)}, bf16[2,512,128]{2,1,0:T(8,128)(2,1)}, u32[]{:S(2)}) copy-start(bf16[2,512,128]{2,1,0:T(8,128)(2,1)} %value_up.1) | copy-start | bytes 786436
  83.3 35.6 %all-to-all-start.2 = ((bf16[8,144,512]{2,1,0:T(8,128)(2,1)}), bf16[8,144,512]{2,1,0:T(8,128)(2,1)S(1)}, u32[]{:S(2)}, u32[]{:S(2)}) async-start(bf16[8,144,512]{2,1,0:T(8,128)(2,1)} %prompt_attention.1), calls=%async_computation.2 | async-start | bytes 2359296 | tf_op jit(solution)/shard_map/all_to_all | solution.py:284
  119.5 2.0 %copy-start = (bf16[256,7168]{1,0:T(8,128)(2,1)S(1)}, bf16[256,7168]{1,0:T(8,128)(2,1)}, u32[]{:S(2)}) copy-start(bf16[256,7168]{1,0:T(8,128)(2,1)} %weight.1) | copy-start | bytes 11010052
  123.3 4.8 %copy-start.2 = (s32[64,8]{0,1:T(8,128)S(1)}, s32[64,8]{0,1:T(8,128)}, u32[]{:S(2)}) copy-start(s32[64,8]{0,1:T(8,128)} %param.16) | copy-start | bytes 6148
  123.3 4.8 %copy-start.3 = (f32[64,8]{0,1:T(8,128)S(1)}, f32[64,8]{0,1:T(8,128)}, u32[]{:S(2)}) copy-start(f32[64,8]{0,1:T(8,128)} %param.17) | copy-start | bytes 6148
  123.3 33.0 %all-to-all-start.3 = ((bf16[32,64,256]{2,1,0:T(8,128)(2,1)}), bf16[32,64,256]{2,1,0:T(8,128)(2,1)S(1)}, u32[]{:S(2)}, u32[]{:S(2)}) async-start(bf16[32,64,256]{2,1,0:T(8,128)(2,1)} %project.1), calls=%async_computation.3 | async-start | bytes 2097152 | tf_op jit(solution)/shard_map/all_to_all | solution.py:284
  156.4 6.7 %copy-start.6 = (bf16[7168]{0:T(1024)(128)(2,1)S(1)}, bf16[7168]{0:T(1024)(128)(2,1)}, u32[]{:S(2)}) copy-start(bf16[7168]{0:T(1024)(128)(2,1)} %param.15) | copy-start | bytes 43012
  157.5 20.2 %all-to-all-start.4 = ((bf16[32,24,256]{2,1,0:T(8,128)(2,1)}), bf16[32,24,256]{2,1,0:T(8,128)(2,1)S(1)}, u32[]{:S(2)}, u32[]{:S(2)}) async-start(bf16[32,24,256]{2,1,0:T(8,128)(2,1)} %bitcast.10), calls=%async_computation.4 | async-start | bytes 786432 | tf_op jit(solution)/shard_map/all_to_all | solution.py:284

commit v5 on v4

--- a/solution.py
+++ b/solution.py
@@ -17,17 +17,19 @@
 EPSILON = 1e-06
 SCALE = QK_DIM ** (-0.5)
 
-NY, NZ, NX = 8, 8, 4
-DEVS = NZ * NX
+NY, NQ, NL, NX = 8, 4, 2, 4
+NEAR = NX * NL
+DEVS = NQ * NEAR
 PIECE = 192 // NY
-KEYS = 192 * NX
+KEYS = 192 * NEAR
 MINE = 2 * ROWS
 SENT = MINE + 16
 SLOTS = EXPERTS * CAP
 OWN_SLOTS = SLOTS // DEVS
+SPAN = D // NEAR
 BLOCK = 256
-BLOCKS = D // BLOCK
-STEP = 4
+WIDTHS = [min(BLOCK, SPAN - q * BLOCK) for q in range(NQ)]
+STEP = 2
 
 bf16 = jnp.bfloat16
 f32 = jnp.float32
@@ -90,16 +92,16 @@
     return high, mid, rest - mid
 
 
-def attention_kernel(z, keys, *refs):
-    queries, out = refs[:NZ], refs[NZ]
+def attention_kernel(zq, keys, *refs):
+    queries, out = refs[:NQ], refs[NQ]
     index = lax.broadcasted_iota(jnp.int32, (16, 128), 0)
-    for step in range(NZ // STEP):
+    for step in range(NQ // STEP):
         shifts = range(step * STEP, (step + 1) * STEP)
         query = jnp.concatenate([queries[k][...] for k in shifts], axis=0)
         best, total, latent = attend(query, keys[...])
         for i, k in enumerate(shifts):
             part = slice(i * MINE, (i + 1) * MINE)
-            owner = (z[0] + NZ - k) & (NZ - 1)
+            owner = (zq[0] + NQ - k) & (NQ - 1)
             out[owner, :MINE, :] = latent[part]
             rows = three(columns_to_lanes(best[part])) + three(columns_to_lanes(total[part]))
             table = jnp.zeros((16, 128), f32)
@@ -109,15 +111,15 @@
             out[owner, MINE:, 128:] = jnp.zeros((16, LAT_KV - 128), bf16)
 
 
-def prompt_attention(z, keys, queries):
+def prompt_attention(zq, keys, queries):
     return pl.pallas_call(
         attention_kernel,
-        out_shape=jax.ShapeDtypeStruct((NZ, SENT, LAT_KV), bf16),
-        in_specs=[SMEM] + [VMEM] * (1 + NZ),
+        out_shape=jax.ShapeDtypeStruct((NQ, SENT, LAT_KV), bf16),
+        in_specs=[SMEM] + [VMEM] * (1 + NQ),
         out_specs=VMEM,
         compiler_params=params(),
         name="prompt_attention",
-    )(z, keys, *queries)
+    )(zq, keys, *queries)
 
 
 def own_kernel(query, keys, latents, stats):
@@ -150,7 +152,7 @@
 
 def combine_kernel(arrived, own_latents, own_stats, value_up, out):
     bests, totals = [own_stats[0:1, :]], [own_stats[1:2, :]]
-    for z in range(NZ):
+    for z in range(NQ):
         stats = arrived[z, MINE:, :128].astype(f32)
         bests.append(stats[0:1] + stats[1:2] + stats[2:3])
         totals.append(stats[3:4] + stats[4:5] + stats[5:6])
@@ -167,7 +169,7 @@
         table = jnp.where(index == i, jnp.broadcast_to(share / whole, (128, 128)), table)
     table = jnp.transpose(table)
     latent = table[:, 0:1] * own_latents[...].astype(f32)
-    for z in range(NZ):
+    for z in range(NQ):
         latent = latent + table[:, z + 1 : z + 2] * arrived[z, :MINE, :].astype(f32)
     latent = latent.astype(bf16)
     for head in range(2):
@@ -186,23 +188,53 @@
     )(arrived, own_latents, own_stats, value_up)
 
 
-def project_kernel(head_values, weight, out):
-    for block in range(BLOCKS):
-        part = slice(block * BLOCK, (block + 1) * BLOCK)
-        out[block] = dot(head_values[...], weight[:, part]).astype(bf16)
-    for block in range(BLOCKS, DEVS):
-        out[block] = jnp.zeros((ROWS, BLOCK), bf16)
+def project_kernel(head_values, weight, out, held, sems):
+    copies = [
+        pltpu.make_async_copy(weight.at[:, i * SPAN : (i + 1) * SPAN], held.at[i], sems.at[i])
+        for i in range(NEAR)
+    ]
+    for copy in copies:
+        copy.start()
+    for i, copy in enumerate(copies):
+        copy.wait()
+        out[i] = dot(head_values[...], held[i]).astype(bf16)
 
 
 def project(head_values, weight):
     return pl.pallas_call(
         project_kernel,
-        out_shape=jax.ShapeDtypeStruct((DEVS, ROWS, BLOCK), bf16),
-        in_specs=[VMEM] * 2,
-        out_specs=VMEM,
+        out_shape=jax.ShapeDtypeStruct((NEAR, ROWS, SPAN), bf16),
+        in_specs=[VMEM, pl.BlockSpec(memory_space=pltpu.HBM)],
+        out_specs=VMEM,
+        scratch_shapes=[
+            pltpu.VMEM((NEAR, 2 * HEAD_V, SPAN), bf16),
+            pltpu.SemaphoreType.DMA((NEAR,)),
+        ],
         compiler_params=params(),
         name="project",
     )(head_values, weight)
+
+
+def add_kernel(arrived, out):
+    total = arrived[0].astype(f32)
+    for i in range(1, NEAR):
+        total = total + arrived[i].astype(f32)
+    total = total.astype(bf16)
+    for q, width in enumerate(WIDTHS):
+        out[q, :, :width] = total[:, q * BLOCK : q * BLOCK + width]
+        if width < BLOCK:
+            out[q, :, width:] = jnp.zeros((ROWS, BLOCK - width), bf16)
+
+
+def add(arrived):
+    return pl.pallas_call(
+        add_kernel,
+        out_shape=jax.ShapeDtypeStruct((NQ, ROWS, BLOCK), bf16),
+        in_specs=[VMEM],
+        out_specs=VMEM,
+        compiler_params=params(),
+        name="add",
+    )(arrived)
 
 
 def slots_kernel(routes, gates, picks, slot_gates):
@@ -240,8 +272,8 @@
 
 def dispatch_kernel(arrived, picks, out):
     total = arrived[0].astype(f32)
-    for dev in range(1, DEVS):
-        total = total + arrived[dev].astype(f32)
+    for q in range(1, NQ):
+        total = total + arrived[q].astype(f32)
     out[...] = dot(picks[...], total.astype(bf16)).astype(bf16)
 
 
@@ -257,13 +289,22 @@
 
 
 def norm_kernel(arrived, gain, out):
-    blocks = [arrived[block].astype(f32) for block in range(BLOCKS)]
-    square = blocks[0] * blocks[0]
-    for block in blocks[1:]:
-        square = square + block * block
+    blocks = []
+    for x in range(NX):
+        for zl in range(NL):
+            for q, width in enumerate(WIDTHS):
+                block = arrived[(q * NL + zl) * NX + x]
+                blocks.append(block[:, :width].astype(f32))
+    square = jnp.zeros((OWN_SLOTS, 128), f32)
+    for block in blocks:
+        for lane in range(0, block.shape[1], 128):
+            part = block[:, lane : lane + 128]
+            square = square + part * part
     scale = lax.rsqrt(jnp.sum(square, axis=1, keepdims=True) * (1.0 / D) + EPSILON)
-    for i, block in enumerate(blocks):
-        part = slice(i * BLOCK, (i + 1) * BLOCK)
+    start = 0
+    for block in blocks:
+        part = slice(start, start + block.shape[1])
+        start = start + block.shape[1]
         normed = block * scale * gain[:, part].astype(f32)
         for expert in range(OWN_SLOTS // CAP):
             out[expert, :, part] = normed[expert * CAP : (expert + 1) * CAP]
@@ -296,38 +337,38 @@
     gates,
 ):
     core = lax.axis_index("core")[None].astype(jnp.int32)
-    z = lax.axis_index("z")[None].astype(jnp.int32)
-    dev = lax.axis_index("z") * NX + lax.axis_index("x")
+    zq = lax.axis_index("zq")[None].astype(jnp.int32)
+    dev = (lax.axis_index("zq") * NL + lax.axis_index("zl")) * NX + lax.axis_index("x")
 
     query = queries.reshape(ROWS, 2, LAT).transpose(1, 0, 2).reshape(MINE, LAT)
 
     def shifted(k):
-        return lax.ppermute(query, "z", [(i, (i + k) % NZ) for i in range(NZ)])
+        return lax.ppermute(query, "zq", [(i, (i + k) % NQ) for i in range(NQ)])
 
     pieces = exchange(prompt_cache.reshape(NY, PIECE, LAT), "y")
-    near = [1, NZ - 1, 2, NZ - 2]
-    pieces, *arrived = lax.optimization_barrier((pieces, *[shifted(k) for k in near]))
+    pieces, one, three_ = lax.optimization_barrier((pieces, shifted(1), shifted(3)))
     other = lax.ppermute(pieces, "core", [(0, 1), (1, 0)])
     served = exchange(pick(core, prompt_of_group, pieces, other), "y").reshape(NY * PIECE, LAT)
-    keys = lax.all_gather(served, "x", axis=0, tiled=True)
-    far = [k for k in range(1, NZ) if k not in near]
-    by_shift = dict(zip(near + far, arrived + [shifted(k) for k in far]))
-    all_queries = [query] + [by_shift[k] for k in range(1, NZ)]
+    served, two = lax.optimization_barrier((served, shifted(2)))
+    keys = exchange(jnp.broadcast_to(served, (NEAR, NY * PIECE, LAT)), ("x", "zl"))
+    keys = keys.reshape(KEYS, LAT)
+    all_queries = [query, one, two, three_]
     own_latents, own_stats = own_attention(query, new_latents.reshape(ROWS, LAT))
     picks, all_gates = slots(routes.T, gates.T)
     slot_gates = lax.dynamic_slice_in_dim(all_gates, dev * OWN_SLOTS, OWN_SLOTS, 0)
 
-    partial = exchange(prompt_attention(z, keys, all_queries), "z")
+    partial = exchange(prompt_attention(zq, keys, all_queries), "zq")
     head_values = combine(partial, own_latents, own_stats, value_up)
-    sums = exchange(project(head_values, out_weight), ("z", "x"))
+    sums = exchange(add(exchange(project(head_values, out_weight), ("x", "zl"))), "zq")
     rows = dispatch(sums, picks).reshape(DEVS, OWN_SLOTS, BLOCK)
-    slot_rows = norm(exchange(rows, ("z", "x")), norm_gain.reshape(1, D))
+    slot_rows = norm(exchange(rows, ("zq", "zl", "x")), norm_gain.reshape(1, D))
     return (slot_rows[None], slot_gates.reshape(1, OWN_SLOTS // CAP, CAP))
 
 
 def solution(mesh):
-    fine = Mesh(mesh.devices.reshape(NY, 2, NZ, NX), ("y", "core", "z", "x"))
-    group, dev = ("y", "core"), ("z", "x")
+    axes = ("y", "core", "zq", "zl", "x")
+    fine = Mesh(mesh.devices.reshape(NY, 2, NQ, NL, NX), axes)
+    group, dev = axes[:2], axes[2:]
     return jax.shard_map(
         local,
         mesh=fine,

time: 180 us -> 169 us (0.939)
  starting transfers between devices: 66.3 us -> 56.3 us
  waiting for transfers between devices: 81.3 us -> 74.6 us
  blocking collectives: 14.5 us -> 18.6 us
    all_to_all x0 -> x1, blocking collectives: none -> 18.6 us  [exchange(): return lax.all_to_all(value, axes, split_axis=0, concat_axis=0, tiled=True)]
    ppermute x7 -> x3, starting transfers between devices: 33.5 us -> 16.8 us  [shifted(): return lax.ppermute(query, 'zq', [(i, (i + k) % NQ) for i in range(NQ)])]
    all_gather x1 -> x0, blocking collectives: 14.5 us -> none  [local(): keys = lax.all_gather(served, 'x', axis=0, tiled=True)]
    all_to_all x5 -> x6, waiting for transfers between devices: 72.2 us -> 59.5 us  [exchange(): return lax.all_to_all(value, axes, split_axis=0, concat_axis=0, tiled=True)]
    all_to_all x5 -> x6, starting transfers between devices: 30.9 us -> 37.6 us  [exchange(): return lax.all_to_all(value, axes, split_axis=0, concat_axis=0, tiled=True)]
    ppermute x7 -> x3, waiting for transfers between devices: 7.58 us -> 13.6 us  [shifted(): return lax.ppermute(query, 'zq', [(i, (i + k) % NQ) for i in range(NQ)])]
    pallas_call x2 -> x3, Pallas kernels: 6.01 us -> 6.59 us  [the longest x1 3.68 us: prompt_attention(): pl.pallas_call(attention_kernel, out_shape=jax.ShapeDtypeStruct((NQ, SENT...]
  transfers between devices with their start and end apart: 13 -> 10, of which waited for: 7 -> 8; matrix products, arithmetic and copies ran while one was open for 1% -> 1% of each run, Pallas kernels for 1% -> 1%
where the time goes in v5:
time: 169 us; the launch traced here: 168 us
  waiting for transfers between devices  74.6 us (44%)
  starting transfers between devices  56.3 us (33%)
  blocking collectives  18.6 us (11%)
  Pallas kernels  11.7 us (7%)
  local copies, waits for them, and re-layouts  6.04 us (4%)
    all_to_all x6, waiting for transfers between devices, exchange(): return lax.all_to_all(value, axes, split_axis=0, concat_axis=0, tiled=True)  59.5 us
    all_to_all x6, starting transfers between devices, exchange(): return lax.all_to_all(value, axes, split_axis=0, concat_axis=0, tiled=True)  37.6 us
    all_to_all x1, blocking collectives, exchange(): return lax.all_to_all(value, axes, split_axis=0, concat_axis=0, tiled=True)  18.6 us
    ppermute x3, starting transfers between devices, shifted(): return lax.ppermute(query, 'zq', [(i, (i + k) % NQ) for i in range(NQ)])  16.8 us
    ppermute x3, waiting for transfers between devices, shifted(): return lax.ppermute(query, 'zq', [(i, (i + k) % NQ) for i in range(NQ)])  13.6 us
    pallas_call x1, Pallas kernels, prompt_attention(): pl.pallas_call(attention_kernel, out_shape=jax.ShapeDtypeStruct((NQ, SENT...  3.68 us
    unnamed x15, local copies, waits for them, and re-layouts  3.39 us
  transfers between devices with their start and end apart: 10, of which 8 were waited for; matrix products, arithmetic and copies ran while one was open for 1% of the time, Pallas kernels for 1%

profile of v5, /device:TPU:8, one launch (start us, length us, event | category | flops | bytes accessed | tf_op | source)
XLA Modules:
  0.0 167.9 jit_solution(10075094441072098598)
XLA Ops:
  0.6 9.1 %all-to-all-start = ((bf16[8,24,576]{2,1,0:T(8,128)(2,1)}), bf16[8,24,576]{2,1,0:T(8,128)(2,1)S(1)}, u32[]{:S(2)}, u32[]{:S(2)}) async-start(bf16[8,24,576]{2,1,0:T(8,128)(2,1)} %bitcast.23), calls=%async_computation | async-start | bytes 491520 | tf_op jit(solution)/shard_map/all_to_all | solution.py:325
  9.8 0.9 copy.13
  10.7 4.5 %collective-permute-start = (bf16[128,576]{1,0:T(8,128)(2,1)S(1)}, bf16[128,576]{1,0:T(8,128)(2,1)S(1)}, u32[]{:S(2)}, u32[]{:S(2)}) collective-permute-start(bf16[128,576]{1,0:T(8,128)(2,1)S(1)} %bitcast.14), channel_id=1, source_target_pairs={{0,8},{8,16},{16,24},{24,0},{1,9},{9,17},{17,25},{25,1},{2,10},{10... | collective-permute-start | bytes 442376 | tf_op jit(solution)/shard_map/ppermute | solution.py:346
  15.2 6.8 %collective-permute-start.1 = (bf16[128,576]{1,0:T(8,128)(2,1)S(1)}, bf16[128,576]{1,0:T(8,128)(2,1)S(1)}, u32[]{:S(2)}, u32[]{:S(2)}) collective-permute-start(bf16[128,576]{1,0:T(8,128)(2,1)S(1)} %bitcast.15), channel_id=1, source_target_pairs={{0,24},{8,0},{16,8},{24,16},{1,25},{9,1},{17,9},{25,17},{2,26},{10... | collective-permute-start | bytes 442376 | tf_op jit(solution)/shard_map/ppermute | solution.py:346
  22.0 1.8 %collective-permute-done.refs_1_ = bf16[128,576]{1,0:T(8,128)(2,1)S(1)} collective-permute-done((bf16[128,576]{1,0:T(8,128)(2,1)S(1)}, bf16[128,576]{1,0:T(8,128)(2,1)S(1)}, u32[]{:S(2)}, u32[]{:S(2)}) %collective-permute-start) | collective-permute-done | bytes 147488 | tf_op jit(solution)/shard_map/ppermute | solution.py:346
  23.8 5.6 %collective-permute-done.1.refs_3_ = bf16[128,576]{1,0:T(8,128)(2,1)S(1)} collective-permute-done((bf16[128,576]{1,0:T(8,128)(2,1)S(1)}, bf16[128,576]{1,0:T(8,128)(2,1)S(1)}, u32[]{:S(2)}, u32[]{:S(2)}) %collective-permute-start.1) | collective-permute-done | bytes 147488 | tf_op jit(solution)/shard_map/ppermute | solution.py:346
  29.4 0.0 all-to-all-done.mine
  29.4 1.9 %collective-permute-start.2 = (bf16[8,24,576]{2,1,0:T(8,128)(2,1)S(1)}, bf16[8,24,576]{2,1,0:T(8,128)(2,1)S(1)}, u32[]{:S(2)}, u32[]{:S(2)}) collective-permute-start(bf16[8,24,576]{2,1,0:T(8,128)(2,1)S(1)} %all-to-all-done.mine), channel_id=1, source_target_pairs={{0,32},{32,0},{1,33},{33,1},{2,34},{34,2},{3,35},{35,3},{4,36},{36... | collective-permute-start | bytes 663560 | tf_op jit(solution)/shard_map/ppermute | solution.py:350
  31.4 1.5 collective-permute-done.2.other
  32.8 0.0 copy-start.4
  32.8 0.7 copy-done.4
  33.5 1.4 pick.1
  34.9 7.2 %all-to-all-start.1 = ((bf16[8,24,576]{2,1,0:T(8,128)(2,1)}), bf16[8,24,576]{2,1,0:T(8,128)(2,1)S(1)}, u32[]{:S(2)}, u32[]{:S(2)}) async-start(bf16[8,24,576]{2,1,0:T(8,128)(2,1)} %pick.1), calls=%async_computation.1 | async-start | bytes 491520 | tf_op jit(solution)/shard_map/all_to_all | solution.py:325
  42.1 5.5 %collective-permute-start.3 = (bf16[128,576]{1,0:T(8,128)(2,1)S(1)}, bf16[128,576]{1,0:T(8,128)(2,1)S(1)}, u32[]{:S(2)}, u32[]{:S(2)}) collective-permute-start(bf16[128,576]{1,0:T(8,128)(2,1)S(1)} %bitcast.16), channel_id=1, source_target_pairs={{0,16},{8,24},{16,0},{24,8},{1,17},{9,25},{17,1},{25,9},{2,18},{10... | collective-permute-start | bytes 442376 | tf_op jit(solution)/shard_map/ppermute | solution.py:346
  47.6 6.2 %collective-permute-done.3.refs_2_ = bf16[128,576]{1,0:T(8,128)(2,1)S(1)} collective-permute-done((bf16[128,576]{1,0:T(8,128)(2,1)S(1)}, bf16[128,576]{1,0:T(8,128)(2,1)S(1)}, u32[]{:S(2)}, u32[]{:S(2)}) %collective-permute-start.3) | collective-permute-done | bytes 147488 | tf_op jit(solution)/shard_map/ppermute | solution.py:346
  53.8 0.0 all-to-all-done.1
  53.8 1.5 broadcast_in_dim.14
  55.3 4.3 %all-to-all-start.2 = ((bf16[8,192,576]{2,1,0:T(8,128)(2,1)}), bf16[8,192,576]{2,1,0:T(8,128)(2,1)S(1)}, u32[]{:S(2)}, u32[]{:S(2)}) async-start(bf16[8,192,576]{2,1,0:T(8,128)(2,1)} %broadcast_in_dim.14), calls=%async_computation.2 | async-start | bytes 3932160 | tf_op jit(solution)/shard_map/all_to_all | solution.py:325
  59.6 24.1 %all-to-all-done.2 = bf16[8,192,576]{2,1,0:T(8,128)(2,1)S(1)} async-done(((bf16[8,192,576]{2,1,0:T(8,128)(2,1)}), bf16[8,192,576]{2,1,0:T(8,128)(2,1)S(1)}, u32[]{:S(2)}, u32[]{:S(2)}) %all-to-all-start.2) | async-done | bytes 1769504 | tf_op jit(solution)/shard_map/all_to_all | solution.py:325
  83.7 0.0 copy-start.5
  83.7 0.0 copy-start.1
  83.7 3.7 %prompt_attention.1 = bf16[4,144,512]{2,1,0:T(8,128)(2,1)} custom-call(s32[1]{0:T(128)} %bitcast.zq, bf16[1536,576]{1,0:T(8,128)(2,1)S(1)} %bitcast.13, bf16[128,576]{1,0:T(8,128)(2,1)S(1)} %bitcast.17, bf16[128,576]{1,0:T(8,128)(2,1)S(1)} %collective-permute-done.refs_1_, bf16[128,576]{1,0:T(8,128)(2,1)S(1)} %collective-permute-done.3.refs_2_, ...), custom_call_target="tpu_custom_call" | custom-call | tf_op jit(solution)/shard_map/prompt_attention/pallas_call | solution.py:115
  87.4 9.7 %all-to-all-start.3 = ((bf16[4,144,512]{2,1,0:T(8,128)(2,1)}), bf16[4,144,512]{2,1,0:T(8,128)(2,1)S(1)}, u32[]{:S(2)}, u32[]{:S(2)}) async-start(bf16[4,144,512]{2,1,0:T(8,128)(2,1)} %prompt_attention.1), calls=%async_computation.3 | async-start | bytes 1179648 | tf_op jit(solution)/shard_map/all_to_all | solution.py:325
  97.1 0.0 copy-done.5
  97.1 0.5 own_attention.1
  97.6 15.1 %all-to-all-done.3.arrived = bf16[4,144,512]{2,1,0:T(8,128)(2,1)S(1)} async-done(((bf16[4,144,512]{2,1,0:T(8,128)(2,1)}), bf16[4,144,512]{2,1,0:T(8,128)(2,1)S(1)}, u32[]{:S(2)}, u32[]{:S(2)}) %all-to-all-start.3) | async-done | bytes 589856 | tf_op jit(solution)/shard_map/all_to_all | solution.py:325
  112.7 0.0 copy-done.1
  112.7 0.4 combine.1.head_values
  113.2 2.0 %copy-done = bf16[256,7168]{1,0:T(8,128)(2,1)S(1)} copy-done((bf16[256,7168]{1,0:T(8,128)(2,1)S(1)}, bf16[256,7168]{1,0:T(8,128)(2,1)}, u32[]{:S(2)}) %copy-start) | copy-done | bytes 3670040
  115.2 2.1 %project.1 = bf16[8,64,896]{2,1,0:T(8,128)(2,1)S(1)} custom-call(bf16[64,256]{1,0:T(8,128)(2,1)S(1)} %combine.1.head_values, bf16[256,7168]{1,0:T(8,128)(2,1)S(1)} %copy-done), custom_call_target="tpu_custom_call" | custom-call | tf_op jit(solution)/shard_map/project/pallas_call | solution.py:204
  117.4 0.0 copy-start.2
  117.4 0.0 copy-start.3
  117.4 0.0 copy-start.6
  117.4 18.6 %all_to_all.35.arrived = bf16[8,64,896]{2,1,0:T(8,128)(2,1)S(1)} all-to-all(bf16[8,64,896]{2,1,0:T(8,128)(2,1)S(1)} %project.1), channel_id=1, replica_groups=mesh['y'=8,'core'=2,'zq'=4,'zl'=2,'x'=4] {'x','zl'}, dimensions={0} | all-to-all | bytes 1835008 | tf_op jit(solution)/shard_map/all_to_all | solution.py:325
  136.0 0.8 add.14
  136.8 3.4 %all-to-all-start.5 = ((bf16[4,64,256]{2,1,0:T(8,128)(2,1)}), bf16[4,64,256]{2,1,0:T(8,128)(2,1)S(1)}, u32[]{:S(2)}, u32[]{:S(2)}) async-start(bf16[4,64,256]{2,1,0:T(8,128)(2,1)} %add.14), calls=%async_computation.5 | async-start | bytes 262144 | tf_op jit(solution)/shard_map/all_to_all | solution.py:325
  140.1 0.0 copy-done.2
  140.1 0.0 copy-done.3
  140.1 0.6 slots.1
  140.7 8.1 %all-to-all-done.5.arrived = bf16[4,64,256]{2,1,0:T(8,128)(2,1)S(1)} async-done(((bf16[4,64,256]{2,1,0:T(8,128)(2,1)}), bf16[4,64,256]{2,1,0:T(8,128)(2,1)S(1)}, u32[]{:S(2)}, u32[]{:S(2)}) %all-to-all-start.5) | async-done | bytes 131104 | tf_op jit(solution)/shard_map/all_to_all | solution.py:325
  148.8 1.0 dispatch.1
  149.8 3.9 %all-to-all-start.6 = ((bf16[32,24,256]{2,1,0:T(8,128)(2,1)}), bf16[32,24,256]{2,1,0:T(8,128)(2,1)S(1)}, u32[]{:S(2)}, u32[]{:S(2)}) async-start(bf16[32,24,256]{2,1,0:T(8,128)(2,1)} %bitcast.11), calls=%async_computation.6 | async-start | bytes 786432 | tf_op jit(solution)/shard_map/all_to_all | solution.py:325
  153.7 0.0 copy-done.6
  153.8 0.1 dynamic-slice_reduce_fusion
  153.9 0.1 reshape.39
  154.0 0.7 copy.14
  154.6 12.1 %all-to-all-done.6.arrived = bf16[32,24,256]{2,1,0:T(8,128)(2,1)S(1)} async-done(((bf16[32,24,256]{2,1,0:T(8,128)(2,1)}), bf16[32,24,256]{2,1,0:T(8,128)(2,1)S(1)}, u32[]{:S(2)}, u32[]{:S(2)}) %all-to-all-start.6) | async-done | bytes 393248 | tf_op jit(solution)/shard_map/all_to_all | solution.py:325
  166.8 1.1 norm.1
  (3 shorter events, 0.1 us)
Async XLA Ops:
  0.6 28.8 %all-to-all-start = ((bf16[8,24,576]{2,1,0:T(8,128)(2,1)}), bf16[8,24,576]{2,1,0:T(8,128)(2,1)S(1)}, u32[]{:S(2)}, u32[]{:S(2)}) async-start(bf16[8,24,576]{2,1,0:T(8,128)(2,1)} %bitcast.23), calls=%async_computation | async-start | bytes 491520 | tf_op jit(solution)/shard_map/all_to_all | solution.py:325
  10.7 13.1 %collective-permute-start = (bf16[128,576]{1,0:T(8,128)(2,1)S(1)}, bf16[128,576]{1,0:T(8,128)(2,1)S(1)}, u32[]{:S(2)}, u32[]{:S(2)}) collective-permute-start(bf16[128,576]{1,0:T(8,128)(2,1)S(1)} %bitcast.14), channel_id=1, source_target_pairs={{0,8},{8,16},{16,24},{24,0},{1,9},{9,17},{17,25},{25,1},{2,10},{10... | collective-permute-start | bytes 442376 | tf_op jit(solution)/shard_map/ppermute | solution.py:346
  15.2 14.2 %collective-permute-start.1 = (bf16[128,576]{1,0:T(8,128)(2,1)S(1)}, bf16[128,576]{1,0:T(8,128)(2,1)S(1)}, u32[]{:S(2)}, u32[]{:S(2)}) collective-permute-start(bf16[128,576]{1,0:T(8,128)(2,1)S(1)} %bitcast.15), channel_id=1, source_target_pairs={{0,24},{8,0},{16,8},{24,16},{1,25},{9,1},{17,9},{25,17},{2,26},{10... | collective-permute-start | bytes 442376 | tf_op jit(solution)/shard_map/ppermute | solution.py:346
  29.4 3.4 %collective-permute-start.2 = (bf16[8,24,576]{2,1,0:T(8,128)(2,1)S(1)}, bf16[8,24,576]{2,1,0:T(8,128)(2,1)S(1)}, u32[]{:S(2)}, u32[]{:S(2)}) collective-permute-start(bf16[8,24,576]{2,1,0:T(8,128)(2,1)S(1)} %all-to-all-done.mine), channel_id=1, source_target_pairs={{0,32},{32,0},{1,33},{33,1},{2,34},{34,2},{3,35},{35,3},{4,36},{36... | collective-permute-start | bytes 663560 | tf_op jit(solution)/shard_map/ppermute | solution.py:350
  32.8 0.7 copy-start.4
  34.9 18.9 %all-to-all-start.1 = ((bf16[8,24,576]{2,1,0:T(8,128)(2,1)}), bf16[8,24,576]{2,1,0:T(8,128)(2,1)S(1)}, u32[]{:S(2)}, u32[]{:S(2)}) async-start(bf16[8,24,576]{2,1,0:T(8,128)(2,1)} %pick.1), calls=%async_computation.1 | async-start | bytes 491520 | tf_op jit(solution)/shard_map/all_to_all | solution.py:325
  42.1 11.7 %collective-permute-start.3 = (bf16[128,576]{1,0:T(8,128)(2,1)S(1)}, bf16[128,576]{1,0:T(8,128)(2,1)S(1)}, u32[]{:S(2)}, u32[]{:S(2)}) collective-permute-start(bf16[128,576]{1,0:T(8,128)(2,1)S(1)} %bitcast.16), channel_id=1, source_target_pairs={{0,16},{8,24},{16,0},{24,8},{1,17},{9,25},{17,1},{25,9},{2,18},{10... | collective-permute-start | bytes 442376 | tf_op jit(solution)/shard_map/ppermute | solution.py:346
  55.3 28.4 %all-to-all-start.2 = ((bf16[8,192,576]{2,1,0:T(8,128)(2,1)}), bf16[8,192,576]{2,1,0:T(8,128)(2,1)S(1)}, u32[]{:S(2)}, u32[]{:S(2)}) async-start(bf16[8,192,576]{2,1,0:T(8,128)(2,1)} %broadcast_in_dim.14), calls=%async_computation.2 | async-start | bytes 3932160 | tf_op jit(solution)/shard_map/all_to_all | solution.py:325
  83.7 13.4 %copy-start.5 = (bf16[1,16,4,576]{3,2,1,0:T(4,128)(2,1)S(1)}, bf16[1,16,4,576]{3,2,1,0:T(4,128)(2,1)}, u32[]{:S(2)}) copy-start(bf16[1,16,4,576]{3,2,1,0:T(4,128)(2,1)} %param.12) | copy-start | bytes 221188
  83.7 29.0 %copy-start.1 = (bf16[2,512,128]{2,1,0:T(8,128)(2,1)S(1)}, bf16[2,512,128]{2,1,0:T(8,128)(2,1)}, u32[]{:S(2)}) copy-start(bf16[2,512,128]{2,1,0:T(8,128)(2,1)} %value_up.1) | copy-start | bytes 786436
  87.4 25.3 %all-to-all-start.3 = ((bf16[4,144,512]{2,1,0:T(8,128)(2,1)}), bf16[4,144,512]{2,1,0:T(8,128)(2,1)S(1)}, u32[]{:S(2)}, u32[]{:S(2)}) async-start(bf16[4,144,512]{2,1,0:T(8,128)(2,1)} %prompt_attention.1), calls=%async_computation.3 | async-start | bytes 1179648 | tf_op jit(solution)/shard_map/all_to_all | solution.py:325
  113.2 2.1 %copy-start = (bf16[256,7168]{1,0:T(8,128)(2,1)S(1)}, bf16[256,7168]{1,0:T(8,128)(2,1)}, u32[]{:S(2)}) copy-start(bf16[256,7168]{1,0:T(8,128)(2,1)} %weight.1) | copy-start | bytes 11010052
  117.4 22.8 %copy-start.2 = (s32[64,8]{0,1:T(8,128)S(1)}, s32[64,8]{0,1:T(8,128)}, u32[]{:S(2)}) copy-start(s32[64,8]{0,1:T(8,128)} %param.16) | copy-start | bytes 6148
  117.4 22.7 %copy-start.3 = (f32[64,8]{0,1:T(8,128)S(1)}, f32[64,8]{0,1:T(8,128)}, u32[]{:S(2)}) copy-start(f32[64,8]{0,1:T(8,128)} %param.17) | copy-start | bytes 6148
  117.4 36.4 %copy-start.6 = (bf16[7168]{0:T(1024)(128)(2,1)S(1)}, bf16[7168]{0:T(1024)(128)(2,1)}, u32[]{:S(2)}) copy-start(bf16[7168]{0:T(1024)(128)(2,1)} %param.15) | copy-start | bytes 43012
  136.8 12.1 %all-to-all-start.5 = ((bf16[4,64,256]{2,1,0:T(8,128)(2,1)}), bf16[4,64,256]{2,1,0:T(8,128)(2,1)S(1)}, u32[]{:S(2)}, u32[]{:S(2)}) async-start(bf16[4,64,256]{2,1,0:T(8,128)(2,1)} %add.14), calls=%async_computation.5 | async-start | bytes 262144 | tf_op jit(solution)/shard_map/all_to_all | solution.py:325
  149.8 16.9 %all-to-all-start.6 = ((bf16[32,24,256]{2,1,0:T(8,128)(2,1)}), bf16[32,24,256]{2,1,0:T(8,128)(2,1)S(1)}, u32[]{:S(2)}, u32[]{:S(2)}) async-start(bf16[32,24,256]{2,1,0:T(8,128)(2,1)} %bitcast.11), calls=%async_computation.6 | async-start | bytes 786432 | tf_op jit(solution)/shard_map/all_to_all | solution.py:325

commit v6 on v3

--- a/solution.py
+++ b/solution.py
@@ -17,18 +17,20 @@
 EPSILON = 1e-06
 SCALE = QK_DIM ** (-0.5)
 
-NY, NZ, NX = 8, 8, 4
-DEVS = NZ * NX
+NY, NQ, NL, NX = 8, 4, 2, 4
+NZ = NQ * NL
+NEAR = NL * NX
+DEVS = NQ * NEAR
 PIECE = 192 // NY
 KEYS = 192 * NX
 MINE = 2 * ROWS
 SENT = MINE + 16
 SLOTS = EXPERTS * CAP
 OWN_SLOTS = SLOTS // DEVS
-BLOCK = 256
-BLOCKS = D // BLOCK
-TILES = -(-LAT // 128)
-PACKED = TILES * MINE + LAT_KV
+NEAR_SLOTS = NEAR * OWN_SLOTS
+SPAN = D // NEAR
+UP_AT = LAT_KV // 128 * MINE + ROWS
+PACKED = UP_AT + LAT_KV
 STEP = 4
 
 bf16 = jnp.bfloat16
@@ -37,8 +39,8 @@
 SMEM = pl.BlockSpec(memory_space=pltpu.SMEM)
 
 
-def params():
-    return pltpu.CompilerParams(vmem_limit_bytes=24 * 1024 * 1024)
+def params(mib=24):
+    return pltpu.CompilerParams(vmem_limit_bytes=mib * 1024 * 1024)
 
 
 def dot(a, b, dims=((1,), (0,))):
@@ -49,30 +51,29 @@
     return jnp.transpose(jnp.broadcast_to(column, (MINE, 128)))[:1]
 
 
-def pick_kernel(wanted, mine, other, out):
-    core = wanted[8]
+def pick_kernel(core, wanted, mine, other, out):
     for y in range(NY):
         prompt = wanted[y]
         row = lax.shift_right_logical(prompt, 1)
 
-        @pl.when((prompt & 1) == core)
+        @pl.when((prompt & 1) == core[0])
         def _():
             out[y] = mine[row]
 
-        @pl.when((prompt & 1) != core)
+        @pl.when((prompt & 1) != core[0])
         def _():
             out[y] = other[row]
 
 
-def pick(wanted, mine, other):
+def pick(core, wanted, mine, other):
     return pl.pallas_call(
         pick_kernel,
         out_shape=jax.ShapeDtypeStruct(mine.shape, mine.dtype),
-        in_specs=[SMEM, VMEM, VMEM],
+        in_specs=[SMEM, SMEM, VMEM, VMEM],
         out_specs=VMEM,
         compiler_params=params(),
         name="pick",
-    )(wanted, mine, other)
+    )(core, wanted, mine, other)
 
 
 def attend(query, keys, visible=None):
@@ -93,40 +94,43 @@
     return high, mid, rest - mid
 
 
-def pack_kernel(core, query, value_up, out):
-    for tile in range(TILES):
-        width = min(128, LAT - tile * 128)
-        part = query[:, tile * 128 : tile * 128 + width]
-        if width < 128:
-            part = jnp.concatenate([part, jnp.zeros((MINE, 128 - width), bf16)], axis=1)
-        out[tile * MINE : (tile + 1) * MINE, :] = part
-    out[TILES * MINE :, :] = value_up[core[0]]
+def pack_kernel(core, query, value_up, out, sem):
+    copy = pltpu.make_async_copy(value_up.at[core[0]], out.at[UP_AT:], sem)
+    copy.start()
+    heads = [query[:, head, :] for head in range(2)]
+    for tile in range(LAT_KV // 128):
+        for head in range(2):
+            first = tile * MINE + head * ROWS
+            out[first : first + ROWS, :] = heads[head][:, tile * 128 : (tile + 1) * 128]
+    out[UP_AT - ROWS : UP_AT, :] = jnp.concatenate([head[:, LAT_KV:] for head in heads], axis=1)
+    copy.wait()
 
 
 def pack(core, query, value_up):
     return pl.pallas_call(
         pack_kernel,
         out_shape=jax.ShapeDtypeStruct((PACKED, 128), bf16),
-        in_specs=[SMEM, VMEM, VMEM],
-        out_specs=VMEM,
-        compiler_params=params(),
+        in_specs=[SMEM, VMEM, pl.BlockSpec(memory_space=pl.ANY)],
+        out_specs=VMEM,
+        scratch_shapes=[pltpu.SemaphoreType.DMA],
+        compiler_params=params(60),
         name="pack",
     )(core, query, value_up)
+
+
+def unpacked(packed, z):
+    tiles = [packed[z, tile * MINE : (tile + 1) * MINE, :] for tile in range(LAT_KV // 128)]
+    rest = packed[z, UP_AT - ROWS : UP_AT, :]
+    width = LAT - LAT_KV
+    tiles.append(jnp.concatenate([rest[:, :width], rest[:, width:]], axis=0))
+    return jnp.concatenate(tiles, axis=1)
 
 
 def attention_kernel(packed, keys, latents, stats):
     index = lax.broadcasted_iota(jnp.int32, (16, 128), 0)
     for step in range(NZ // STEP):
         zs = range(step * STEP, (step + 1) * STEP)
-        query = jnp.concatenate(
-            [
-                jnp.concatenate(
-                    [packed[z, tile * MINE : (tile + 1) * MINE, :] for tile in range(TILES)], axis=1
-                )
-                for z in zs
-            ],
-            axis=0,
-        )[:, :LAT]
+        query = jnp.concatenate([unpacked(packed, z) for z in zs], axis=0)
         best, total, latent = attend(query, keys[...])
         for i, z in enumerate(zs):
             part = slice(i * MINE, (i + 1) * MINE)
@@ -163,11 +167,11 @@
 
     @pl.when(core[0] == 0)
     def _():
-        apply(lambda z: mine[z, TILES * MINE :, :], lambda z: other[z, TILES * MINE :, :])
+        apply(lambda z: mine[z, UP_AT:, :], lambda z: other[z, UP_AT:, :])
 
     @pl.when(core[0] != 0)
     def _():
-        apply(lambda z: other[z, TILES * MINE :, :], lambda z: mine[z, TILES * MINE :, :])
+        apply(lambda z: other[z, UP_AT:, :], lambda z: mine[z, UP_AT:, :])
 
 
 def up_project(core, latents, stats, mine, other):
@@ -249,22 +253,39 @@
 
 
 def project_kernel(head_values, weight, out):
-    for block in range(BLOCKS):
-        part = slice(block * BLOCK, (block + 1) * BLOCK)
-        out[block] = dot(head_values[...], weight[:, part]).astype(bf16)
-    for block in range(BLOCKS, DEVS):
-        out[block] = jnp.zeros((ROWS, BLOCK), bf16)
+    for i in range(NEAR):
+        out[i] = dot(head_values[...], weight[:, i * SPAN : (i + 1) * SPAN]).astype(bf16)
 
 
 def project(head_values, weight):
     return pl.pallas_call(
         project_kernel,
-        out_shape=jax.ShapeDtypeStruct((DEVS, ROWS, BLOCK), bf16),
+        out_shape=jax.ShapeDtypeStruct((NEAR, ROWS, SPAN), bf16),
         in_specs=[VMEM] * 2,
         out_specs=VMEM,
         compiler_params=params(),
         name="project",
     )(head_values, weight)
+
+
+def add_kernel(arrived, out):
+    total = arrived[0].astype(f32)
+    for i in range(1, NEAR):
+        total = total + arrived[i].astype(f32)
+    total = total.astype(bf16)
+    for q in range(NQ):
+        out[q] = total
+
+
+def add(arrived):
+    return pl.pallas_call(
+        add_kernel,
+        out_shape=jax.ShapeDtypeStruct((NQ, ROWS, SPAN), bf16),
+        in_specs=[VMEM],
+        out_specs=VMEM,
+        compiler_params=params(),
+        name="add",
+    )(arrived)
 
 
 def slots_kernel(routes, gates, picks, slot_gates):
@@ -300,33 +321,36 @@
     )(routes, gates)
 
 
-def dispatch_kernel(arrived, picks, out):
+def dispatch_kernel(zq, arrived, picks, out):
     total = arrived[0].astype(f32)
-    for dev in range(1, DEVS):
-        total = total + arrived[dev].astype(f32)
-    out[...] = dot(picks[...], total.astype(bf16)).astype(bf16)
-
-
-def dispatch(arrived, picks):
+    for q in range(1, NQ):
+        total = total + arrived[q].astype(f32)
+    first = pl.multiple_of(zq[0] * NEAR_SLOTS, NEAR_SLOTS)
+    out[...] = dot(picks[pl.ds(first, NEAR_SLOTS), :], total.astype(bf16)).astype(bf16)
+
+
+def dispatch(zq, arrived, picks):
     return pl.pallas_call(
         dispatch_kernel,
-        out_shape=jax.ShapeDtypeStruct((SLOTS, BLOCK), bf16),
-        in_specs=[VMEM] * 2,
+        out_shape=jax.ShapeDtypeStruct((NEAR_SLOTS, SPAN), bf16),
+        in_specs=[SMEM, VMEM, VMEM],
         out_specs=VMEM,
         compiler_params=params(),
         name="dispatch",
-    )(arrived, picks)
+    )(zq, arrived, picks)
 
 
 def norm_kernel(arrived, gain, out):
-    blocks = [arrived[block].astype(f32) for block in range(BLOCKS)]
-    square = blocks[0] * blocks[0]
-    for block in blocks[1:]:
-        square = square + block * block
+    square = jnp.zeros((OWN_SLOTS, 128), f32)
+    for i in range(NEAR):
+        block = arrived[i].astype(f32)
+        for lane in range(0, SPAN, 128):
+            part = block[:, lane : lane + 128]
+            square = square + part * part
     scale = lax.rsqrt(jnp.sum(square, axis=1, keepdims=True) * (1.0 / D) + EPSILON)
-    for i, block in enumerate(blocks):
-        part = slice(i * BLOCK, (i + 1) * BLOCK)
-        normed = block * scale * gain[:, part].astype(f32)
+    for i in range(NEAR):
+        part = slice(i * SPAN, (i + 1) * SPAN)
+        normed = arrived[i].astype(f32) * scale * gain[:, part].astype(f32)
         for expert in range(OWN_SLOTS // CAP):
             out[expert, :, part] = normed[expert * CAP : (expert + 1) * CAP]
 
@@ -357,38 +381,40 @@
     routes,
     gates,
 ):
-    core = lax.axis_index("core")
-    dev = lax.axis_index("z") * NX + lax.axis_index("x")
+    core = lax.axis_index("core")[None].astype(jnp.int32)
+    zq = lax.axis_index("zq")[None].astype(jnp.int32)
+    dev = (lax.axis_index("zq") * NL + lax.axis_index("zl")) * NX + lax.axis_index("x")
+    swap = [(0, 1), (1, 0)]
 
     pieces = exchange(prompt_cache.reshape(NY, PIECE, LAT), "y")
-    other = lax.ppermute(pieces, "core", [(0, 1), (1, 0)])
-    own_prompts = jnp.where(core == 0, prompt_of_group[0::2], prompt_of_group[1::2])
-    wanted = jnp.concatenate([own_prompts, core[None].astype(jnp.int32)])
-    served = exchange(pick(wanted, pieces, other), "y").reshape(NY * PIECE, LAT)
+    other = lax.ppermute(pieces, "core", swap)
+    wanted = jnp.where(core[0] == 0, prompt_of_group[0::2], prompt_of_group[1::2])
+    served = exchange(pick(core, wanted, pieces, other), "y").reshape(NY * PIECE, LAT)
     keys = lax.all_gather(served, "x", axis=0, tiled=True)
 
     query = queries.reshape(ROWS, 2, LAT).transpose(1, 0, 2).reshape(MINE, LAT)
-    core = core[None].astype(jnp.int32)
-    packed = lax.all_gather(pack(core, query, value_up), "z", axis=0, tiled=True)
+    packed = lax.all_gather(pack(core, queries.reshape(ROWS, 2, LAT), value_up), ("zq", "zl"), axis=0, tiled=True)
     packed = packed.reshape(NZ, PACKED, 128)
     packed, keys = lax.optimization_barrier((packed, keys))
-    other_packed = lax.ppermute(packed, "core", [(0, 1), (1, 0)])
-    own_values, own_stats = own_attention(query, new_latents.reshape(ROWS, LAT), value_up)
+    other_packed = lax.ppermute(packed, "core", swap)
     picks, all_gates = slots(routes.T, gates.T)
     slot_gates = lax.dynamic_slice_in_dim(all_gates, dev * OWN_SLOTS, OWN_SLOTS, 0)
 
     latents, stats = prompt_attention(packed, keys)
-    partial = exchange(up_project(core, latents, stats, packed, other_packed), "z")
+    values = up_project(core, latents, stats, packed, other_packed)
+    own_values, own_stats = own_attention(query, new_latents.reshape(ROWS, LAT), value_up)
+    partial = exchange(values, ("zq", "zl"))
     head_values = combine(partial, own_values, own_stats)
-    sums = exchange(project(head_values, out_weight), ("z", "x"))
-    rows = dispatch(sums, picks).reshape(DEVS, OWN_SLOTS, BLOCK)
-    slot_rows = norm(exchange(rows, ("z", "x")), norm_gain.reshape(1, D))
+    sums = exchange(add(exchange(project(head_values, out_weight), ("zl", "x"))), "zq")
+    rows = dispatch(zq, sums, picks).reshape(NEAR, OWN_SLOTS, SPAN)
+    slot_rows = norm(exchange(rows, ("zl", "x")), norm_gain.reshape(1, D))
     return (slot_rows[None], slot_gates.reshape(1, OWN_SLOTS // CAP, CAP))
 
 
 def solution(mesh):
-    fine = Mesh(mesh.devices.reshape(NY, 2, NZ, NX), ("y", "core", "z", "x"))
-    group, dev = ("y", "core"), ("z", "x")
+    axes = ("y", "core", "zq", "zl", "x")
+    fine = Mesh(mesh.devices.reshape(NY, 2, NQ, NL, NX), axes)
+    group, dev = axes[:2], axes[2:]
     return jax.shard_map(
         local,
         mesh=fine,

time: 160 us -> 153 us (0.956)
  the two profiles are of different devices: /device:TPU:8 before, /device:TPU:2 now
where the time goes in v6:
time: 153 us; the launch traced here: 152 us
  blocking collectives  46.6 us (30%)
  waiting for transfers between devices  41.8 us (27%)
  starting transfers between devices  30.5 us (20%)
  between operations  14.2 us (9%)
  Pallas kernels  12.9 us (8%)
  local copies, waits for them, and re-layouts  6.12 us (4%)
    all_to_all x4, waiting for transfers between devices, exchange(): return lax.all_to_all(value, axes, split_axis=0, concat_axis=0, tiled=True)  40.4 us
    all_to_all x2, blocking collectives, exchange(): return lax.all_to_all(value, axes, split_axis=0, concat_axis=0, tiled=True)  31.9 us
    all_to_all x4, starting transfers between devices, exchange(): return lax.all_to_all(value, axes, split_axis=0, concat_axis=0, tiled=True)  26.7 us
    all_gather x1, blocking collectives, local(): keys = lax.all_gather(served, 'x', axis=0, tiled=True)  14.7 us
    unnamed x19, local copies, waits for them, and re-layouts  4.36 us
    pallas_call x1, Pallas kernels, prompt_attention(): pl.pallas_call(attention_kernel, out_shape=(jax.ShapeDtypeStruct((NZ, MIN...  3.24 us
  transfers between devices with their start and end apart: 7, of which 5 were waited for; matrix products, arithmetic and copies ran while one was open for 2% of the time, Pallas kernels for 3%

profile of v6, /device:TPU:2, one launch (start us, length us, event | category | flops | bytes accessed | tf_op | source)
XLA Modules:
  0.0 152.3 jit_solution(12858518570655554733)
XLA Ops:
  7.2 0.0 all-gather.2.cloned.1.call-start
  7.2 2.5 %pack.1 = bf16[1088,128]{1,0:T(8,128)(2,1)} custom-call(s32[1]{0:T(128)} %bitcast.1.core, bf16[64,2,576]{2,1,0:T(2,128)(2,1)} %bitcast.21, bf16[2,512,128]{2,1,0:T(8,128)(2,1)} %value_up.3), custom_call_target="tpu_custom_call" | custom-call | tf_op jit(solution)/shard_map/pack/pallas_call | solution.py:110
  9.8 0.0 all-gather.2.cloned.1.call-update
  9.8 7.1 %all-to-all-start = ((bf16[8,24,576]{2,1,0:T(8,128)(2,1)}), bf16[8,24,576]{2,1,0:T(8,128)(2,1)S(1)}, u32[]{:S(2)}, u32[]{:S(2)}) async-start(bf16[8,24,576]{2,1,0:T(8,128)(2,1)} %bitcast.23), calls=%async_computation | async-start | bytes 491520 | tf_op jit(solution)/shard_map/all_to_all | solution.py:370
  16.9 0.7 slice.6
  17.6 0.7 slice.7
  18.4 10.0 %all-to-all-done.mine = bf16[8,24,576]{2,1,0:T(8,128)(2,1)S(1)} async-done(((bf16[8,24,576]{2,1,0:T(8,128)(2,1)}), bf16[8,24,576]{2,1,0:T(8,128)(2,1)S(1)}, u32[]{:S(2)}, u32[]{:S(2)}) %all-to-all-start) | async-done | bytes 221216 | tf_op jit(solution)/shard_map/all_to_all | solution.py:370
  28.4 1.9 %collective-permute-start = (bf16[8,24,576]{2,1,0:T(8,128)(2,1)S(1)}, bf16[8,24,576]{2,1,0:T(8,128)(2,1)S(1)}, u32[]{:S(2)}, u32[]{:S(2)}) collective-permute-start(bf16[8,24,576]{2,1,0:T(8,128)(2,1)S(1)} %all-to-all-done.mine), channel_id=1, source_target_pairs={{0,32},{32,0},{1,33},{33,1},{2,34},{34,2},{3,35},{35,3},{4,36},{36... | collective-permute-start | bytes 663560 | tf_op jit(solution)/shard_map/ppermute | solution.py:390
  30.4 1.5 collective-permute-done.other
  31.8 0.7 pick.1
  32.5 14.5 %all_to_all.30 = bf16[8,24,576]{2,1,0:T(8,128)(2,1)S(1)} all-to-all(bf16[8,24,576]{2,1,0:T(8,128)(2,1)S(1)} %pick.1), channel_id=1, replica_groups=mesh['y'=8,'core'=2,'zq'=4,'zl'=2,'x'=4] {'y'}, dimensions={0} | all-to-all | bytes 442368 | tf_op jit(solution)/shard_map/all_to_all | solution.py:370
  47.0 14.7 %all_gather.7.keys = bf16[768,576]{1,0:T(8,128)(2,1)S(1)} all-gather(bf16[192,576]{1,0:T(8,128)(2,1)S(1)} %bitcast.19), channel_id=1, replica_groups=mesh['y'=8,'core'=2,'zq'=4,'zl'=2,'x'=4] {'x'}, dimensions={0}, use_global_device_ids=true | all-gather | bytes 1105920 | tf_op jit(solution)/shard_map/all_gather | solution.py:393
  61.8 1.9 %collective-permute-start.1 = (bf16[8,1088,128]{2,1,0:T(8,128)(2,1)}, bf16[8,1088,128]{2,1,0:T(8,128)(2,1)S(1)}, u32[]{:S(2)}, u32[]{:S(2)}) collective-permute-start(bf16[8,1088,128]{2,1,0:T(8,128)(2,1)} %bitcast.13), channel_id=1, source_target_pairs={{0,32},{32,0},{1,33},{33,1},{2,34},{34,2},{3,35},{35,3},{4,36},{36... | collective-permute-start | bytes 6684680 | tf_op jit(solution)/shard_map/ppermute | solution.py:399
  63.7 0.0 copy-start
  63.7 1.6 %copy-done = bf16[8704,128]{1,0:T(8,128)(2,1)S(1)} copy-done((bf16[8704,128]{1,0:T(8,128)(2,1)S(1)}, bf16[8704,128]{1,0:T(8,128)(2,1)}, u32[]{:S(2)}) %copy-start) | copy-done | bytes 2228248
  65.3 3.2 %prompt_attention.1 = (bf16[8,128,512]{2,1,0:T(8,128)(2,1)S(1)}, bf16[8,16,128]{2,1,0:T(8,128)(2,1)S(1)}) custom-call(bf16[8,1088,128]{2,1,0:T(8,128)(2,1)S(1)} %bitcast.14, bf16[768,576]{1,0:T(8,128)(2,1)S(1)} %all_gather.7.keys), custom_call_target="tpu_custom_call" | custom-call | tf_op jit(solution)/shard_map/prompt_attention/pallas_call | solution.py:146
  68.6 0.0 collective-permute-done.1.other
  68.6 0.0 copy-done.1
  68.6 0.0 copy-start.6
  68.6 0.0 copy-start.7
  68.6 0.0 copy-start.3
  68.6 1.2 up_project.1
  69.8 10.8 %all-to-all-start.2 = ((bf16[8,144,128]{2,1,0:T(8,128)(2,1)}), bf16[8,144,128]{2,1,0:T(8,128)(2,1)S(1)}, u32[]{:S(2)}, u32[]{:S(2)}) async-start(bf16[8,144,128]{2,1,0:T(8,128)(2,1)} %up_project.1), calls=%async_computation.2 | async-start | bytes 589824 | tf_op jit(solution)/shard_map/all_to_all | solution.py:370
  80.6 0.0 copy-done.6
  80.6 0.0 copy-done.7
  80.7 0.0 copy-done.3
  80.7 0.6 own_attention.1
  81.3 12.6 %all-to-all-done.2.arrived = bf16[8,144,128]{2,1,0:T(8,128)(2,1)S(1)} async-done(((bf16[8,144,128]{2,1,0:T(8,128)(2,1)}), bf16[8,144,128]{2,1,0:T(8,128)(2,1)S(1)}, u32[]{:S(2)}, u32[]{:S(2)}) %all-to-all-start.2) | async-done | bytes 294944 | tf_op jit(solution)/shard_map/all_to_all | solution.py:370
  93.8 0.4 combine.1.head_values
  94.2 0.0 copy-start.2
  94.3 2.0 %copy-done.2 = bf16[256,7168]{1,0:T(8,128)(2,1)S(1)} copy-done((bf16[256,7168]{1,0:T(8,128)(2,1)S(1)}, bf16[256,7168]{1,0:T(8,128)(2,1)}, u32[]{:S(2)}) %copy-start.2) | copy-done | bytes 3670040
  96.3 0.7 project.1
  96.9 0.0 copy-start.4
  97.0 0.0 copy-start.5
  97.0 17.3 %all_to_all.31.arrived = bf16[8,64,896]{2,1,0:T(8,128)(2,1)S(1)} all-to-all(bf16[8,64,896]{2,1,0:T(8,128)(2,1)S(1)} %project.1), channel_id=1, replica_groups=mesh['y'=8,'core'=2,'zq'=4,'zl'=2,'x'=4] {'zl','x'}, dimensions={0} | all-to-all | bytes 1835008 | tf_op jit(solution)/shard_map/all_to_all | solution.py:370
  114.3 0.9 add.14
  115.2 3.5 %all-to-all-start.4 = ((bf16[4,64,896]{2,1,0:T(8,128)(2,1)}), bf16[4,64,896]{2,1,0:T(8,128)(2,1)S(1)}, u32[]{:S(2)}, u32[]{:S(2)}) async-start(bf16[4,64,896]{2,1,0:T(8,128)(2,1)} %add.14), calls=%async_computation.4 | async-start | bytes 917504 | tf_op jit(solution)/shard_map/all_to_all | solution.py:370
  118.7 0.0 copy-done.4
  118.7 0.0 copy-done.5
  118.7 0.6 slots.1
  119.3 13.0 %all-to-all-done.4.arrived = bf16[4,64,896]{2,1,0:T(8,128)(2,1)S(1)} async-done(((bf16[4,64,896]{2,1,0:T(8,128)(2,1)}), bf16[4,64,896]{2,1,0:T(8,128)(2,1)S(1)}, u32[]{:S(2)}, u32[]{:S(2)}) %all-to-all-start.4) | async-done | bytes 458784 | tf_op jit(solution)/shard_map/all_to_all | solution.py:370
  132.3 1.0 dispatch.1
  133.3 5.3 %all-to-all-start.5 = ((bf16[8,24,896]{2,1,0:T(8,128)(2,1)}), bf16[8,24,896]{2,1,0:T(8,128)(2,1)S(1)}, u32[]{:S(2)}, u32[]{:S(2)}) async-start(bf16[8,24,896]{2,1,0:T(8,128)(2,1)} %bitcast.10), calls=%async_computation.5 | async-start | bytes 688128 | tf_op jit(solution)/shard_map/all_to_all | solution.py:370
  138.6 0.1 dynamic-slice_reduce_fusion
  138.8 0.1 reshape.40
  138.8 0.7 copy.14
  139.5 4.8 %all-to-all-done.5.arrived = bf16[8,24,896]{2,1,0:T(8,128)(2,1)S(1)} async-done(((bf16[8,24,896]{2,1,0:T(8,128)(2,1)}), bf16[8,24,896]{2,1,0:T(8,128)(2,1)S(1)}, u32[]{:S(2)}, u32[]{:S(2)}) %all-to-all-start.5) | async-done | bytes 344096 | tf_op jit(solution)/shard_map/all_to_all | solution.py:370
  144.3 1.1 norm.1
  (8 shorter events, 0.1 us)
Async XLA Ops:
  7.2 54.6 %all-gather.2.cloned.1.call-start = ((), (), s32[]{:S(2)}) async-start(), calls=%async_computation.6 | async-start | bytes 2506752 | tf_op jit(solution)/shard_map/all_gather | solution.py:396
  9.8 18.6 %all-to-all-start = ((bf16[8,24,576]{2,1,0:T(8,128)(2,1)}), bf16[8,24,576]{2,1,0:T(8,128)(2,1)S(1)}, u32[]{:S(2)}, u32[]{:S(2)}) async-start(bf16[8,24,576]{2,1,0:T(8,128)(2,1)} %bitcast.23), calls=%async_computation | async-start | bytes 491520 | tf_op jit(solution)/shard_map/all_to_all | solution.py:370
  28.4 3.4 %collective-permute-start = (bf16[8,24,576]{2,1,0:T(8,128)(2,1)S(1)}, bf16[8,24,576]{2,1,0:T(8,128)(2,1)S(1)}, u32[]{:S(2)}, u32[]{:S(2)}) collective-permute-start(bf16[8,24,576]{2,1,0:T(8,128)(2,1)S(1)} %all-to-all-done.mine), channel_id=1, source_target_pairs={{0,32},{32,0},{1,33},{33,1},{2,34},{34,2},{3,35},{35,3},{4,36},{36... | collective-permute-start | bytes 663560 | tf_op jit(solution)/shard_map/ppermute | solution.py:390
  61.8 6.8 %collective-permute-start.1 = (bf16[8,1088,128]{2,1,0:T(8,128)(2,1)}, bf16[8,1088,128]{2,1,0:T(8,128)(2,1)S(1)}, u32[]{:S(2)}, u32[]{:S(2)}) collective-permute-start(bf16[8,1088,128]{2,1,0:T(8,128)(2,1)} %bitcast.13), channel_id=1, source_target_pairs={{0,32},{32,0},{1,33},{33,1},{2,34},{34,2},{3,35},{35,3},{4,36},{36... | collective-permute-start | bytes 6684680 | tf_op jit(solution)/shard_map/ppermute | solution.py:399
  63.7 1.6 %copy-start = (bf16[8704,128]{1,0:T(8,128)(2,1)S(1)}, bf16[8704,128]{1,0:T(8,128)(2,1)}, u32[]{:S(2)}) copy-start(bf16[8704,128]{1,0:T(8,128)(2,1)} %all-gather.2.cloned.1.call-done) | copy-start | bytes 6684676
  65.3 3.2 %copy-start.1 = (bf16[8704,128]{1,0:T(8,128)(2,1)S(1)}, bf16[8704,128]{1,0:T(8,128)(2,1)}, u32[]{:S(2)}) copy-start(bf16[8704,128]{1,0:T(8,128)(2,1)} %all-gather.2.cloned.1.call-done) | copy-start | bytes 6684676
  68.6 12.0 %copy-start.6 = (bf16[1,16,4,2,576]{4,3,2,1,0:T(2,128)(2,1)S(1)}, bf16[1,16,4,2,576]{4,3,2,1,0:T(2,128)(2,1)}, u32[]{:S(2)}) copy-start(bf16[1,16,4,2,576]{4,3,2,1,0:T(2,128)(2,1)} %param.11) | copy-start | bytes 442372
  68.6 12.0 %copy-start.7 = (bf16[1,16,4,576]{3,2,1,0:T(4,128)(2,1)S(1)}, bf16[1,16,4,576]{3,2,1,0:T(4,128)(2,1)}, u32[]{:S(2)}) copy-start(bf16[1,16,4,576]{3,2,1,0:T(4,128)(2,1)} %param.12) | copy-start | bytes 221188
  68.6 12.1 %copy-start.3 = (bf16[2,512,128]{2,1,0:T(8,128)(2,1)S(1)}, bf16[2,512,128]{2,1,0:T(8,128)(2,1)}, u32[]{:S(2)}) copy-start(bf16[2,512,128]{2,1,0:T(8,128)(2,1)} %value_up.3) | copy-start | bytes 786436
  69.8 24.0 %all-to-all-start.2 = ((bf16[8,144,128]{2,1,0:T(8,128)(2,1)}), bf16[8,144,128]{2,1,0:T(8,128)(2,1)S(1)}, u32[]{:S(2)}, u32[]{:S(2)}) async-start(bf16[8,144,128]{2,1,0:T(8,128)(2,1)} %up_project.1), calls=%async_computation.2 | async-start | bytes 589824 | tf_op jit(solution)/shard_map/all_to_all | solution.py:370
  94.2 2.0 %copy-start.2 = (bf16[256,7168]{1,0:T(8,128)(2,1)S(1)}, bf16[256,7168]{1,0:T(8,128)(2,1)}, u32[]{:S(2)}) copy-start(bf16[256,7168]{1,0:T(8,128)(2,1)} %weight.1) | copy-start | bytes 11010052
  96.9 21.7 %copy-start.4 = (s32[64,8]{0,1:T(8,128)S(1)}, s32[64,8]{0,1:T(8,128)}, u32[]{:S(2)}) copy-start(s32[64,8]{0,1:T(8,128)} %param.16) | copy-start | bytes 6148
  97.0 21.7 %copy-start.5 = (f32[64,8]{0,1:T(8,128)S(1)}, f32[64,8]{0,1:T(8,128)}, u32[]{:S(2)}) copy-start(f32[64,8]{0,1:T(8,128)} %param.17) | copy-start | bytes 6148
  114.3 24.3 %copy-start.8 = (bf16[7168]{0:T(1024)(128)(2,1)S(1)}, bf16[7168]{0:T(1024)(128)(2,1)}, u32[]{:S(2)}) copy-start(bf16[7168]{0:T(1024)(128)(2,1)} %param.15) | copy-start | bytes 43012
  115.2 17.1 %all-to-all-start.4 = ((bf16[4,64,896]{2,1,0:T(8,128)(2,1)}), bf16[4,64,896]{2,1,0:T(8,128)(2,1)S(1)}, u32[]{:S(2)}, u32[]{:S(2)}) async-start(bf16[4,64,896]{2,1,0:T(8,128)(2,1)} %add.14), calls=%async_computation.4 | async-start | bytes 917504 | tf_op jit(solution)/shard_map/all_to_all | solution.py:370
  133.3 11.0 %all-to-all-start.5 = ((bf16[8,24,896]{2,1,0:T(8,128)(2,1)}), bf16[8,24,896]{2,1,0:T(8,128)(2,1)S(1)}, u32[]{:S(2)}, u32[]{:S(2)}) async-start(bf16[8,24,896]{2,1,0:T(8,128)(2,1)} %bitcast.10), calls=%async_computation.5 | async-start | bytes 688128 | tf_op jit(solution)/shard_map/all_to_all | solution.py:370
Sparse Core Ops, SparseCore 0:
  10.7 49.4 all-gather.1

commit v7 on v5

--- a/solution.py
+++ b/solution.py
@@ -18,18 +18,16 @@
 SCALE = QK_DIM ** (-0.5)
 
 NY, NQ, NL, NX = 8, 4, 2, 4
-NEAR = NX * NL
+NEAR = NL * NX
 DEVS = NQ * NEAR
 PIECE = 192 // NY
-KEYS = 192 * NEAR
+KEYS = 192 * NQ
 MINE = 2 * ROWS
 SENT = MINE + 16
 SLOTS = EXPERTS * CAP
 OWN_SLOTS = SLOTS // DEVS
+NEAR_SLOTS = NEAR * OWN_SLOTS
 SPAN = D // NEAR
-BLOCK = 256
-WIDTHS = [min(BLOCK, SPAN - q * BLOCK) for q in range(NQ)]
-STEP = 2
 
 bf16 = jnp.bfloat16
 f32 = jnp.float32
@@ -37,8 +35,8 @@
 SMEM = pl.BlockSpec(memory_space=pltpu.SMEM)
 
 
-def params():
-    return pltpu.CompilerParams(vmem_limit_bytes=24 * 1024 * 1024)
+def params(mib=24):
+    return pltpu.CompilerParams(vmem_limit_bytes=mib * 1024 * 1024)
 
 
 def dot(a, b, dims=((1,), (0,))):
@@ -49,9 +47,9 @@
     return jnp.transpose(jnp.broadcast_to(column, (MINE, 128)))[:1]
 
 
-def pick_kernel(core, prompt_of_group, mine, other, out):
+def pick_kernel(core, wanted, mine, other, out):
     for y in range(NY):
-        prompt = prompt_of_group[2 * y + core[0]]
+        prompt = wanted[y]
         row = lax.shift_right_logical(prompt, 1)
 
         @pl.when((prompt & 1) == core[0])
@@ -63,7 +61,7 @@
             out[y] = other[row]
 
 
-def pick(core, prompt_of_group, mine, other):
+def pick(core, wanted, mine, other):
     return pl.pallas_call(
         pick_kernel,
         out_shape=jax.ShapeDtypeStruct(mine.shape, mine.dtype),
@@ -71,7 +69,7 @@
         out_specs=VMEM,
         compiler_params=params(),
         name="pick",
-    )(core, prompt_of_group, mine, other)
+    )(core, wanted, mine, other)
 
 
 def attend(query, keys, visible=None):
@@ -92,16 +90,16 @@
     return high, mid, rest - mid
 
 
-def attention_kernel(zq, keys, *refs):
-    queries, out = refs[:NQ], refs[NQ]
+def attention_kernel(zl, mine, other, keys, out):
     index = lax.broadcasted_iota(jnp.int32, (16, 128), 0)
-    for step in range(NQ // STEP):
-        shifts = range(step * STEP, (step + 1) * STEP)
-        query = jnp.concatenate([queries[k][...] for k in shifts], axis=0)
+    for step in range(NL):
+        queries = (mine, other)[step]
+        first = (zl[0] ^ step) * NX
+        query = jnp.concatenate([queries[x] for x in range(NX)], axis=0)
         best, total, latent = attend(query, keys[...])
-        for i, k in enumerate(shifts):
+        for i in range(NX):
             part = slice(i * MINE, (i + 1) * MINE)
-            owner = (zq[0] + NQ - k) & (NQ - 1)
+            owner = first + i
             out[owner, :MINE, :] = latent[part]
             rows = three(columns_to_lanes(best[part])) + three(columns_to_lanes(total[part]))
             table = jnp.zeros((16, 128), f32)
@@ -111,15 +109,15 @@
             out[owner, MINE:, 128:] = jnp.zeros((16, LAT_KV - 128), bf16)
 
 
-def prompt_attention(zq, keys, queries):
+def prompt_attention(zl, mine, other, keys):
     return pl.pallas_call(
         attention_kernel,
-        out_shape=jax.ShapeDtypeStruct((NQ, SENT, LAT_KV), bf16),
-        in_specs=[SMEM] + [VMEM] * (1 + NQ),
+        out_shape=jax.ShapeDtypeStruct((NEAR, SENT, LAT_KV), bf16),
+        in_specs=[SMEM] + [VMEM] * 3,
         out_specs=VMEM,
         compiler_params=params(),
         name="prompt_attention",
-    )(zq, keys, *queries)
+    )(zl, mine, other, keys)
 
 
 def own_kernel(query, keys, latents, stats):
@@ -152,7 +150,7 @@
 
 def combine_kernel(arrived, own_latents, own_stats, value_up, out):
     bests, totals = [own_stats[0:1, :]], [own_stats[1:2, :]]
-    for z in range(NQ):
+    for z in range(NEAR):
         stats = arrived[z, MINE:, :128].astype(f32)
         bests.append(stats[0:1] + stats[1:2] + stats[2:3])
         totals.append(stats[3:4] + stats[4:5] + stats[5:6])
@@ -169,7 +167,7 @@
         table = jnp.where(index == i, jnp.broadcast_to(share / whole, (128, 128)), table)
     table = jnp.transpose(table)
     latent = table[:, 0:1] * own_latents[...].astype(f32)
-    for z in range(NQ):
+    for z in range(NEAR):
         latent = latent + table[:, z + 1 : z + 2] * arrived[z, :MINE, :].astype(f32)
     latent = latent.astype(bf16)
     for head in range(2):
@@ -188,28 +186,17 @@
     )(arrived, own_latents, own_stats, value_up)
 
 
-def project_kernel(head_values, weight, out, held, sems):
-    copies = [
-        pltpu.make_async_copy(weight.at[:, i * SPAN : (i + 1) * SPAN], held.at[i], sems.at[i])
-        for i in range(NEAR)
-    ]
-    for copy in copies:
-        copy.start()
-    for i, copy in enumerate(copies):
-        copy.wait()
-        out[i] = dot(head_values[...], held[i]).astype(bf16)
+def project_kernel(head_values, weight, out):
+    for i in range(NEAR):
+        out[i] = dot(head_values[...], weight[:, i * SPAN : (i + 1) * SPAN]).astype(bf16)
 
 
 def project(head_values, weight):
     return pl.pallas_call(
         project_kernel,
         out_shape=jax.ShapeDtypeStruct((NEAR, ROWS, SPAN), bf16),
-        in_specs=[VMEM, pl.BlockSpec(memory_space=pltpu.HBM)],
-        out_specs=VMEM,
-        scratch_shapes=[
-            pltpu.VMEM((NEAR, 2 * HEAD_V, SPAN), bf16),
-            pltpu.SemaphoreType.DMA((NEAR,)),
-        ],
+        in_specs=[VMEM] * 2,
+        out_specs=VMEM,
         compiler_params=params(),
         name="project",
     )(head_values, weight)
@@ -220,16 +207,14 @@
     for i in range(1, NEAR):
         total = total + arrived[i].astype(f32)
     total = total.astype(bf16)
-    for q, width in enumerate(WIDTHS):
-        out[q, :, :width] = total[:, q * BLOCK : q * BLOCK + width]
-        if width < BLOCK:
-            out[q, :, width:] = jnp.zeros((ROWS, BLOCK - width), bf16)
+    for q in range(NQ):
+        out[q] = total
 
 
 def add(arrived):
     return pl.pallas_call(
         add_kernel,
-        out_shape=jax.ShapeDtypeStruct((NQ, ROWS, BLOCK), bf16),
+        out_shape=jax.ShapeDtypeStruct((NQ, ROWS, SPAN), bf16),
         in_specs=[VMEM],
         out_specs=VMEM,
         compiler_params=params(),
@@ -270,42 +255,36 @@
     )(routes, gates)
 
 
-def dispatch_kernel(arrived, picks, out):
+def dispatch_kernel(zq, arrived, picks, out):
     total = arrived[0].astype(f32)
     for q in range(1, NQ):
         total = total + arrived[q].astype(f32)
-    out[...] = dot(picks[...], total.astype(bf16)).astype(bf16)
-
-
-def dispatch(arrived, picks):
+    first = pl.multiple_of(zq[0] * NEAR_SLOTS, NEAR_SLOTS)
+    out[...] = dot(picks[pl.ds(first, NEAR_SLOTS), :], total.astype(bf16)).astype(bf16)
+
+
+def dispatch(zq, arrived, picks):
     return pl.pallas_call(
         dispatch_kernel,
-        out_shape=jax.ShapeDtypeStruct((SLOTS, BLOCK), bf16),
-        in_specs=[VMEM] * 2,
+        out_shape=jax.ShapeDtypeStruct((NEAR_SLOTS, SPAN), bf16),
+        in_specs=[SMEM, VMEM, VMEM],
         out_specs=VMEM,
         compiler_params=params(),
         name="dispatch",
-    )(arrived, picks)
+    )(zq, arrived, picks)
 
 
 def norm_kernel(arrived, gain, out):
-    blocks = []
-    for x in range(NX):
-        for zl in range(NL):
-            for q, width in enumerate(WIDTHS):
-                block = arrived[(q * NL + zl) * NX + x]
-                blocks.append(block[:, :width].astype(f32))
     square = jnp.zeros((OWN_SLOTS, 128), f32)
-    for block in blocks:
-        for lane in range(0, block.shape[1], 128):
+    for i in range(NEAR):
+        block = arrived[i].astype(f32)
+        for lane in range(0, SPAN, 128):
             part = block[:, lane : lane + 128]
             square = square + part * part
     scale = lax.rsqrt(jnp.sum(square, axis=1, keepdims=True) * (1.0 / D) + EPSILON)
-    start = 0
-    for block in blocks:
-        part = slice(start, start + block.shape[1])
-        start = start + block.shape[1]
-        normed = block * scale * gain[:, part].astype(f32)
+    for i in range(NEAR):
+        part = slice(i * SPAN, (i + 1) * SPAN)
+        normed = arrived[i].astype(f32) * scale * gain[:, part].astype(f32)
         for expert in range(OWN_SLOTS // CAP):
             out[expert, :, part] = normed[expert * CAP : (expert + 1) * CAP]
 
@@ -338,30 +317,30 @@
 ):
     core = lax.axis_index("core")[None].astype(jnp.int32)
     zq = lax.axis_index("zq")[None].astype(jnp.int32)
+    zl = lax.axis_index("zl")[None].astype(jnp.int32)
     dev = (lax.axis_index("zq") * NL + lax.axis_index("zl")) * NX + lax.axis_index("x")
+    swap = [(0, 1), (1, 0)]
 
     query = queries.reshape(ROWS, 2, LAT).transpose(1, 0, 2).reshape(MINE, LAT)
-
-    def shifted(k):
-        return lax.ppermute(query, "zq", [(i, (i + k) % NQ) for i in range(NQ)])
-
     pieces = exchange(prompt_cache.reshape(NY, PIECE, LAT), "y")
-    pieces, one, three_ = lax.optimization_barrier((pieces, shifted(1), shifted(3)))
-    other = lax.ppermute(pieces, "core", [(0, 1), (1, 0)])
-    served = exchange(pick(core, prompt_of_group, pieces, other), "y").reshape(NY * PIECE, LAT)
-    served, two = lax.optimization_barrier((served, shifted(2)))
-    keys = exchange(jnp.broadcast_to(served, (NEAR, NY * PIECE, LAT)), ("x", "zl"))
-    keys = keys.reshape(KEYS, LAT)
-    all_queries = [query, one, two, three_]
+    pieces, query = lax.optimization_barrier((pieces, query))
+    all_queries = exchange(jnp.broadcast_to(query, (NX, MINE, LAT)), "x")
+    other = lax.ppermute(pieces, "core", swap)
+    wanted = jnp.where(core[0] == 0, prompt_of_group[0::2], prompt_of_group[1::2])
+    picked = pick(core, wanted, pieces, other)
+    picked, all_queries = lax.optimization_barrier((picked, all_queries))
+    other_queries = lax.ppermute(all_queries, "zl", swap)
+    served = exchange(picked, "y").reshape(NY * PIECE, LAT)
+    keys = lax.all_gather(served, "zq", axis=0, tiled=True)
     own_latents, own_stats = own_attention(query, new_latents.reshape(ROWS, LAT))
     picks, all_gates = slots(routes.T, gates.T)
     slot_gates = lax.dynamic_slice_in_dim(all_gates, dev * OWN_SLOTS, OWN_SLOTS, 0)
 
-    partial = exchange(prompt_attention(zq, keys, all_queries), "zq")
+    partial = exchange(prompt_attention(zl, all_queries, other_queries, keys), ("zl", "x"))
     head_values = combine(partial, own_latents, own_stats, value_up)
-    sums = exchange(add(exchange(project(head_values, out_weight), ("x", "zl"))), "zq")
-    rows = dispatch(sums, picks).reshape(DEVS, OWN_SLOTS, BLOCK)
-    slot_rows = norm(exchange(rows, ("zq", "zl", "x")), norm_gain.reshape(1, D))
+    sums = exchange(add(exchange(project(head_values, out_weight), ("zl", "x"))), "zq")
+    rows = dispatch(zq, sums, picks).reshape(NEAR, OWN_SLOTS, SPAN)
+    slot_rows = norm(exchange(rows, ("zl", "x")), norm_gain.reshape(1, D))
     return (slot_rows[None], slot_gates.reshape(1, OWN_SLOTS // CAP, CAP))
 
 

time: 169 us -> 150 us (0.89)
  blocking collectives: 18.6 us -> 47.6 us
  waiting for transfers between devices: 74.6 us -> 46.6 us
  starting transfers between devices: 56.3 us -> 37.2 us
    all_gather x0 -> x1, blocking collectives: none -> 33.3 us  [local(): keys = lax.all_gather(served, 'zq', axis=0, tiled=True)]
    all_to_all x6, waiting for transfers between devices: 59.5 us -> 45.2 us  [exchange(): return lax.all_to_all(value, axes, split_axis=0, concat_axis=0, tiled=True)]
    ppermute x4 -> x2, waiting for transfers between devices: 15.1 us -> 1.47 us  [the longest x1 1.46 us: local(): other = lax.ppermute(pieces, 'core', swap)]
    ppermute x4 -> x2, starting transfers between devices: 18.7 us -> 6.19 us  [the longest x1 4.27 us: local(): other_queries = lax.ppermute(all_queries, 'zl', swap)]
    all_to_all x6, starting transfers between devices: 37.6 us -> 31 us  [exchange(): return lax.all_to_all(value, axes, split_axis=0, concat_axis=0, tiled=True)]
    all_to_all x1, blocking collectives: 18.6 us -> 14.2 us  [exchange(): return lax.all_to_all(value, axes, split_axis=0, concat_axis=0, tiled=True)]
  transfers between devices with their start and end apart: 10 -> 8, of which waited for: 8 -> 7; matrix products, arithmetic and copies ran while one was open for 1% -> 2% of each run, Pallas kernels for 1% -> 2%
where the time goes in v7:
time: 150 us; the launch traced here: 149 us
  blocking collectives  47.6 us (32%)
  waiting for transfers between devices  46.6 us (31%)
  starting transfers between devices  37.2 us (25%)
  Pallas kernels  11 us (7%)
  local copies, waits for them, and re-layouts  5.76 us (4%)
    all_to_all x6, waiting for transfers between devices, exchange(): return lax.all_to_all(value, axes, split_axis=0, concat_axis=0, tiled=True)  45.2 us
    all_gather x1, blocking collectives, local(): keys = lax.all_gather(served, 'zq', axis=0, tiled=True)  33.3 us
    all_to_all x6, starting transfers between devices, exchange(): return lax.all_to_all(value, axes, split_axis=0, concat_axis=0, tiled=True)  31 us
    all_to_all x1, blocking collectives, exchange(): return lax.all_to_all(value, axes, split_axis=0, concat_axis=0, tiled=True)  14.2 us
    ppermute x1, starting transfers between devices, local(): other_queries = lax.ppermute(all_queries, 'zl', swap)  4.27 us
    pallas_call x1, Pallas kernels, prompt_attention(): pl.pallas_call(attention_kernel, out_shape=jax.ShapeDtypeStruct((NEAR, SE...  4.24 us
  transfers between devices with their start and end apart: 8, of which 7 were waited for; matrix products, arithmetic and copies ran while one was open for 2% of the time, Pallas kernels for 2%

profile of v7, /device:TPU:8, one launch (start us, length us, event | category | flops | bytes accessed | tf_op | source)
XLA Modules:
  0.0 148.9 jit_solution(16435740004998994581)
XLA Ops:
  0.6 9.1 %all-to-all-start = ((bf16[8,24,576]{2,1,0:T(8,128)(2,1)}), bf16[8,24,576]{2,1,0:T(8,128)(2,1)S(1)}, u32[]{:S(2)}, u32[]{:S(2)}) async-start(bf16[8,24,576]{2,1,0:T(8,128)(2,1)} %bitcast.19), calls=%async_computation | async-start | bytes 491520 | tf_op jit(solution)/shard_map/all_to_all | solution.py:304
  9.8 0.9 copy.15
  10.7 0.0 copy-start.6
  10.7 7.9 %all-to-all-done.mine = bf16[8,24,576]{2,1,0:T(8,128)(2,1)S(1)} async-done(((bf16[8,24,576]{2,1,0:T(8,128)(2,1)}), bf16[8,24,576]{2,1,0:T(8,128)(2,1)S(1)}, u32[]{:S(2)}, u32[]{:S(2)}) %all-to-all-start) | async-done | bytes 221216 | tf_op jit(solution)/shard_map/all_to_all | solution.py:304
  18.6 0.1 copy.16
  18.8 0.9 broadcast_in_dim.18
  19.7 3.9 %all-to-all-start.1 = ((bf16[4,128,576]{1,2,0:T(8,128)(2,1)}), bf16[4,128,576]{1,2,0:T(8,128)(2,1)S(1)}, u32[]{:S(2)}, u32[]{:S(2)}) async-start(bf16[4,128,576]{1,2,0:T(8,128)(2,1)} %broadcast_in_dim.18), calls=%async_computation.1 | async-start | bytes 1179648 | tf_op jit(solution)/shard_map/all_to_all | solution.py:304
  23.6 0.0 copy-done.6
  23.6 0.1 slice.6
  23.7 0.1 slice.7
  23.8 1.9 %collective-permute-start = (bf16[8,24,576]{2,1,0:T(8,128)(2,1)S(1)}, bf16[8,24,576]{2,1,0:T(8,128)(2,1)S(1)}, u32[]{:S(2)}, u32[]{:S(2)}) collective-permute-start(bf16[8,24,576]{2,1,0:T(8,128)(2,1)S(1)} %all-to-all-done.mine), channel_id=1, source_target_pairs={{0,32},{32,0},{1,33},{33,1},{2,34},{34,2},{3,35},{35,3},{4,36},{36... | collective-permute-start | bytes 663560 | tf_op jit(solution)/shard_map/ppermute | solution.py:328
  25.7 1.5 collective-permute-done.other
  27.2 1.4 pick.1
  28.6 3.5 %all-to-all-done.1 = bf16[4,128,576]{1,2,0:T(8,128)(2,1)S(1)} async-done(((bf16[4,128,576]{1,2,0:T(8,128)(2,1)}), bf16[4,128,576]{1,2,0:T(8,128)(2,1)S(1)}, u32[]{:S(2)}, u32[]{:S(2)}) %all-to-all-start.1) | async-done | bytes 589856 | tf_op jit(solution)/shard_map/all_to_all | solution.py:304
  32.0 4.8 %all-to-all-start.2 = ((bf16[8,24,576]{2,1,0:T(8,128)(2,1)}), bf16[8,24,576]{2,1,0:T(8,128)(2,1)S(1)}, u32[]{:S(2)}, u32[]{:S(2)}) async-start(bf16[8,24,576]{2,1,0:T(8,128)(2,1)} %pick.1), calls=%async_computation.2 | async-start | bytes 491520 | tf_op jit(solution)/shard_map/all_to_all | solution.py:304
  36.8 4.3 %collective-permute-start.1 = (bf16[4,128,576]{1,2,0:T(8,128)(2,1)S(1)}, bf16[4,128,576]{1,2,0:T(8,128)(2,1)S(1)}, u32[]{:S(2)}, u32[]{:S(2)}) collective-permute-start(bf16[4,128,576]{1,2,0:T(8,128)(2,1)S(1)} %all-to-all-done.1), channel_id=1, source_target_pairs={{0,4},{4,0},{1,5},{5,1},{2,6},{6,2},{3,7},{7,3},{8,12},{12,8},{9,1... | collective-permute-start | bytes 1769480 | tf_op jit(solution)/shard_map/ppermute | solution.py:332
  41.1 0.3 copy.17.mine
  41.4 3.9 %all-to-all-done.2 = bf16[8,24,576]{2,1,0:T(8,128)(2,1)S(1)} async-done(((bf16[8,24,576]{2,1,0:T(8,128)(2,1)}), bf16[8,24,576]{2,1,0:T(8,128)(2,1)S(1)}, u32[]{:S(2)}, u32[]{:S(2)}) %all-to-all-start.2) | async-done | bytes 221216 | tf_op jit(solution)/shard_map/all_to_all | solution.py:304
  45.3 33.3 %all_gather.3.keys = bf16[768,576]{1,0:T(8,128)(2,1)S(1)} all-gather(bf16[192,576]{1,0:T(8,128)(2,1)S(1)} %bitcast.17), channel_id=1, replica_groups=mesh['y'=8,'core'=2,'zq'=4,'zl'=2,'x'=4] {'zq'}, dimensions={0}, use_global_device_ids=true | all-gather | bytes 1105920 | tf_op jit(solution)/shard_map/all_gather | solution.py:334
  78.7 0.0 collective-permute-done.1
  78.7 0.3 copy.18.other
  79.0 4.2 %prompt_attention.1 = bf16[8,144,512]{2,1,0:T(8,128)(2,1)} custom-call(s32[1]{0:T(128)} %bitcast.1.zl, bf16[4,128,576]{2,1,0:T(8,128)(2,1)S(1)} %copy.17.mine, bf16[4,128,576]{2,1,0:T(8,128)(2,1)S(1)} %copy.18.other, bf16[768,576]{1,0:T(8,128)(2,1)S(1)} %all_gather.3.keys), custom_call_target="tpu_custom_call" | custom-call | tf_op jit(solution)/shard_map/prompt_attention/pallas_call | solution.py:113
  83.2 0.0 copy-start.4
  83.2 0.0 copy-start.1
  83.2 3.7 %all-to-all-start.3 = ((bf16[8,144,512]{2,1,0:T(8,128)(2,1)}), bf16[8,144,512]{2,1,0:T(8,128)(2,1)S(1)}, u32[]{:S(2)}, u32[]{:S(2)}) async-start(bf16[8,144,512]{2,1,0:T(8,128)(2,1)} %prompt_attention.1), calls=%async_computation.3 | async-start | bytes 2359296 | tf_op jit(solution)/shard_map/all_to_all | solution.py:304
  86.9 0.0 copy-done.4
  87.0 0.5 own_attention.1
  87.5 10.7 %all-to-all-done.3.arrived = bf16[8,144,512]{2,1,0:T(8,128)(2,1)S(1)} async-done(((bf16[8,144,512]{2,1,0:T(8,128)(2,1)}), bf16[8,144,512]{2,1,0:T(8,128)(2,1)S(1)}, u32[]{:S(2)}, u32[]{:S(2)}) %all-to-all-start.3) | async-done | bytes 1179680 | tf_op jit(solution)/shard_map/all_to_all | solution.py:304
  98.1 0.0 copy-done.1
  98.1 0.6 combine.1.head_values
  98.7 2.0 %copy-done = bf16[256,7168]{1,0:T(8,128)(2,1)S(1)} copy-done((bf16[256,7168]{1,0:T(8,128)(2,1)S(1)}, bf16[256,7168]{1,0:T(8,128)(2,1)}, u32[]{:S(2)}) %copy-start) | copy-done | bytes 3670040
  100.8 0.7 project.1
  101.4 14.2 %all_to_all.35.arrived = bf16[8,64,896]{2,1,0:T(8,128)(2,1)S(1)} all-to-all(bf16[8,64,896]{2,1,0:T(8,128)(2,1)S(1)} %project.1), channel_id=1, replica_groups=mesh['y'=8,'core'=2,'zq'=4,'zl'=2,'x'=4] {'zl','x'}, dimensions={0} | all-to-all | bytes 1835008 | tf_op jit(solution)/shard_map/all_to_all | solution.py:304
  115.7 0.0 copy-start.2
  115.7 0.9 add.14
  116.6 6.1 %all-to-all-start.5 = ((bf16[4,64,896]{2,1,0:T(8,128)(2,1)}), bf16[4,64,896]{2,1,0:T(8,128)(2,1)S(1)}, u32[]{:S(2)}, u32[]{:S(2)}) async-start(bf16[4,64,896]{2,1,0:T(8,128)(2,1)} %add.14), calls=%async_computation.5 | async-start | bytes 917504 | tf_op jit(solution)/shard_map/all_to_all | solution.py:304
  122.6 0.0 copy-done.2
  122.6 0.0 copy-done.3
  122.6 0.6 slots.1
  123.2 12.6 %all-to-all-done.5.arrived = bf16[4,64,896]{2,1,0:T(8,128)(2,1)S(1)} async-done(((bf16[4,64,896]{2,1,0:T(8,128)(2,1)}), bf16[4,64,896]{2,1,0:T(8,128)(2,1)S(1)}, u32[]{:S(2)}, u32[]{:S(2)}) %all-to-all-start.5) | async-done | bytes 458784 | tf_op jit(solution)/shard_map/all_to_all | solution.py:304
  135.8 1.0 dispatch.1
  136.8 3.4 %all-to-all-start.6 = ((bf16[8,24,896]{2,1,0:T(8,128)(2,1)}), bf16[8,24,896]{2,1,0:T(8,128)(2,1)S(1)}, u32[]{:S(2)}, u32[]{:S(2)}) async-start(bf16[8,24,896]{2,1,0:T(8,128)(2,1)} %bitcast.10), calls=%async_computation.6 | async-start | bytes 688128 | tf_op jit(solution)/shard_map/all_to_all | solution.py:304
  140.3 0.0 copy-done.5
  140.3 0.1 dynamic-slice_reduce_fusion
  140.4 0.1 reshape.35
  140.5 0.7 copy.19
  141.2 6.6 %all-to-all-done.6.arrived = bf16[8,24,896]{2,1,0:T(8,128)(2,1)S(1)} async-done(((bf16[8,24,896]{2,1,0:T(8,128)(2,1)}), bf16[8,24,896]{2,1,0:T(8,128)(2,1)S(1)}, u32[]{:S(2)}, u32[]{:S(2)}) %all-to-all-start.6) | async-done | bytes 344096 | tf_op jit(solution)/shard_map/all_to_all | solution.py:304
  147.7 1.1 norm.1
  (6 shorter events, 0.1 us)
Async XLA Ops:
  0.6 18.0 %all-to-all-start = ((bf16[8,24,576]{2,1,0:T(8,128)(2,1)}), bf16[8,24,576]{2,1,0:T(8,128)(2,1)S(1)}, u32[]{:S(2)}, u32[]{:S(2)}) async-start(bf16[8,24,576]{2,1,0:T(8,128)(2,1)} %bitcast.19), calls=%async_computation | async-start | bytes 491520 | tf_op jit(solution)/shard_map/all_to_all | solution.py:304
  10.7 12.9 %copy-start.6 = (s32[16]{0:T(128)S(1)}, s32[16]{0:T(128)}, u32[]{:S(2)}) copy-start(s32[16]{0:T(128)} %param.10) | copy-start | bytes 196
  19.7 12.3 %all-to-all-start.1 = ((bf16[4,128,576]{1,2,0:T(8,128)(2,1)}), bf16[4,128,576]{1,2,0:T(8,128)(2,1)S(1)}, u32[]{:S(2)}, u32[]{:S(2)}) async-start(bf16[4,128,576]{1,2,0:T(8,128)(2,1)} %broadcast_in_dim.18), calls=%async_computation.1 | async-start | bytes 1179648 | tf_op jit(solution)/shard_map/all_to_all | solution.py:304
  23.8 3.4 %collective-permute-start = (bf16[8,24,576]{2,1,0:T(8,128)(2,1)S(1)}, bf16[8,24,576]{2,1,0:T(8,128)(2,1)S(1)}, u32[]{:S(2)}, u32[]{:S(2)}) collective-permute-start(bf16[8,24,576]{2,1,0:T(8,128)(2,1)S(1)} %all-to-all-done.mine), channel_id=1, source_target_pairs={{0,32},{32,0},{1,33},{33,1},{2,34},{34,2},{3,35},{35,3},{4,36},{36... | collective-permute-start | bytes 663560 | tf_op jit(solution)/shard_map/ppermute | solution.py:328
  32.0 13.3 %all-to-all-start.2 = ((bf16[8,24,576]{2,1,0:T(8,128)(2,1)}), bf16[8,24,576]{2,1,0:T(8,128)(2,1)S(1)}, u32[]{:S(2)}, u32[]{:S(2)}) async-start(bf16[8,24,576]{2,1,0:T(8,128)(2,1)} %pick.1), calls=%async_computation.2 | async-start | bytes 491520 | tf_op jit(solution)/shard_map/all_to_all | solution.py:304
  36.8 41.9 %collective-permute-start.1 = (bf16[4,128,576]{1,2,0:T(8,128)(2,1)S(1)}, bf16[4,128,576]{1,2,0:T(8,128)(2,1)S(1)}, u32[]{:S(2)}, u32[]{:S(2)}) collective-permute-start(bf16[4,128,576]{1,2,0:T(8,128)(2,1)S(1)} %all-to-all-done.1), channel_id=1, source_target_pairs={{0,4},{4,0},{1,5},{5,1},{2,6},{6,2},{3,7},{7,3},{8,12},{12,8},{9,1... | collective-permute-start | bytes 1769480 | tf_op jit(solution)/shard_map/ppermute | solution.py:332
  83.2 3.7 %copy-start.4 = (bf16[1,16,4,576]{3,2,1,0:T(4,128)(2,1)S(1)}, bf16[1,16,4,576]{3,2,1,0:T(4,128)(2,1)}, u32[]{:S(2)}) copy-start(bf16[1,16,4,576]{3,2,1,0:T(4,128)(2,1)} %param.12) | copy-start | bytes 221188
  83.2 14.9 %copy-start.1 = (bf16[2,512,128]{2,1,0:T(8,128)(2,1)S(1)}, bf16[2,512,128]{2,1,0:T(8,128)(2,1)}, u32[]{:S(2)}) copy-start(bf16[2,512,128]{2,1,0:T(8,128)(2,1)} %value_up.1) | copy-start | bytes 786436
  83.2 14.9 %all-to-all-start.3 = ((bf16[8,144,512]{2,1,0:T(8,128)(2,1)}), bf16[8,144,512]{2,1,0:T(8,128)(2,1)S(1)}, u32[]{:S(2)}, u32[]{:S(2)}) async-start(bf16[8,144,512]{2,1,0:T(8,128)(2,1)} %prompt_attention.1), calls=%async_computation.3 | async-start | bytes 2359296 | tf_op jit(solution)/shard_map/all_to_all | solution.py:304
  98.7 2.0 %copy-start = (bf16[256,7168]{1,0:T(8,128)(2,1)S(1)}, bf16[256,7168]{1,0:T(8,128)(2,1)}, u32[]{:S(2)}) copy-start(bf16[256,7168]{1,0:T(8,128)(2,1)} %weight.1) | copy-start | bytes 11010052
  115.7 7.0 %copy-start.2 = (s32[64,8]{0,1:T(8,128)S(1)}, s32[64,8]{0,1:T(8,128)}, u32[]{:S(2)}) copy-start(s32[64,8]{0,1:T(8,128)} %param.16) | copy-start | bytes 6148
  115.7 7.0 %copy-start.3 = (f32[64,8]{0,1:T(8,128)S(1)}, f32[64,8]{0,1:T(8,128)}, u32[]{:S(2)}) copy-start(f32[64,8]{0,1:T(8,128)} %param.17) | copy-start | bytes 6148
  116.5 23.7 %copy-start.5 = (bf16[7168]{0:T(1024)(128)(2,1)S(1)}, bf16[7168]{0:T(1024)(128)(2,1)}, u32[]{:S(2)}) copy-start(bf16[7168]{0:T(1024)(128)(2,1)} %param.15) | copy-start | bytes 43012
  116.6 19.3 %all-to-all-start.5 = ((bf16[4,64,896]{2,1,0:T(8,128)(2,1)}), bf16[4,64,896]{2,1,0:T(8,128)(2,1)S(1)}, u32[]{:S(2)}, u32[]{:S(2)}) async-start(bf16[4,64,896]{2,1,0:T(8,128)(2,1)} %add.14), calls=%async_computation.5 | async-start | bytes 917504 | tf_op jit(solution)/shard_map/all_to_all | solution.py:304
  136.8 10.9 %all-to-all-start.6 = ((bf16[8,24,896]{2,1,0:T(8,128)(2,1)}), bf16[8,24,896]{2,1,0:T(8,128)(2,1)S(1)}, u32[]{:S(2)}, u32[]{:S(2)}) async-start(bf16[8,24,896]{2,1,0:T(8,128)(2,1)} %bitcast.10), calls=%async_computation.6 | async-start | bytes 688128 | tf_op jit(solution)/shard_map/all_to_all | solution.py:304

commit v8 on v7

--- a/solution.py
+++ b/solution.py
@@ -28,6 +28,8 @@
 OWN_SLOTS = SLOTS // DEVS
 NEAR_SLOTS = NEAR * OWN_SLOTS
 SPAN = D // NEAR
+FOUR = 4
+PACKED = LAT_KV // 128 * MINE + ROWS
 
 bf16 = jnp.bfloat16
 f32 = jnp.float32
@@ -39,6 +41,10 @@
     return pltpu.CompilerParams(vmem_limit_bytes=mib * 1024 * 1024)
 
 
+def cost(micros):
+    return pl.CostEstimate(flops=0, bytes_accessed=3_000_000 * micros, transcendentals=0)
+
+
 def dot(a, b, dims=((1,), (0,))):
     return lax.dot_general(a, b, (dims, ((), ())), preferred_element_type=f32)
 
@@ -70,6 +76,42 @@
         compiler_params=params(),
         name="pick",
     )(core, wanted, mine, other)
+
+
+def spread_kernel(query, copies, single):
+    heads = [query[:, head, :] for head in range(2)]
+    rest = jnp.concatenate([head[:, LAT_KV:] for head in heads], axis=1)
+    for head in range(2):
+        single[head * ROWS : (head + 1) * ROWS, :] = heads[head]
+    for i in range(FOUR):
+        for tile in range(LAT_KV // 128):
+            for head in range(2):
+                first = tile * MINE + head * ROWS
+                copies[i, first : first + ROWS, :] = heads[head][:, tile * 128 : (tile + 1) * 128]
+        copies[i, PACKED - ROWS :, :] = rest
+
+
+def spread(query):
+    return pl.pallas_call(
+        spread_kernel,
+        out_shape=(
+            jax.ShapeDtypeStruct((FOUR, PACKED, 128), bf16),
+            jax.ShapeDtypeStruct((MINE, LAT), bf16),
+        ),
+        in_specs=[VMEM],
+        out_specs=(VMEM, VMEM),
+        compiler_params=params(),
+        cost_estimate=cost(2),
+        name="spread",
+    )(query)
+
+
+def unpacked(packed, i):
+    tiles = [packed[i, tile * MINE : (tile + 1) * MINE, :] for tile in range(LAT_KV // 128)]
+    rest = packed[i, PACKED - ROWS :, :]
+    width = LAT - LAT_KV
+    tiles.append(jnp.concatenate([rest[:, :width], rest[:, width:]], axis=0))
+    return jnp.concatenate(tiles, axis=1)
 
 
 def attend(query, keys, visible=None):
@@ -90,16 +132,16 @@
     return high, mid, rest - mid
 
 
-def attention_kernel(zl, mine, other, keys, out):
+def attention_kernel(xh, mine, other, keys, out):
     index = lax.broadcasted_iota(jnp.int32, (16, 128), 0)
     for step in range(NL):
         queries = (mine, other)[step]
-        first = (zl[0] ^ step) * NX
-        query = jnp.concatenate([queries[x] for x in range(NX)], axis=0)
+        first = (xh[0] ^ step) * 2
+        query = jnp.concatenate([unpacked(queries, i) for i in range(FOUR)], axis=0)
         best, total, latent = attend(query, keys[...])
-        for i in range(NX):
+        for i in range(FOUR):
             part = slice(i * MINE, (i + 1) * MINE)
-            owner = first + i
+            owner = first + (i // 2) * NX + i % 2
             out[owner, :MINE, :] = latent[part]
             rows = three(columns_to_lanes(best[part])) + three(columns_to_lanes(total[part]))
             table = jnp.zeros((16, 128), f32)
@@ -109,7 +151,7 @@
             out[owner, MINE:, 128:] = jnp.zeros((16, LAT_KV - 128), bf16)
 
 
-def prompt_attention(zl, mine, other, keys):
+def prompt_attention(xh, mine, other, keys):
     return pl.pallas_call(
         attention_kernel,
         out_shape=jax.ShapeDtypeStruct((NEAR, SENT, LAT_KV), bf16),
@@ -117,7 +159,7 @@
         out_specs=VMEM,
         compiler_params=params(),
         name="prompt_attention",
-    )(zl, mine, other, keys)
+    )(xh, mine, other, keys)
 
 
 def own_kernel(query, keys, latents, stats):
@@ -317,36 +359,36 @@
 ):
     core = lax.axis_index("core")[None].astype(jnp.int32)
     zq = lax.axis_index("zq")[None].astype(jnp.int32)
-    zl = lax.axis_index("zl")[None].astype(jnp.int32)
-    dev = (lax.axis_index("zq") * NL + lax.axis_index("zl")) * NX + lax.axis_index("x")
+    xh = lax.axis_index("xh")[None].astype(jnp.int32)
+    dev = (lax.axis_index("zq") * NL + lax.axis_index("zl")) * NX + (lax.axis_index("xh") * 2 + lax.axis_index("xl"))
     swap = [(0, 1), (1, 0)]
 
-    query = queries.reshape(ROWS, 2, LAT).transpose(1, 0, 2).reshape(MINE, LAT)
+    copies, query = spread(queries.reshape(ROWS, 2, LAT))
     pieces = exchange(prompt_cache.reshape(NY, PIECE, LAT), "y")
-    pieces, query = lax.optimization_barrier((pieces, query))
-    all_queries = exchange(jnp.broadcast_to(query, (NX, MINE, LAT)), "x")
+    pieces, copies = lax.optimization_barrier((pieces, copies))
+    all_queries = exchange(copies, ("zl", "xl"))
     other = lax.ppermute(pieces, "core", swap)
     wanted = jnp.where(core[0] == 0, prompt_of_group[0::2], prompt_of_group[1::2])
     picked = pick(core, wanted, pieces, other)
     picked, all_queries = lax.optimization_barrier((picked, all_queries))
-    other_queries = lax.ppermute(all_queries, "zl", swap)
+    other_queries = lax.ppermute(all_queries, "xh", swap)
     served = exchange(picked, "y").reshape(NY * PIECE, LAT)
     keys = lax.all_gather(served, "zq", axis=0, tiled=True)
     own_latents, own_stats = own_attention(query, new_latents.reshape(ROWS, LAT))
     picks, all_gates = slots(routes.T, gates.T)
     slot_gates = lax.dynamic_slice_in_dim(all_gates, dev * OWN_SLOTS, OWN_SLOTS, 0)
 
-    partial = exchange(prompt_attention(zl, all_queries, other_queries, keys), ("zl", "x"))
+    partial = exchange(prompt_attention(xh, all_queries, other_queries, keys), ("zl", "xh", "xl"))
     head_values = combine(partial, own_latents, own_stats, value_up)
-    sums = exchange(add(exchange(project(head_values, out_weight), ("zl", "x"))), "zq")
+    sums = exchange(add(exchange(project(head_values, out_weight), ("zl", "xh", "xl"))), "zq")
     rows = dispatch(zq, sums, picks).reshape(NEAR, OWN_SLOTS, SPAN)
-    slot_rows = norm(exchange(rows, ("zl", "x")), norm_gain.reshape(1, D))
+    slot_rows = norm(exchange(rows, ("zl", "xh", "xl")), norm_gain.reshape(1, D))
     return (slot_rows[None], slot_gates.reshape(1, OWN_SLOTS // CAP, CAP))
 
 
 def solution(mesh):
-    axes = ("y", "core", "zq", "zl", "x")
-    fine = Mesh(mesh.devices.reshape(NY, 2, NQ, NL, NX), axes)
+    axes = ("y", "core", "zq", "zl", "xh", "xl")
+    fine = Mesh(mesh.devices.reshape(NY, 2, NQ, NL, 2, NX // 2), axes)
     group, dev = axes[:2], axes[2:]
     return jax.shard_map(
         local,

time: 150 us -> 145 us (0.967)
  the two profiles are of different devices: /device:TPU:8 before, /device:TPU:48 now
where the time goes in v8:
time: 145 us; the launch traced here: 144 us
  starting transfers between devices  42.4 us (29%)
  blocking collectives  42.4 us (29%)
  waiting for transfers between devices  42 us (29%)
  Pallas kernels  12.5 us (9%)
  local copies, waits for them, and re-layouts  4.09 us (3%)
    all_to_all x6, waiting for transfers between devices, exchange(): return lax.all_to_all(value, axes, split_axis=0, concat_axis=0, tiled=True)  40.5 us
    all_to_all x6, starting transfers between devices, exchange(): return lax.all_to_all(value, axes, split_axis=0, concat_axis=0, tiled=True)  35.8 us
    all_gather x1, blocking collectives, local(): keys = lax.all_gather(served, 'zq', axis=0, tiled=True)  25.3 us
    all_to_all x1, blocking collectives, exchange(): return lax.all_to_all(value, axes, split_axis=0, concat_axis=0, tiled=True)  17.1 us
    ppermute x1, starting transfers between devices, local(): other_queries = lax.ppermute(all_queries, 'xh', swap)  4.7 us
    pallas_call x1, Pallas kernels, prompt_attention(): pl.pallas_call(attention_kernel, out_shape=jax.ShapeDtypeStruct((NEAR, SE...  4.25 us
    unnamed x17, local copies, waits for them, and re-layouts  3.64 us
  transfers between devices with their start and end apart: 8, of which 7 were waited for; matrix products, arithmetic and copies ran while one was open for 1% of the time, Pallas kernels for 3%

profile of v8, /device:TPU:48, one launch (start us, length us, event | category | flops | bytes accessed | tf_op | source)
XLA Modules:
  0.0 144.2 jit_solution(15798648744184395135)
XLA Ops:
  0.6 0.0 copy-start.7
  0.6 8.6 %all-to-all-start = ((bf16[8,24,576]{2,1,0:T(8,128)(2,1)}), bf16[8,24,576]{2,1,0:T(8,128)(2,1)S(1)}, u32[]{:S(2)}, u32[]{:S(2)}) async-start(bf16[8,24,576]{2,1,0:T(8,128)(2,1)} %bitcast.15), calls=%async_computation | async-start | bytes 491520 | tf_op jit(solution)/shard_map/all_to_all | solution.py:346
  9.2 0.0 copy-start.2
  9.2 0.9 copy-done.2
  10.2 1.6 %spread.1 = (bf16[4,576,128]{2,1,0:T(8,128)(2,1)}, bf16[128,576]{1,0:T(8,128)(2,1)S(1)}) custom-call(bf16[64,2,576]{2,1,0:T(2,128)(2,1)S(1)} %bitcast.10), custom_call_target="tpu_custom_call" | custom-call | bytes 6000000 | tf_op jit(solution)/shard_map/spread/pallas_call | solution.py:95
  11.7 4.0 %all-to-all-done.mine = bf16[8,24,576]{2,1,0:T(8,128)(2,1)S(1)} async-done(((bf16[8,24,576]{2,1,0:T(8,128)(2,1)}), bf16[8,24,576]{2,1,0:T(8,128)(2,1)S(1)}, u32[]{:S(2)}, u32[]{:S(2)}) %all-to-all-start) | async-done | bytes 221216 | tf_op jit(solution)/shard_map/all_to_all | solution.py:346
  15.8 4.2 %all-to-all-start.1 = ((bf16[4,576,128]{2,1,0:T(8,128)(2,1)}), bf16[4,576,128]{2,1,0:T(8,128)(2,1)S(1)}, u32[]{:S(2)}, u32[]{:S(2)}) async-start(bf16[4,576,128]{2,1,0:T(8,128)(2,1)} %get-tuple-element.14), calls=%async_computation.1 | async-start | bytes 1179648 | tf_op jit(solution)/shard_map/all_to_all | solution.py:346
  19.9 0.0 copy-done.7
  19.9 0.1 slice.6
  20.0 0.1 slice.7
  20.1 1.9 %collective-permute-start = (bf16[8,24,576]{2,1,0:T(8,128)(2,1)S(1)}, bf16[8,24,576]{2,1,0:T(8,128)(2,1)S(1)}, u32[]{:S(2)}, u32[]{:S(2)}) collective-permute-start(bf16[8,24,576]{2,1,0:T(8,128)(2,1)S(1)} %all-to-all-done.mine), channel_id=1, source_target_pairs={{0,32},{32,0},{1,33},{33,1},{2,34},{34,2},{3,35},{35,3},{4,36},{36... | collective-permute-start | bytes 663560 | tf_op jit(solution)/shard_map/ppermute | solution.py:370
  22.0 1.5 %collective-permute-done.other = bf16[8,24,576]{2,1,0:T(8,128)(2,1)S(1)} collective-permute-done((bf16[8,24,576]{2,1,0:T(8,128)(2,1)S(1)}, bf16[8,24,576]{2,1,0:T(8,128)(2,1)S(1)}, u32[]{:S(2)}, u32[]{:S(2)}) %collective-permute-start) | collective-permute-done | bytes 221216 | tf_op jit(solution)/shard_map/ppermute | solution.py:370
  23.5 1.4 pick.1
  24.9 3.3 %all-to-all-done.1.mine = bf16[4,576,128]{2,1,0:T(8,128)(2,1)S(1)} async-done(((bf16[4,576,128]{2,1,0:T(8,128)(2,1)}), bf16[4,576,128]{2,1,0:T(8,128)(2,1)S(1)}, u32[]{:S(2)}, u32[]{:S(2)}) %all-to-all-start.1) | async-done | bytes 589856 | tf_op jit(solution)/shard_map/all_to_all | solution.py:346
  28.2 5.9 %all-to-all-start.2 = ((bf16[8,24,576]{2,1,0:T(8,128)(2,1)}), bf16[8,24,576]{2,1,0:T(8,128)(2,1)S(1)}, u32[]{:S(2)}, u32[]{:S(2)}) async-start(bf16[8,24,576]{2,1,0:T(8,128)(2,1)} %pick.1), calls=%async_computation.2 | async-start | bytes 491520 | tf_op jit(solution)/shard_map/all_to_all | solution.py:346
  34.0 4.7 %collective-permute-start.1 = (bf16[4,576,128]{2,1,0:T(8,128)(2,1)S(1)}, bf16[4,576,128]{2,1,0:T(8,128)(2,1)S(1)}, u32[]{:S(2)}, u32[]{:S(2)}) collective-permute-start(bf16[4,576,128]{2,1,0:T(8,128)(2,1)S(1)} %all-to-all-done.1.mine), channel_id=1, source_target_pairs={{0,2},{2,0},{1,3},{3,1},{4,6},{6,4},{5,7},{7,5},{8,10},{10,8},{9,1... | collective-permute-start | bytes 1769480 | tf_op jit(solution)/shard_map/ppermute | solution.py:374
  38.8 2.0 %all-to-all-done.2 = bf16[8,24,576]{2,1,0:T(8,128)(2,1)S(1)} async-done(((bf16[8,24,576]{2,1,0:T(8,128)(2,1)}), bf16[8,24,576]{2,1,0:T(8,128)(2,1)S(1)}, u32[]{:S(2)}, u32[]{:S(2)}) %all-to-all-start.2) | async-done | bytes 221216 | tf_op jit(solution)/shard_map/all_to_all | solution.py:346
  40.7 25.3 %all_gather.3.keys = bf16[768,576]{1,0:T(8,128)(2,1)S(1)} all-gather(bf16[192,576]{1,0:T(8,128)(2,1)S(1)} %bitcast.13), channel_id=1, replica_groups=mesh['y'=8,'core'=2,'zq'=4,'zl'=2,'xh'=2,'xl'=2] {'zq'}, dimensions={0}, use_global_device_ids=true | all-gather | bytes 1105920 | tf_op jit(solution)/shard_map/all_gather | solution.py:376
  66.0 0.0 collective-permute-done.1.other
  66.0 4.2 %prompt_attention.1 = bf16[8,144,512]{2,1,0:T(8,128)(2,1)} custom-call(s32[1]{0:T(128)} %bitcast.1.xh, bf16[4,576,128]{2,1,0:T(8,128)(2,1)S(1)} %all-to-all-done.1.mine, bf16[4,576,128]{2,1,0:T(8,128)(2,1)S(1)} %collective-permute-done.1.other, bf16[768,576]{1,0:T(8,128)(2,1)S(1)} %all_gather.3.keys), custom_call_target="tpu_custom_call" | custom-call | tf_op jit(solution)/shard_map/prompt_attention/pallas_call | solution.py:155
  70.3 0.0 copy-start.5
  70.3 7.0 %all-to-all-start.3 = ((bf16[8,144,512]{2,1,0:T(8,128)(2,1)}), bf16[8,144,512]{2,1,0:T(8,128)(2,1)S(1)}, u32[]{:S(2)}, u32[]{:S(2)}) async-start(bf16[8,144,512]{2,1,0:T(8,128)(2,1)} %prompt_attention.1), calls=%async_computation.3 | async-start | bytes 2359296 | tf_op jit(solution)/shard_map/all_to_all | solution.py:346
  77.3 0.0 copy-done.5
  77.3 0.5 own_attention.1
  77.8 13.1 %all-to-all-done.3.arrived = bf16[8,144,512]{2,1,0:T(8,128)(2,1)S(1)} async-done(((bf16[8,144,512]{2,1,0:T(8,128)(2,1)}), bf16[8,144,512]{2,1,0:T(8,128)(2,1)S(1)}, u32[]{:S(2)}, u32[]{:S(2)}) %all-to-all-start.3) | async-done | bytes 1179680 | tf_op jit(solution)/shard_map/all_to_all | solution.py:346
  90.9 0.0 copy-done.1
  90.9 0.6 combine.1.head_values
  91.5 0.0 copy-start
  91.5 2.0 %copy-done = bf16[256,7168]{1,0:T(8,128)(2,1)S(1)} copy-done((bf16[256,7168]{1,0:T(8,128)(2,1)S(1)}, bf16[256,7168]{1,0:T(8,128)(2,1)}, u32[]{:S(2)}) %copy-start) | copy-done | bytes 3670040
  93.6 0.7 project.1
  94.2 17.1 %all_to_all.35.arrived = bf16[8,64,896]{2,1,0:T(8,128)(2,1)S(1)} all-to-all(bf16[8,64,896]{2,1,0:T(8,128)(2,1)S(1)} %project.1), channel_id=1, replica_groups=mesh['y'=8,'core'=2,'zq'=4,'zl'=2,'xh'=2,'xl'=2] {'zl','xh','xl'}, dimensions={0} | all-to-all | bytes 1835008 | tf_op jit(solution)/shard_map/all_to_all | solution.py:346
  111.4 0.0 copy-start.3
  111.4 0.0 copy-start.4
  111.4 0.9 add.18
  112.3 0.0 copy-start.6
  112.3 5.6 %all-to-all-start.5 = ((bf16[4,64,896]{2,1,0:T(8,128)(2,1)}), bf16[4,64,896]{2,1,0:T(8,128)(2,1)S(1)}, u32[]{:S(2)}, u32[]{:S(2)}) async-start(bf16[4,64,896]{2,1,0:T(8,128)(2,1)} %add.18), calls=%async_computation.5 | async-start | bytes 917504 | tf_op jit(solution)/shard_map/all_to_all | solution.py:346
  117.9 0.0 copy-done.3
  117.9 0.0 copy-done.4
  117.9 0.6 slots.1
  118.5 11.4 %all-to-all-done.5.arrived = bf16[4,64,896]{2,1,0:T(8,128)(2,1)S(1)} async-done(((bf16[4,64,896]{2,1,0:T(8,128)(2,1)}), bf16[4,64,896]{2,1,0:T(8,128)(2,1)S(1)}, u32[]{:S(2)}, u32[]{:S(2)}) %all-to-all-start.5) | async-done | bytes 458784 | tf_op jit(solution)/shard_map/all_to_all | solution.py:346
  130.0 1.0 dispatch.1
  130.9 4.5 %all-to-all-start.6 = ((bf16[8,24,896]{2,1,0:T(8,128)(2,1)}), bf16[8,24,896]{2,1,0:T(8,128)(2,1)S(1)}, u32[]{:S(2)}, u32[]{:S(2)}) async-start(bf16[8,24,896]{2,1,0:T(8,128)(2,1)} %bitcast.8), calls=%async_computation.6 | async-start | bytes 688128 | tf_op jit(solution)/shard_map/all_to_all | solution.py:346
  135.5 0.0 copy-done.6
  135.5 0.1 dynamic-slice_reduce_fusion
  135.6 0.1 reshape.31
  135.7 0.7 copy.12
  136.4 6.6 %all-to-all-done.6.arrived = bf16[8,24,896]{2,1,0:T(8,128)(2,1)S(1)} async-done(((bf16[8,24,896]{2,1,0:T(8,128)(2,1)}), bf16[8,24,896]{2,1,0:T(8,128)(2,1)S(1)}, u32[]{:S(2)}, u32[]{:S(2)}) %all-to-all-start.6) | async-done | bytes 344096 | tf_op jit(solution)/shard_map/all_to_all | solution.py:346
  143.0 1.1 norm.1
  (4 shorter events, 0.1 us)
Async XLA Ops:
  0.6 19.3 %copy-start.7 = (s32[16]{0:T(128)S(1)}, s32[16]{0:T(128)}, u32[]{:S(2)}) copy-start(s32[16]{0:T(128)} %param.10) | copy-start | bytes 196
  0.6 15.1 %all-to-all-start = ((bf16[8,24,576]{2,1,0:T(8,128)(2,1)}), bf16[8,24,576]{2,1,0:T(8,128)(2,1)S(1)}, u32[]{:S(2)}, u32[]{:S(2)}) async-start(bf16[8,24,576]{2,1,0:T(8,128)(2,1)} %bitcast.15), calls=%async_computation | async-start | bytes 491520 | tf_op jit(solution)/shard_map/all_to_all | solution.py:346
  9.2 0.9 copy-start.2
  15.8 12.4 %all-to-all-start.1 = ((bf16[4,576,128]{2,1,0:T(8,128)(2,1)}), bf16[4,576,128]{2,1,0:T(8,128)(2,1)S(1)}, u32[]{:S(2)}, u32[]{:S(2)}) async-start(bf16[4,576,128]{2,1,0:T(8,128)(2,1)} %get-tuple-element.14), calls=%async_computation.1 | async-start | bytes 1179648 | tf_op jit(solution)/shard_map/all_to_all | solution.py:346
  20.1 3.4 %collective-permute-start = (bf16[8,24,576]{2,1,0:T(8,128)(2,1)S(1)}, bf16[8,24,576]{2,1,0:T(8,128)(2,1)S(1)}, u32[]{:S(2)}, u32[]{:S(2)}) collective-permute-start(bf16[8,24,576]{2,1,0:T(8,128)(2,1)S(1)} %all-to-all-done.mine), channel_id=1, source_target_pairs={{0,32},{32,0},{1,33},{33,1},{2,34},{34,2},{3,35},{35,3},{4,36},{36... | collective-permute-start | bytes 663560 | tf_op jit(solution)/shard_map/ppermute | solution.py:370
  28.2 12.6 %all-to-all-start.2 = ((bf16[8,24,576]{2,1,0:T(8,128)(2,1)}), bf16[8,24,576]{2,1,0:T(8,128)(2,1)S(1)}, u32[]{:S(2)}, u32[]{:S(2)}) async-start(bf16[8,24,576]{2,1,0:T(8,128)(2,1)} %pick.1), calls=%async_computation.2 | async-start | bytes 491520 | tf_op jit(solution)/shard_map/all_to_all | solution.py:346
  34.0 32.0 %collective-permute-start.1 = (bf16[4,576,128]{2,1,0:T(8,128)(2,1)S(1)}, bf16[4,576,128]{2,1,0:T(8,128)(2,1)S(1)}, u32[]{:S(2)}, u32[]{:S(2)}) collective-permute-start(bf16[4,576,128]{2,1,0:T(8,128)(2,1)S(1)} %all-to-all-done.1.mine), channel_id=1, source_target_pairs={{0,2},{2,0},{1,3},{3,1},{4,6},{6,4},{5,7},{7,5},{8,10},{10,8},{9,1... | collective-permute-start | bytes 1769480 | tf_op jit(solution)/shard_map/ppermute | solution.py:374
  70.3 7.0 %copy-start.5 = (bf16[1,16,4,576]{3,2,1,0:T(4,128)(2,1)S(1)}, bf16[1,16,4,576]{3,2,1,0:T(4,128)(2,1)}, u32[]{:S(2)}) copy-start(bf16[1,16,4,576]{3,2,1,0:T(4,128)(2,1)} %param.12) | copy-start | bytes 221188
  70.3 20.6 %copy-start.1 = (bf16[2,512,128]{2,1,0:T(8,128)(2,1)S(1)}, bf16[2,512,128]{2,1,0:T(8,128)(2,1)}, u32[]{:S(2)}) copy-start(bf16[2,512,128]{2,1,0:T(8,128)(2,1)} %value_up.1) | copy-start | bytes 786436
  70.3 20.6 %all-to-all-start.3 = ((bf16[8,144,512]{2,1,0:T(8,128)(2,1)}), bf16[8,144,512]{2,1,0:T(8,128)(2,1)S(1)}, u32[]{:S(2)}, u32[]{:S(2)}) async-start(bf16[8,144,512]{2,1,0:T(8,128)(2,1)} %prompt_attention.1), calls=%async_computation.3 | async-start | bytes 2359296 | tf_op jit(solution)/shard_map/all_to_all | solution.py:346
  91.5 2.0 %copy-start = (bf16[256,7168]{1,0:T(8,128)(2,1)S(1)}, bf16[256,7168]{1,0:T(8,128)(2,1)}, u32[]{:S(2)}) copy-start(bf16[256,7168]{1,0:T(8,128)(2,1)} %weight.1) | copy-start | bytes 11010052
  111.4 6.5 %copy-start.3 = (s32[64,8]{0,1:T(8,128)S(1)}, s32[64,8]{0,1:T(8,128)}, u32[]{:S(2)}) copy-start(s32[64,8]{0,1:T(8,128)} %param.16) | copy-start | bytes 6148
  111.4 6.5 %copy-start.4 = (f32[64,8]{0,1:T(8,128)S(1)}, f32[64,8]{0,1:T(8,128)}, u32[]{:S(2)}) copy-start(f32[64,8]{0,1:T(8,128)} %param.17) | copy-start | bytes 6148
  112.3 23.2 %copy-start.6 = (bf16[7168]{0:T(1024)(128)(2,1)S(1)}, bf16[7168]{0:T(1024)(128)(2,1)}, u32[]{:S(2)}) copy-start(bf16[7168]{0:T(1024)(128)(2,1)} %param.15) | copy-start | bytes 43012
  112.3 17.7 %all-to-all-start.5 = ((bf16[4,64,896]{2,1,0:T(8,128)(2,1)}), bf16[4,64,896]{2,1,0:T(8,128)(2,1)S(1)}, u32[]{:S(2)}, u32[]{:S(2)}) async-start(bf16[4,64,896]{2,1,0:T(8,128)(2,1)} %add.18), calls=%async_computation.5 | async-start | bytes 917504 | tf_op jit(solution)/shard_map/all_to_all | solution.py:346
  130.9 12.1 %all-to-all-start.6 = ((bf16[8,24,896]{2,1,0:T(8,128)(2,1)}), bf16[8,24,896]{2,1,0:T(8,128)(2,1)S(1)}, u32[]{:S(2)}, u32[]{:S(2)}) async-start(bf16[8,24,896]{2,1,0:T(8,128)(2,1)} %bitcast.8), calls=%async_computation.6 | async-start | bytes 688128 | tf_op jit(solution)/shard_map/all_to_all | solution.py:346

commit v9 on v8

--- a/solution.py
+++ b/solution.py
@@ -23,7 +23,9 @@
 PIECE = 192 // NY
 KEYS = 192 * NQ
 MINE = 2 * ROWS
-SENT = MINE + 16
+LANES = LAT_KV // 128
+STATS = LANES * MINE
+SENT = STATS + 16
 SLOTS = EXPERTS * CAP
 OWN_SLOTS = SLOTS // DEVS
 NEAR_SLOTS = NEAR * OWN_SLOTS
@@ -134,27 +136,28 @@
 
 def attention_kernel(xh, mine, other, keys, out):
     index = lax.broadcasted_iota(jnp.int32, (16, 128), 0)
-    for step in range(NL):
-        queries = (mine, other)[step]
-        first = (xh[0] ^ step) * 2
-        query = jnp.concatenate([unpacked(queries, i) for i in range(FOUR)], axis=0)
+    for step in range(1):
+        query = jnp.concatenate(
+            [unpacked(queries, i) for queries in (mine, other) for i in range(FOUR)], axis=0
+        )
         best, total, latent = attend(query, keys[...])
-        for i in range(FOUR):
+        for i in range(2 * FOUR):
             part = slice(i * MINE, (i + 1) * MINE)
-            owner = first + (i // 2) * NX + i % 2
-            out[owner, :MINE, :] = latent[part]
+            owner = (xh[0] ^ (i // FOUR)) * 2 + (i % FOUR // 2) * NX + i % 2
+            for tile in range(LANES):
+                lanes = slice(tile * 128, (tile + 1) * 128)
+                out[owner, tile * MINE : (tile + 1) * MINE, :] = latent[part, lanes]
             rows = three(columns_to_lanes(best[part])) + three(columns_to_lanes(total[part]))
             table = jnp.zeros((16, 128), f32)
             for j, row in enumerate(rows):
                 table = jnp.where(index == j, jnp.broadcast_to(row, (16, 128)), table)
-            out[owner, MINE:, :128] = table.astype(bf16)
-            out[owner, MINE:, 128:] = jnp.zeros((16, LAT_KV - 128), bf16)
+            out[owner, STATS:, :] = table.astype(bf16)
 
 
 def prompt_attention(xh, mine, other, keys):
     return pl.pallas_call(
         attention_kernel,
-        out_shape=jax.ShapeDtypeStruct((NEAR, SENT, LAT_KV), bf16),
+        out_shape=jax.ShapeDtypeStruct((NEAR, SENT, 128), bf16),
         in_specs=[SMEM] + [VMEM] * 3,
         out_specs=VMEM,
         compiler_params=params(),
@@ -193,7 +196,7 @@
 def combine_kernel(arrived, own_latents, own_stats, value_up, out):
     bests, totals = [own_stats[0:1, :]], [own_stats[1:2, :]]
     for z in range(NEAR):
-        stats = arrived[z, MINE:, :128].astype(f32)
+        stats = arrived[z, STATS:, :].astype(f32)
         bests.append(stats[0:1] + stats[1:2] + stats[2:3])
         totals.append(stats[3:4] + stats[4:5] + stats[5:6])
     top = bests[0]
@@ -208,10 +211,15 @@
     for i, share in enumerate(shares):
         table = jnp.where(index == i, jnp.broadcast_to(share / whole, (128, 128)), table)
     table = jnp.transpose(table)
-    latent = table[:, 0:1] * own_latents[...].astype(f32)
-    for z in range(NEAR):
-        latent = latent + table[:, z + 1 : z + 2] * arrived[z, :MINE, :].astype(f32)
-    latent = latent.astype(bf16)
+    tiles = []
+    for tile in range(LANES):
+        lanes = slice(tile * 128, (tile + 1) * 128)
+        latent = table[:, 0:1] * own_latents[:, lanes].astype(f32)
+        for z in range(NEAR):
+            part = arrived[z, tile * MINE : (tile + 1) * MINE, :].astype(f32)
+            latent = latent + table[:, z + 1 : z + 2] * part
+        tiles.append(latent.astype(bf16))
+    latent = jnp.concatenate(tiles, axis=1)
     for head in range(2):
         values = dot(latent[head * ROWS : (head + 1) * ROWS], value_up[head])
         out[:, head * HEAD_V : (head + 1) * HEAD_V] = values.astype(bf16)

time: 145 us -> 143 us (0.986)
  no operation moved by 1% of the time
where the time goes in v9:
time: 143 us; the launch traced here: 142 us
  blocking collectives  42.4 us (30%)
  starting transfers between devices  42.3 us (30%)
  waiting for transfers between devices  40.9 us (29%)
  Pallas kernels  11.9 us (8%)
  local copies, waits for them, and re-layouts  4.09 us (3%)
    all_to_all x6, waiting for transfers between devices, exchange(): return lax.all_to_all(value, axes, split_axis=0, concat_axis=0, tiled=True)  39.4 us
    all_to_all x6, starting transfers between devices, exchange(): return lax.all_to_all(value, axes, split_axis=0, concat_axis=0, tiled=True)  35.6 us
    all_gather x1, blocking collectives, local(): keys = lax.all_gather(served, 'zq', axis=0, tiled=True)  25.3 us
    all_to_all x1, blocking collectives, exchange(): return lax.all_to_all(value, axes, split_axis=0, concat_axis=0, tiled=True)  17.1 us
    ppermute x1, starting transfers between devices, local(): other_queries = lax.ppermute(all_queries, 'xh', swap)  4.7 us
    unnamed x17, local copies, waits for them, and re-layouts  3.64 us
    pallas_call x1, Pallas kernels, prompt_attention(): pl.pallas_call(attention_kernel, out_shape=jax.ShapeDtypeStruct((NEAR, SE...  3.55 us
  transfers between devices with their start and end apart: 8, of which 7 were waited for; matrix products, arithmetic and copies ran while one was open for 1% of the time, Pallas kernels for 3%

profile of v9, /device:TPU:48, one launch (start us, length us, event | category | flops | bytes accessed | tf_op | source)
XLA Modules:
  0.0 142.3 jit_solution(13006031694729377372)
XLA Ops:
  0.6 0.0 copy-start.7
  0.6 8.6 %all-to-all-start = ((bf16[8,24,576]{2,1,0:T(8,128)(2,1)}), bf16[8,24,576]{2,1,0:T(8,128)(2,1)S(1)}, u32[]{:S(2)}, u32[]{:S(2)}) async-start(bf16[8,24,576]{2,1,0:T(8,128)(2,1)} %bitcast.15), calls=%async_computation | async-start | bytes 491520 | tf_op jit(solution)/shard_map/all_to_all | solution.py:354
  9.2 0.0 copy-start.2
  9.2 0.9 copy-done.2
  10.2 1.6 %spread.1 = (bf16[4,576,128]{2,1,0:T(8,128)(2,1)}, bf16[128,576]{1,0:T(8,128)(2,1)S(1)}) custom-call(bf16[64,2,576]{2,1,0:T(2,128)(2,1)S(1)} %bitcast.10), custom_call_target="tpu_custom_call" | custom-call | bytes 6000000 | tf_op jit(solution)/shard_map/spread/pallas_call | solution.py:97
  11.7 4.0 %all-to-all-done.mine = bf16[8,24,576]{2,1,0:T(8,128)(2,1)S(1)} async-done(((bf16[8,24,576]{2,1,0:T(8,128)(2,1)}), bf16[8,24,576]{2,1,0:T(8,128)(2,1)S(1)}, u32[]{:S(2)}, u32[]{:S(2)}) %all-to-all-start) | async-done | bytes 221216 | tf_op jit(solution)/shard_map/all_to_all | solution.py:354
  15.8 4.2 %all-to-all-start.1 = ((bf16[4,576,128]{2,1,0:T(8,128)(2,1)}), bf16[4,576,128]{2,1,0:T(8,128)(2,1)S(1)}, u32[]{:S(2)}, u32[]{:S(2)}) async-start(bf16[4,576,128]{2,1,0:T(8,128)(2,1)} %get-tuple-element.14), calls=%async_computation.1 | async-start | bytes 1179648 | tf_op jit(solution)/shard_map/all_to_all | solution.py:354
  19.9 0.0 copy-done.7
  19.9 0.1 slice.6
  20.0 0.1 slice.7
  20.1 1.9 %collective-permute-start = (bf16[8,24,576]{2,1,0:T(8,128)(2,1)S(1)}, bf16[8,24,576]{2,1,0:T(8,128)(2,1)S(1)}, u32[]{:S(2)}, u32[]{:S(2)}) collective-permute-start(bf16[8,24,576]{2,1,0:T(8,128)(2,1)S(1)} %all-to-all-done.mine), channel_id=1, source_target_pairs={{0,32},{32,0},{1,33},{33,1},{2,34},{34,2},{3,35},{35,3},{4,36},{36... | collective-permute-start | bytes 663560 | tf_op jit(solution)/shard_map/ppermute | solution.py:378
  22.0 1.5 %collective-permute-done.other = bf16[8,24,576]{2,1,0:T(8,128)(2,1)S(1)} collective-permute-done((bf16[8,24,576]{2,1,0:T(8,128)(2,1)S(1)}, bf16[8,24,576]{2,1,0:T(8,128)(2,1)S(1)}, u32[]{:S(2)}, u32[]{:S(2)}) %collective-permute-start) | collective-permute-done | bytes 221216 | tf_op jit(solution)/shard_map/ppermute | solution.py:378
  23.5 1.4 pick.1
  24.9 3.3 %all-to-all-done.1.mine = bf16[4,576,128]{2,1,0:T(8,128)(2,1)S(1)} async-done(((bf16[4,576,128]{2,1,0:T(8,128)(2,1)}), bf16[4,576,128]{2,1,0:T(8,128)(2,1)S(1)}, u32[]{:S(2)}, u32[]{:S(2)}) %all-to-all-start.1) | async-done | bytes 589856 | tf_op jit(solution)/shard_map/all_to_all | solution.py:354
  28.2 5.9 %all-to-all-start.2 = ((bf16[8,24,576]{2,1,0:T(8,128)(2,1)}), bf16[8,24,576]{2,1,0:T(8,128)(2,1)S(1)}, u32[]{:S(2)}, u32[]{:S(2)}) async-start(bf16[8,24,576]{2,1,0:T(8,128)(2,1)} %pick.1), calls=%async_computation.2 | async-start | bytes 491520 | tf_op jit(solution)/shard_map/all_to_all | solution.py:354
  34.0 4.7 %collective-permute-start.1 = (bf16[4,576,128]{2,1,0:T(8,128)(2,1)S(1)}, bf16[4,576,128]{2,1,0:T(8,128)(2,1)S(1)}, u32[]{:S(2)}, u32[]{:S(2)}) collective-permute-start(bf16[4,576,128]{2,1,0:T(8,128)(2,1)S(1)} %all-to-all-done.1.mine), channel_id=1, source_target_pairs={{0,2},{2,0},{1,3},{3,1},{4,6},{6,4},{5,7},{7,5},{8,10},{10,8},{9,1... | collective-permute-start | bytes 1769480 | tf_op jit(solution)/shard_map/ppermute | solution.py:382
  38.8 2.0 %all-to-all-done.2 = bf16[8,24,576]{2,1,0:T(8,128)(2,1)S(1)} async-done(((bf16[8,24,576]{2,1,0:T(8,128)(2,1)}), bf16[8,24,576]{2,1,0:T(8,128)(2,1)S(1)}, u32[]{:S(2)}, u32[]{:S(2)}) %all-to-all-start.2) | async-done | bytes 221216 | tf_op jit(solution)/shard_map/all_to_all | solution.py:354
  40.7 25.3 %all_gather.3.keys = bf16[768,576]{1,0:T(8,128)(2,1)S(1)} all-gather(bf16[192,576]{1,0:T(8,128)(2,1)S(1)} %bitcast.13), channel_id=1, replica_groups=mesh['y'=8,'core'=2,'zq'=4,'zl'=2,'xh'=2,'xl'=2] {'zq'}, dimensions={0}, use_global_device_ids=true | all-gather | bytes 1105920 | tf_op jit(solution)/shard_map/all_gather | solution.py:384
  66.0 0.0 collective-permute-done.1.other
  66.0 3.6 %prompt_attention.1 = bf16[8,528,128]{2,1,0:T(8,128)(2,1)} custom-call(s32[1]{0:T(128)} %bitcast.1.xh, bf16[4,576,128]{2,1,0:T(8,128)(2,1)S(1)} %all-to-all-done.1.mine, bf16[4,576,128]{2,1,0:T(8,128)(2,1)S(1)} %collective-permute-done.1.other, bf16[768,576]{1,0:T(8,128)(2,1)S(1)} %all_gather.3.keys), custom_call_target="tpu_custom_call" | custom-call | tf_op jit(solution)/shard_map/prompt_attention/pallas_call | solution.py:158
  69.6 0.0 copy-start.5
  69.6 0.0 copy-start.1
  69.6 7.0 %all-to-all-start.3 = ((bf16[8,528,128]{2,1,0:T(8,128)(2,1)}), bf16[8,528,128]{2,1,0:T(8,128)(2,1)S(1)}, u32[]{:S(2)}, u32[]{:S(2)}) async-start(bf16[8,528,128]{2,1,0:T(8,128)(2,1)} %prompt_attention.1), calls=%async_computation.3 | async-start | bytes 2162688 | tf_op jit(solution)/shard_map/all_to_all | solution.py:354
  76.6 0.0 copy-done.5
  76.6 0.5 own_attention.1
  77.1 12.1 %all-to-all-done.3.arrived = bf16[8,528,128]{2,1,0:T(8,128)(2,1)S(1)} async-done(((bf16[8,528,128]{2,1,0:T(8,128)(2,1)}), bf16[8,528,128]{2,1,0:T(8,128)(2,1)S(1)}, u32[]{:S(2)}, u32[]{:S(2)}) %all-to-all-start.3) | async-done | bytes 1081376 | tf_op jit(solution)/shard_map/all_to_all | solution.py:354
  89.2 0.0 copy-done.1
  89.2 0.6 combine.1.head_values
  89.8 0.0 copy-start
  89.8 2.0 %copy-done = bf16[256,7168]{1,0:T(8,128)(2,1)S(1)} copy-done((bf16[256,7168]{1,0:T(8,128)(2,1)S(1)}, bf16[256,7168]{1,0:T(8,128)(2,1)}, u32[]{:S(2)}) %copy-start) | copy-done | bytes 3670040
  91.8 0.7 project.1
  92.5 17.1 %all_to_all.35.arrived = bf16[8,64,896]{2,1,0:T(8,128)(2,1)S(1)} all-to-all(bf16[8,64,896]{2,1,0:T(8,128)(2,1)S(1)} %project.1), channel_id=1, replica_groups=mesh['y'=8,'core'=2,'zq'=4,'zl'=2,'xh'=2,'xl'=2] {'zl','xh','xl'}, dimensions={0} | all-to-all | bytes 1835008 | tf_op jit(solution)/shard_map/all_to_all | solution.py:354
  109.6 0.0 copy-start.3
  109.6 0.0 copy-start.4
  109.6 0.9 add.18
  110.5 5.5 %all-to-all-start.5 = ((bf16[4,64,896]{2,1,0:T(8,128)(2,1)}), bf16[4,64,896]{2,1,0:T(8,128)(2,1)S(1)}, u32[]{:S(2)}, u32[]{:S(2)}) async-start(bf16[4,64,896]{2,1,0:T(8,128)(2,1)} %add.18), calls=%async_computation.5 | async-start | bytes 917504 | tf_op jit(solution)/shard_map/all_to_all | solution.py:354
  116.0 0.0 copy-done.3
  116.0 0.0 copy-done.4
  116.0 0.6 slots.1
  116.6 11.4 %all-to-all-done.5.arrived = bf16[4,64,896]{2,1,0:T(8,128)(2,1)S(1)} async-done(((bf16[4,64,896]{2,1,0:T(8,128)(2,1)}), bf16[4,64,896]{2,1,0:T(8,128)(2,1)S(1)}, u32[]{:S(2)}, u32[]{:S(2)}) %all-to-all-start.5) | async-done | bytes 458784 | tf_op jit(solution)/shard_map/all_to_all | solution.py:354
  128.1 1.0 dispatch.1
  129.1 4.5 %all-to-all-start.6 = ((bf16[8,24,896]{2,1,0:T(8,128)(2,1)}), bf16[8,24,896]{2,1,0:T(8,128)(2,1)S(1)}, u32[]{:S(2)}, u32[]{:S(2)}) async-start(bf16[8,24,896]{2,1,0:T(8,128)(2,1)} %bitcast.8), calls=%async_computation.6 | async-start | bytes 688128 | tf_op jit(solution)/shard_map/all_to_all | solution.py:354
  133.6 0.0 copy-done.6
  133.6 0.1 dynamic-slice_reduce_fusion
  133.8 0.1 reshape.31
  133.8 0.7 copy.12
  134.5 6.6 %all-to-all-done.6.arrived = bf16[8,24,896]{2,1,0:T(8,128)(2,1)S(1)} async-done(((bf16[8,24,896]{2,1,0:T(8,128)(2,1)}), bf16[8,24,896]{2,1,0:T(8,128)(2,1)S(1)}, u32[]{:S(2)}, u32[]{:S(2)}) %all-to-all-start.6) | async-done | bytes 344096 | tf_op jit(solution)/shard_map/all_to_all | solution.py:354
  141.2 1.1 norm.1
  (4 shorter events, 0.1 us)
Async XLA Ops:
  0.6 19.3 %copy-start.7 = (s32[16]{0:T(128)S(1)}, s32[16]{0:T(128)}, u32[]{:S(2)}) copy-start(s32[16]{0:T(128)} %param.10) | copy-start | bytes 196
  0.6 15.1 %all-to-all-start = ((bf16[8,24,576]{2,1,0:T(8,128)(2,1)}), bf16[8,24,576]{2,1,0:T(8,128)(2,1)S(1)}, u32[]{:S(2)}, u32[]{:S(2)}) async-start(bf16[8,24,576]{2,1,0:T(8,128)(2,1)} %bitcast.15), calls=%async_computation | async-start | bytes 491520 | tf_op jit(solution)/shard_map/all_to_all | solution.py:354
  9.2 0.9 copy-start.2
  15.8 12.4 %all-to-all-start.1 = ((bf16[4,576,128]{2,1,0:T(8,128)(2,1)}), bf16[4,576,128]{2,1,0:T(8,128)(2,1)S(1)}, u32[]{:S(2)}, u32[]{:S(2)}) async-start(bf16[4,576,128]{2,1,0:T(8,128)(2,1)} %get-tuple-element.14), calls=%async_computation.1 | async-start | bytes 1179648 | tf_op jit(solution)/shard_map/all_to_all | solution.py:354
  20.1 3.4 %collective-permute-start = (bf16[8,24,576]{2,1,0:T(8,128)(2,1)S(1)}, bf16[8,24,576]{2,1,0:T(8,128)(2,1)S(1)}, u32[]{:S(2)}, u32[]{:S(2)}) collective-permute-start(bf16[8,24,576]{2,1,0:T(8,128)(2,1)S(1)} %all-to-all-done.mine), channel_id=1, source_target_pairs={{0,32},{32,0},{1,33},{33,1},{2,34},{34,2},{3,35},{35,3},{4,36},{36... | collective-permute-start | bytes 663560 | tf_op jit(solution)/shard_map/ppermute | solution.py:378
  28.2 12.6 %all-to-all-start.2 = ((bf16[8,24,576]{2,1,0:T(8,128)(2,1)}), bf16[8,24,576]{2,1,0:T(8,128)(2,1)S(1)}, u32[]{:S(2)}, u32[]{:S(2)}) async-start(bf16[8,24,576]{2,1,0:T(8,128)(2,1)} %pick.1), calls=%async_computation.2 | async-start | bytes 491520 | tf_op jit(solution)/shard_map/all_to_all | solution.py:354
  34.0 32.0 %collective-permute-start.1 = (bf16[4,576,128]{2,1,0:T(8,128)(2,1)S(1)}, bf16[4,576,128]{2,1,0:T(8,128)(2,1)S(1)}, u32[]{:S(2)}, u32[]{:S(2)}) collective-permute-start(bf16[4,576,128]{2,1,0:T(8,128)(2,1)S(1)} %all-to-all-done.1.mine), channel_id=1, source_target_pairs={{0,2},{2,0},{1,3},{3,1},{4,6},{6,4},{5,7},{7,5},{8,10},{10,8},{9,1... | collective-permute-start | bytes 1769480 | tf_op jit(solution)/shard_map/ppermute | solution.py:382
  69.6 7.0 %copy-start.5 = (bf16[1,16,4,576]{3,2,1,0:T(4,128)(2,1)S(1)}, bf16[1,16,4,576]{3,2,1,0:T(4,128)(2,1)}, u32[]{:S(2)}) copy-start(bf16[1,16,4,576]{3,2,1,0:T(4,128)(2,1)} %param.12) | copy-start | bytes 221188
  69.6 19.6 %copy-start.1 = (bf16[2,512,128]{2,1,0:T(8,128)(2,1)S(1)}, bf16[2,512,128]{2,1,0:T(8,128)(2,1)}, u32[]{:S(2)}) copy-start(bf16[2,512,128]{2,1,0:T(8,128)(2,1)} %value_up.1) | copy-start | bytes 786436
  69.6 19.6 %all-to-all-start.3 = ((bf16[8,528,128]{2,1,0:T(8,128)(2,1)}), bf16[8,528,128]{2,1,0:T(8,128)(2,1)S(1)}, u32[]{:S(2)}, u32[]{:S(2)}) async-start(bf16[8,528,128]{2,1,0:T(8,128)(2,1)} %prompt_attention.1), calls=%async_computation.3 | async-start | bytes 2162688 | tf_op jit(solution)/shard_map/all_to_all | solution.py:354
  89.8 2.1 %copy-start = (bf16[256,7168]{1,0:T(8,128)(2,1)S(1)}, bf16[256,7168]{1,0:T(8,128)(2,1)}, u32[]{:S(2)}) copy-start(bf16[256,7168]{1,0:T(8,128)(2,1)} %weight.1) | copy-start | bytes 11010052
  109.6 6.4 %copy-start.3 = (s32[64,8]{0,1:T(8,128)S(1)}, s32[64,8]{0,1:T(8,128)}, u32[]{:S(2)}) copy-start(s32[64,8]{0,1:T(8,128)} %param.16) | copy-start | bytes 6148
  109.6 6.4 %copy-start.4 = (f32[64,8]{0,1:T(8,128)S(1)}, f32[64,8]{0,1:T(8,128)}, u32[]{:S(2)}) copy-start(f32[64,8]{0,1:T(8,128)} %param.17) | copy-start | bytes 6148
  110.5 17.6 %all-to-all-start.5 = ((bf16[4,64,896]{2,1,0:T(8,128)(2,1)}), bf16[4,64,896]{2,1,0:T(8,128)(2,1)S(1)}, u32[]{:S(2)}, u32[]{:S(2)}) async-start(bf16[4,64,896]{2,1,0:T(8,128)(2,1)} %add.18), calls=%async_computation.5 | async-start | bytes 917504 | tf_op jit(solution)/shard_map/all_to_all | solution.py:354
  116.0 17.6 %copy-start.6 = (bf16[7168]{0:T(1024)(128)(2,1)S(1)}, bf16[7168]{0:T(1024)(128)(2,1)}, u32[]{:S(2)}) copy-start(bf16[7168]{0:T(1024)(128)(2,1)} %param.15) | copy-start | bytes 43012
  129.1 12.1 %all-to-all-start.6 = ((bf16[8,24,896]{2,1,0:T(8,128)(2,1)}), bf16[8,24,896]{2,1,0:T(8,128)(2,1)S(1)}, u32[]{:S(2)}, u32[]{:S(2)}) async-start(bf16[8,24,896]{2,1,0:T(8,128)(2,1)} %bitcast.8), calls=%async_computation.6 | async-start | bytes 688128 | tf_op jit(solution)/shard_map/all_to_all | solution.py:354

commit v10 on v9

--- a/solution.py
+++ b/solution.py
@@ -123,7 +123,7 @@
     best = jnp.max(scores, axis=1, keepdims=True)
     weights = jnp.exp(scores - best)
     total = jnp.sum(weights, axis=1, keepdims=True)
-    latent = dot(weights.astype(bf16), keys[:, :LAT_KV]) / total
+    latent = dot(weights.astype(bf16), keys[:, :LAT_KV]) * (1.0 / total)
     return best, total, latent.astype(bf16)
 
 

time: 143 us -> 143 us (level)
  no operation moved by 1% of the time
where the time goes in v10:
time: 143 us; the launch traced here: 142 us
  blocking collectives  42.4 us (30%)
  starting transfers between devices  42.3 us (30%)
  waiting for transfers between devices  40.9 us (29%)
  Pallas kernels  11.9 us (8%)
  local copies, waits for them, and re-layouts  4.09 us (3%)
    all_to_all x6, waiting for transfers between devices, exchange(): return lax.all_to_all(value, axes, split_axis=0, concat_axis=0, tiled=True)  39.4 us
    all_to_all x6, starting transfers between devices, exchange(): return lax.all_to_all(value, axes, split_axis=0, concat_axis=0, tiled=True)  35.6 us
    all_gather x1, blocking collectives, local(): keys = lax.all_gather(served, 'zq', axis=0, tiled=True)  25.3 us
    all_to_all x1, blocking collectives, exchange(): return lax.all_to_all(value, axes, split_axis=0, concat_axis=0, tiled=True)  17.1 us
    ppermute x1, starting transfers between devices, local(): other_queries = lax.ppermute(all_queries, 'xh', swap)  4.7 us
    unnamed x17, local copies, waits for them, and re-layouts  3.64 us
    pallas_call x1, Pallas kernels, prompt_attention(): pl.pallas_call(attention_kernel, out_shape=jax.ShapeDtypeStruct((NEAR, SE...  3.55 us
  transfers between devices with their start and end apart: 8, of which 7 were waited for; matrix products, arithmetic and copies ran while one was open for 1% of the time, Pallas kernels for 3%

profile of v10, /device:TPU:48, one launch (start us, length us, event | category | flops | bytes accessed | tf_op | source)
XLA Modules:
  0.0 142.3 jit_solution(13006031694729377372)
XLA Ops:
  0.6 0.0 copy-start.7
  0.6 8.6 %all-to-all-start = ((bf16[8,24,576]{2,1,0:T(8,128)(2,1)}), bf16[8,24,576]{2,1,0:T(8,128)(2,1)S(1)}, u32[]{:S(2)}, u32[]{:S(2)}) async-start(bf16[8,24,576]{2,1,0:T(8,128)(2,1)} %bitcast.15), calls=%async_computation | async-start | bytes 491520 | tf_op jit(solution)/shard_map/all_to_all | solution.py:354
  9.2 0.0 copy-start.2
  9.2 0.9 copy-done.2
  10.2 1.6 %spread.1 = (bf16[4,576,128]{2,1,0:T(8,128)(2,1)}, bf16[128,576]{1,0:T(8,128)(2,1)S(1)}) custom-call(bf16[64,2,576]{2,1,0:T(2,128)(2,1)S(1)} %bitcast.10), custom_call_target="tpu_custom_call" | custom-call | bytes 6000000 | tf_op jit(solution)/shard_map/spread/pallas_call | solution.py:97
  11.7 4.0 %all-to-all-done.mine = bf16[8,24,576]{2,1,0:T(8,128)(2,1)S(1)} async-done(((bf16[8,24,576]{2,1,0:T(8,128)(2,1)}), bf16[8,24,576]{2,1,0:T(8,128)(2,1)S(1)}, u32[]{:S(2)}, u32[]{:S(2)}) %all-to-all-start) | async-done | bytes 221216 | tf_op jit(solution)/shard_map/all_to_all | solution.py:354
  15.8 4.2 %all-to-all-start.1 = ((bf16[4,576,128]{2,1,0:T(8,128)(2,1)}), bf16[4,576,128]{2,1,0:T(8,128)(2,1)S(1)}, u32[]{:S(2)}, u32[]{:S(2)}) async-start(bf16[4,576,128]{2,1,0:T(8,128)(2,1)} %get-tuple-element.14), calls=%async_computation.1 | async-start | bytes 1179648 | tf_op jit(solution)/shard_map/all_to_all | solution.py:354
  19.9 0.0 copy-done.7
  19.9 0.1 slice.6
  20.0 0.1 slice.7
  20.1 1.9 %collective-permute-start = (bf16[8,24,576]{2,1,0:T(8,128)(2,1)S(1)}, bf16[8,24,576]{2,1,0:T(8,128)(2,1)S(1)}, u32[]{:S(2)}, u32[]{:S(2)}) collective-permute-start(bf16[8,24,576]{2,1,0:T(8,128)(2,1)S(1)} %all-to-all-done.mine), channel_id=1, source_target_pairs={{0,32},{32,0},{1,33},{33,1},{2,34},{34,2},{3,35},{35,3},{4,36},{36... | collective-permute-start | bytes 663560 | tf_op jit(solution)/shard_map/ppermute | solution.py:378
  22.0 1.5 %collective-permute-done.other = bf16[8,24,576]{2,1,0:T(8,128)(2,1)S(1)} collective-permute-done((bf16[8,24,576]{2,1,0:T(8,128)(2,1)S(1)}, bf16[8,24,576]{2,1,0:T(8,128)(2,1)S(1)}, u32[]{:S(2)}, u32[]{:S(2)}) %collective-permute-start) | collective-permute-done | bytes 221216 | tf_op jit(solution)/shard_map/ppermute | solution.py:378
  23.5 1.4 pick.1
  24.9 3.3 %all-to-all-done.1.mine = bf16[4,576,128]{2,1,0:T(8,128)(2,1)S(1)} async-done(((bf16[4,576,128]{2,1,0:T(8,128)(2,1)}), bf16[4,576,128]{2,1,0:T(8,128)(2,1)S(1)}, u32[]{:S(2)}, u32[]{:S(2)}) %all-to-all-start.1) | async-done | bytes 589856 | tf_op jit(solution)/shard_map/all_to_all | solution.py:354
  28.2 5.9 %all-to-all-start.2 = ((bf16[8,24,576]{2,1,0:T(8,128)(2,1)}), bf16[8,24,576]{2,1,0:T(8,128)(2,1)S(1)}, u32[]{:S(2)}, u32[]{:S(2)}) async-start(bf16[8,24,576]{2,1,0:T(8,128)(2,1)} %pick.1), calls=%async_computation.2 | async-start | bytes 491520 | tf_op jit(solution)/shard_map/all_to_all | solution.py:354
  34.0 4.7 %collective-permute-start.1 = (bf16[4,576,128]{2,1,0:T(8,128)(2,1)S(1)}, bf16[4,576,128]{2,1,0:T(8,128)(2,1)S(1)}, u32[]{:S(2)}, u32[]{:S(2)}) collective-permute-start(bf16[4,576,128]{2,1,0:T(8,128)(2,1)S(1)} %all-to-all-done.1.mine), channel_id=1, source_target_pairs={{0,2},{2,0},{1,3},{3,1},{4,6},{6,4},{5,7},{7,5},{8,10},{10,8},{9,1... | collective-permute-start | bytes 1769480 | tf_op jit(solution)/shard_map/ppermute | solution.py:382
  38.8 2.0 %all-to-all-done.2 = bf16[8,24,576]{2,1,0:T(8,128)(2,1)S(1)} async-done(((bf16[8,24,576]{2,1,0:T(8,128)(2,1)}), bf16[8,24,576]{2,1,0:T(8,128)(2,1)S(1)}, u32[]{:S(2)}, u32[]{:S(2)}) %all-to-all-start.2) | async-done | bytes 221216 | tf_op jit(solution)/shard_map/all_to_all | solution.py:354
  40.7 25.3 %all_gather.3.keys = bf16[768,576]{1,0:T(8,128)(2,1)S(1)} all-gather(bf16[192,576]{1,0:T(8,128)(2,1)S(1)} %bitcast.13), channel_id=1, replica_groups=mesh['y'=8,'core'=2,'zq'=4,'zl'=2,'xh'=2,'xl'=2] {'zq'}, dimensions={0}, use_global_device_ids=true | all-gather | bytes 1105920 | tf_op jit(solution)/shard_map/all_gather | solution.py:384
  66.0 0.0 collective-permute-done.1.other
  66.0 3.6 %prompt_attention.1 = bf16[8,528,128]{2,1,0:T(8,128)(2,1)} custom-call(s32[1]{0:T(128)} %bitcast.1.xh, bf16[4,576,128]{2,1,0:T(8,128)(2,1)S(1)} %all-to-all-done.1.mine, bf16[4,576,128]{2,1,0:T(8,128)(2,1)S(1)} %collective-permute-done.1.other, bf16[768,576]{1,0:T(8,128)(2,1)S(1)} %all_gather.3.keys), custom_call_target="tpu_custom_call" | custom-call | tf_op jit(solution)/shard_map/prompt_attention/pallas_call | solution.py:158
  69.6 0.0 copy-start.5
  69.6 0.0 copy-start.1
  69.6 7.0 %all-to-all-start.3 = ((bf16[8,528,128]{2,1,0:T(8,128)(2,1)}), bf16[8,528,128]{2,1,0:T(8,128)(2,1)S(1)}, u32[]{:S(2)}, u32[]{:S(2)}) async-start(bf16[8,528,128]{2,1,0:T(8,128)(2,1)} %prompt_attention.1), calls=%async_computation.3 | async-start | bytes 2162688 | tf_op jit(solution)/shard_map/all_to_all | solution.py:354
  76.6 0.0 copy-done.5
  76.6 0.5 own_attention.1
  77.1 12.1 %all-to-all-done.3.arrived = bf16[8,528,128]{2,1,0:T(8,128)(2,1)S(1)} async-done(((bf16[8,528,128]{2,1,0:T(8,128)(2,1)}), bf16[8,528,128]{2,1,0:T(8,128)(2,1)S(1)}, u32[]{:S(2)}, u32[]{:S(2)}) %all-to-all-start.3) | async-done | bytes 1081376 | tf_op jit(solution)/shard_map/all_to_all | solution.py:354
  89.2 0.0 copy-done.1
  89.2 0.6 combine.1.head_values
  89.8 0.0 copy-start
  89.8 2.0 %copy-done = bf16[256,7168]{1,0:T(8,128)(2,1)S(1)} copy-done((bf16[256,7168]{1,0:T(8,128)(2,1)S(1)}, bf16[256,7168]{1,0:T(8,128)(2,1)}, u32[]{:S(2)}) %copy-start) | copy-done | bytes 3670040
  91.8 0.7 project.1
  92.5 17.1 %all_to_all.35.arrived = bf16[8,64,896]{2,1,0:T(8,128)(2,1)S(1)} all-to-all(bf16[8,64,896]{2,1,0:T(8,128)(2,1)S(1)} %project.1), channel_id=1, replica_groups=mesh['y'=8,'core'=2,'zq'=4,'zl'=2,'xh'=2,'xl'=2] {'zl','xh','xl'}, dimensions={0} | all-to-all | bytes 1835008 | tf_op jit(solution)/shard_map/all_to_all | solution.py:354
  109.6 0.0 copy-start.3
  109.6 0.0 copy-start.4
  109.6 0.9 add.18
  110.5 5.5 %all-to-all-start.5 = ((bf16[4,64,896]{2,1,0:T(8,128)(2,1)}), bf16[4,64,896]{2,1,0:T(8,128)(2,1)S(1)}, u32[]{:S(2)}, u32[]{:S(2)}) async-start(bf16[4,64,896]{2,1,0:T(8,128)(2,1)} %add.18), calls=%async_computation.5 | async-start | bytes 917504 | tf_op jit(solution)/shard_map/all_to_all | solution.py:354
  116.0 0.0 copy-done.3
  116.0 0.0 copy-done.4
  116.0 0.6 slots.1
  116.6 11.4 %all-to-all-done.5.arrived = bf16[4,64,896]{2,1,0:T(8,128)(2,1)S(1)} async-done(((bf16[4,64,896]{2,1,0:T(8,128)(2,1)}), bf16[4,64,896]{2,1,0:T(8,128)(2,1)S(1)}, u32[]{:S(2)}, u32[]{:S(2)}) %all-to-all-start.5) | async-done | bytes 458784 | tf_op jit(solution)/shard_map/all_to_all | solution.py:354
  128.1 1.0 dispatch.1
  129.1 4.5 %all-to-all-start.6 = ((bf16[8,24,896]{2,1,0:T(8,128)(2,1)}), bf16[8,24,896]{2,1,0:T(8,128)(2,1)S(1)}, u32[]{:S(2)}, u32[]{:S(2)}) async-start(bf16[8,24,896]{2,1,0:T(8,128)(2,1)} %bitcast.8), calls=%async_computation.6 | async-start | bytes 688128 | tf_op jit(solution)/shard_map/all_to_all | solution.py:354
  133.6 0.0 copy-done.6
  133.6 0.1 dynamic-slice_reduce_fusion
  133.8 0.1 reshape.31
  133.8 0.7 copy.12
  134.5 6.6 %all-to-all-done.6.arrived = bf16[8,24,896]{2,1,0:T(8,128)(2,1)S(1)} async-done(((bf16[8,24,896]{2,1,0:T(8,128)(2,1)}), bf16[8,24,896]{2,1,0:T(8,128)(2,1)S(1)}, u32[]{:S(2)}, u32[]{:S(2)}) %all-to-all-start.6) | async-done | bytes 344096 | tf_op jit(solution)/shard_map/all_to_all | solution.py:354
  141.2 1.1 norm.1
  (4 shorter events, 0.1 us)
Async XLA Ops:
  0.6 19.3 %copy-start.7 = (s32[16]{0:T(128)S(1)}, s32[16]{0:T(128)}, u32[]{:S(2)}) copy-start(s32[16]{0:T(128)} %param.10) | copy-start | bytes 196
  0.6 15.1 %all-to-all-start = ((bf16[8,24,576]{2,1,0:T(8,128)(2,1)}), bf16[8,24,576]{2,1,0:T(8,128)(2,1)S(1)}, u32[]{:S(2)}, u32[]{:S(2)}) async-start(bf16[8,24,576]{2,1,0:T(8,128)(2,1)} %bitcast.15), calls=%async_computation | async-start | bytes 491520 | tf_op jit(solution)/shard_map/all_to_all | solution.py:354
  9.2 0.9 copy-start.2
  15.8 12.4 %all-to-all-start.1 = ((bf16[4,576,128]{2,1,0:T(8,128)(2,1)}), bf16[4,576,128]{2,1,0:T(8,128)(2,1)S(1)}, u32[]{:S(2)}, u32[]{:S(2)}) async-start(bf16[4,576,128]{2,1,0:T(8,128)(2,1)} %get-tuple-element.14), calls=%async_computation.1 | async-start | bytes 1179648 | tf_op jit(solution)/shard_map/all_to_all | solution.py:354
  20.1 3.4 %collective-permute-start = (bf16[8,24,576]{2,1,0:T(8,128)(2,1)S(1)}, bf16[8,24,576]{2,1,0:T(8,128)(2,1)S(1)}, u32[]{:S(2)}, u32[]{:S(2)}) collective-permute-start(bf16[8,24,576]{2,1,0:T(8,128)(2,1)S(1)} %all-to-all-done.mine), channel_id=1, source_target_pairs={{0,32},{32,0},{1,33},{33,1},{2,34},{34,2},{3,35},{35,3},{4,36},{36... | collective-permute-start | bytes 663560 | tf_op jit(solution)/shard_map/ppermute | solution.py:378
  28.2 12.6 %all-to-all-start.2 = ((bf16[8,24,576]{2,1,0:T(8,128)(2,1)}), bf16[8,24,576]{2,1,0:T(8,128)(2,1)S(1)}, u32[]{:S(2)}, u32[]{:S(2)}) async-start(bf16[8,24,576]{2,1,0:T(8,128)(2,1)} %pick.1), calls=%async_computation.2 | async-start | bytes 491520 | tf_op jit(solution)/shard_map/all_to_all | solution.py:354
  34.0 32.0 %collective-permute-start.1 = (bf16[4,576,128]{2,1,0:T(8,128)(2,1)S(1)}, bf16[4,576,128]{2,1,0:T(8,128)(2,1)S(1)}, u32[]{:S(2)}, u32[]{:S(2)}) collective-permute-start(bf16[4,576,128]{2,1,0:T(8,128)(2,1)S(1)} %all-to-all-done.1.mine), channel_id=1, source_target_pairs={{0,2},{2,0},{1,3},{3,1},{4,6},{6,4},{5,7},{7,5},{8,10},{10,8},{9,1... | collective-permute-start | bytes 1769480 | tf_op jit(solution)/shard_map/ppermute | solution.py:382
  69.6 7.0 %copy-start.5 = (bf16[1,16,4,576]{3,2,1,0:T(4,128)(2,1)S(1)}, bf16[1,16,4,576]{3,2,1,0:T(4,128)(2,1)}, u32[]{:S(2)}) copy-start(bf16[1,16,4,576]{3,2,1,0:T(4,128)(2,1)} %param.12) | copy-start | bytes 221188
  69.6 19.6 %copy-start.1 = (bf16[2,512,128]{2,1,0:T(8,128)(2,1)S(1)}, bf16[2,512,128]{2,1,0:T(8,128)(2,1)}, u32[]{:S(2)}) copy-start(bf16[2,512,128]{2,1,0:T(8,128)(2,1)} %value_up.1) | copy-start | bytes 786436
  69.6 19.6 %all-to-all-start.3 = ((bf16[8,528,128]{2,1,0:T(8,128)(2,1)}), bf16[8,528,128]{2,1,0:T(8,128)(2,1)S(1)}, u32[]{:S(2)}, u32[]{:S(2)}) async-start(bf16[8,528,128]{2,1,0:T(8,128)(2,1)} %prompt_attention.1), calls=%async_computation.3 | async-start | bytes 2162688 | tf_op jit(solution)/shard_map/all_to_all | solution.py:354
  89.8 2.1 %copy-start = (bf16[256,7168]{1,0:T(8,128)(2,1)S(1)}, bf16[256,7168]{1,0:T(8,128)(2,1)}, u32[]{:S(2)}) copy-start(bf16[256,7168]{1,0:T(8,128)(2,1)} %weight.1) | copy-start | bytes 11010052
  109.6 6.4 %copy-start.3 = (s32[64,8]{0,1:T(8,128)S(1)}, s32[64,8]{0,1:T(8,128)}, u32[]{:S(2)}) copy-start(s32[64,8]{0,1:T(8,128)} %param.16) | copy-start | bytes 6148
  109.6 6.4 %copy-start.4 = (f32[64,8]{0,1:T(8,128)S(1)}, f32[64,8]{0,1:T(8,128)}, u32[]{:S(2)}) copy-start(f32[64,8]{0,1:T(8,128)} %param.17) | copy-start | bytes 6148
  110.5 17.6 %all-to-all-start.5 = ((bf16[4,64,896]{2,1,0:T(8,128)(2,1)}), bf16[4,64,896]{2,1,0:T(8,128)(2,1)S(1)}, u32[]{:S(2)}, u32[]{:S(2)}) async-start(bf16[4,64,896]{2,1,0:T(8,128)(2,1)} %add.18), calls=%async_computation.5 | async-start | bytes 917504 | tf_op jit(solution)/shard_map/all_to_all | solution.py:354
  116.0 17.6 %copy-start.6 = (bf16[7168]{0:T(1024)(128)(2,1)S(1)}, bf16[7168]{0:T(1024)(128)(2,1)}, u32[]{:S(2)}) copy-start(bf16[7168]{0:T(1024)(128)(2,1)} %param.15) | copy-start | bytes 43012
  129.1 12.1 %all-to-all-start.6 = ((bf16[8,24,896]{2,1,0:T(8,128)(2,1)}), bf16[8,24,896]{2,1,0:T(8,128)(2,1)S(1)}, u32[]{:S(2)}, u32[]{:S(2)}) async-start(bf16[8,24,896]{2,1,0:T(8,128)(2,1)} %bitcast.8), calls=%async_computation.6 | async-start | bytes 688128 | tf_op jit(solution)/shard_map/all_to_all | solution.py:354

commit v11 on v10

--- a/solution.py
+++ b/solution.py
@@ -55,26 +55,30 @@
     return jnp.transpose(jnp.broadcast_to(column, (MINE, 128)))[:1]
 
 
-def pick_kernel(core, wanted, mine, other, out):
+def pick_kernel(core, wanted, mine, other, out, sems):
     for y in range(NY):
         prompt = wanted[y]
         row = lax.shift_right_logical(prompt, 1)
 
         @pl.when((prompt & 1) == core[0])
         def _():
-            out[y] = mine[row]
+            pltpu.make_async_copy(mine.at[row], out.at[y], sems.at[y]).start()
 
         @pl.when((prompt & 1) != core[0])
         def _():
-            out[y] = other[row]
+            pltpu.make_async_copy(other.at[row], out.at[y], sems.at[y]).start()
+
+    for y in range(NY):
+        pltpu.make_async_copy(mine.at[0], out.at[y], sems.at[y]).wait()
 
 
 def pick(core, wanted, mine, other):
     return pl.pallas_call(
         pick_kernel,
         out_shape=jax.ShapeDtypeStruct(mine.shape, mine.dtype),
-        in_specs=[SMEM, SMEM, VMEM, VMEM],
-        out_specs=VMEM,
+        in_specs=[SMEM, SMEM] + [pl.BlockSpec(memory_space=pl.ANY)] * 2,
+        out_specs=pl.BlockSpec(memory_space=pl.ANY),
+        scratch_shapes=[pltpu.SemaphoreType.DMA((NY,))],
         compiler_params=params(),
         name="pick",
     )(core, wanted, mine, other)

time: 143 us -> 143 us (level)
  starting transfers between devices: 42.3 us -> 40.3 us
  blocking collectives: 42.4 us -> 43.9 us
    all_to_all x6, starting transfers between devices: 35.6 us -> 33.6 us  [exchange(): return lax.all_to_all(value, axes, split_axis=0, concat_axis=0, tiled=True)]
where the time goes in v11:
time: 143 us; the launch traced here: 142 us
  blocking collectives  43.9 us (31%)
  waiting for transfers between devices  41.5 us (29%)
  starting transfers between devices  40.3 us (28%)
  Pallas kernels  11.8 us (8%)
  local copies, waits for them, and re-layouts  4.09 us (3%)
    all_to_all x6, waiting for transfers between devices, exchange(): return lax.all_to_all(value, axes, split_axis=0, concat_axis=0, tiled=True)  40 us
    all_to_all x6, starting transfers between devices, exchange(): return lax.all_to_all(value, axes, split_axis=0, concat_axis=0, tiled=True)  33.6 us
    all_gather x1, blocking collectives, local(): keys = lax.all_gather(served, 'zq', axis=0, tiled=True)  26.4 us
    all_to_all x1, blocking collectives, exchange(): return lax.all_to_all(value, axes, split_axis=0, concat_axis=0, tiled=True)  17.5 us
    ppermute x1, starting transfers between devices, local(): other_queries = lax.ppermute(all_queries, 'xh', swap)  4.7 us
    unnamed x17, local copies, waits for them, and re-layouts  3.64 us
    pallas_call x1, Pallas kernels, prompt_attention(): pl.pallas_call(attention_kernel, out_shape=jax.ShapeDtypeStruct((NEAR, SE...  3.55 us
  transfers between devices with their start and end apart: 8, of which 7 were waited for; matrix products, arithmetic and copies ran while one was open for 1% of the time, Pallas kernels for 3%

profile of v11, /device:TPU:48, one launch (start us, length us, event | category | flops | bytes accessed | tf_op | source)
XLA Modules:
  0.0 142.3 jit_solution(1420640583458521283)
XLA Ops:
  0.6 0.0 copy-start.7
  0.6 8.6 %all-to-all-start = ((bf16[8,24,576]{2,1,0:T(8,128)(2,1)}), bf16[8,24,576]{2,1,0:T(8,128)(2,1)S(1)}, u32[]{:S(2)}, u32[]{:S(2)}) async-start(bf16[8,24,576]{2,1,0:T(8,128)(2,1)} %bitcast.15), calls=%async_computation | async-start | bytes 491520 | tf_op jit(solution)/shard_map/all_to_all | solution.py:358
  9.2 0.0 copy-start.2
  9.2 0.9 copy-done.2
  10.2 1.6 %spread.1 = (bf16[4,576,128]{2,1,0:T(8,128)(2,1)}, bf16[128,576]{1,0:T(8,128)(2,1)S(1)}) custom-call(bf16[64,2,576]{2,1,0:T(2,128)(2,1)S(1)} %bitcast.10), custom_call_target="tpu_custom_call" | custom-call | bytes 6000000 | tf_op jit(solution)/shard_map/spread/pallas_call | solution.py:101
  11.7 4.0 %all-to-all-done.mine = bf16[8,24,576]{2,1,0:T(8,128)(2,1)S(1)} async-done(((bf16[8,24,576]{2,1,0:T(8,128)(2,1)}), bf16[8,24,576]{2,1,0:T(8,128)(2,1)S(1)}, u32[]{:S(2)}, u32[]{:S(2)}) %all-to-all-start) | async-done | bytes 221216 | tf_op jit(solution)/shard_map/all_to_all | solution.py:358
  15.8 4.2 %all-to-all-start.1 = ((bf16[4,576,128]{2,1,0:T(8,128)(2,1)}), bf16[4,576,128]{2,1,0:T(8,128)(2,1)S(1)}, u32[]{:S(2)}, u32[]{:S(2)}) async-start(bf16[4,576,128]{2,1,0:T(8,128)(2,1)} %get-tuple-element.14), calls=%async_computation.1 | async-start | bytes 1179648 | tf_op jit(solution)/shard_map/all_to_all | solution.py:358
  19.9 0.0 copy-done.7
  19.9 0.1 slice.6
  20.0 0.1 slice.7
  20.1 1.9 %collective-permute-start = (bf16[8,24,576]{2,1,0:T(8,128)(2,1)S(1)}, bf16[8,24,576]{2,1,0:T(8,128)(2,1)S(1)}, u32[]{:S(2)}, u32[]{:S(2)}) collective-permute-start(bf16[8,24,576]{2,1,0:T(8,128)(2,1)S(1)} %all-to-all-done.mine), channel_id=1, source_target_pairs={{0,32},{32,0},{1,33},{33,1},{2,34},{34,2},{3,35},{35,3},{4,36},{36... | collective-permute-start | bytes 663560 | tf_op jit(solution)/shard_map/ppermute | solution.py:382
  22.0 1.5 %collective-permute-done.other = bf16[8,24,576]{2,1,0:T(8,128)(2,1)S(1)} collective-permute-done((bf16[8,24,576]{2,1,0:T(8,128)(2,1)S(1)}, bf16[8,24,576]{2,1,0:T(8,128)(2,1)S(1)}, u32[]{:S(2)}, u32[]{:S(2)}) %collective-permute-start) | collective-permute-done | bytes 221216 | tf_op jit(solution)/shard_map/ppermute | solution.py:382
  23.5 1.3 pick.1
  24.8 3.3 %all-to-all-done.1.mine = bf16[4,576,128]{2,1,0:T(8,128)(2,1)S(1)} async-done(((bf16[4,576,128]{2,1,0:T(8,128)(2,1)}), bf16[4,576,128]{2,1,0:T(8,128)(2,1)S(1)}, u32[]{:S(2)}, u32[]{:S(2)}) %all-to-all-start.1) | async-done | bytes 589856 | tf_op jit(solution)/shard_map/all_to_all | solution.py:358
  28.2 5.9 %all-to-all-start.2 = ((bf16[8,24,576]{2,1,0:T(8,128)(2,1)}), bf16[8,24,576]{2,1,0:T(8,128)(2,1)S(1)}, u32[]{:S(2)}, u32[]{:S(2)}) async-start(bf16[8,24,576]{2,1,0:T(8,128)(2,1)} %pick.1), calls=%async_computation.2 | async-start | bytes 491520 | tf_op jit(solution)/shard_map/all_to_all | solution.py:358
  34.0 4.7 %collective-permute-start.1 = (bf16[4,576,128]{2,1,0:T(8,128)(2,1)S(1)}, bf16[4,576,128]{2,1,0:T(8,128)(2,1)S(1)}, u32[]{:S(2)}, u32[]{:S(2)}) collective-permute-start(bf16[4,576,128]{2,1,0:T(8,128)(2,1)S(1)} %all-to-all-done.1.mine), channel_id=1, source_target_pairs={{0,2},{2,0},{1,3},{3,1},{4,6},{6,4},{5,7},{7,5},{8,10},{10,8},{9,1... | collective-permute-start | bytes 1769480 | tf_op jit(solution)/shard_map/ppermute | solution.py:386
  38.8 2.0 %all-to-all-done.2 = bf16[8,24,576]{2,1,0:T(8,128)(2,1)S(1)} async-done(((bf16[8,24,576]{2,1,0:T(8,128)(2,1)}), bf16[8,24,576]{2,1,0:T(8,128)(2,1)S(1)}, u32[]{:S(2)}, u32[]{:S(2)}) %all-to-all-start.2) | async-done | bytes 221216 | tf_op jit(solution)/shard_map/all_to_all | solution.py:358
  40.7 26.4 %all_gather.3.keys = bf16[768,576]{1,0:T(8,128)(2,1)S(1)} all-gather(bf16[192,576]{1,0:T(8,128)(2,1)S(1)} %bitcast.13), channel_id=1, replica_groups=mesh['y'=8,'core'=2,'zq'=4,'zl'=2,'xh'=2,'xl'=2] {'zq'}, dimensions={0}, use_global_device_ids=true | all-gather | bytes 1105920 | tf_op jit(solution)/shard_map/all_gather | solution.py:388
  67.2 0.0 collective-permute-done.1.other
  67.2 3.6 %prompt_attention.1 = bf16[8,528,128]{2,1,0:T(8,128)(2,1)} custom-call(s32[1]{0:T(128)} %bitcast.1.xh, bf16[4,576,128]{2,1,0:T(8,128)(2,1)S(1)} %all-to-all-done.1.mine, bf16[4,576,128]{2,1,0:T(8,128)(2,1)S(1)} %collective-permute-done.1.other, bf16[768,576]{1,0:T(8,128)(2,1)S(1)} %all_gather.3.keys), custom_call_target="tpu_custom_call" | custom-call | tf_op jit(solution)/shard_map/prompt_attention/pallas_call | solution.py:162
  70.7 0.0 copy-start.5
  70.7 0.0 copy-start.1
  70.7 5.3 %all-to-all-start.3 = ((bf16[8,528,128]{2,1,0:T(8,128)(2,1)}), bf16[8,528,128]{2,1,0:T(8,128)(2,1)S(1)}, u32[]{:S(2)}, u32[]{:S(2)}) async-start(bf16[8,528,128]{2,1,0:T(8,128)(2,1)} %prompt_attention.1), calls=%async_computation.3 | async-start | bytes 2162688 | tf_op jit(solution)/shard_map/all_to_all | solution.py:358
  76.0 0.0 copy-done.5
  76.1 0.5 own_attention.1
  76.6 12.6 %all-to-all-done.3.arrived = bf16[8,528,128]{2,1,0:T(8,128)(2,1)S(1)} async-done(((bf16[8,528,128]{2,1,0:T(8,128)(2,1)}), bf16[8,528,128]{2,1,0:T(8,128)(2,1)S(1)}, u32[]{:S(2)}, u32[]{:S(2)}) %all-to-all-start.3) | async-done | bytes 1081376 | tf_op jit(solution)/shard_map/all_to_all | solution.py:358
  89.2 0.0 copy-done.1
  89.2 0.6 combine.1.head_values
  89.8 0.0 copy-start
  89.8 2.0 %copy-done = bf16[256,7168]{1,0:T(8,128)(2,1)S(1)} copy-done((bf16[256,7168]{1,0:T(8,128)(2,1)S(1)}, bf16[256,7168]{1,0:T(8,128)(2,1)}, u32[]{:S(2)}) %copy-start) | copy-done | bytes 3670040
  91.9 0.7 project.1
  92.5 17.5 %all_to_all.35.arrived = bf16[8,64,896]{2,1,0:T(8,128)(2,1)S(1)} all-to-all(bf16[8,64,896]{2,1,0:T(8,128)(2,1)S(1)} %project.1), channel_id=1, replica_groups=mesh['y'=8,'core'=2,'zq'=4,'zl'=2,'xh'=2,'xl'=2] {'zl','xh','xl'}, dimensions={0} | all-to-all | bytes 1835008 | tf_op jit(solution)/shard_map/all_to_all | solution.py:358
  110.0 0.0 copy-start.3
  110.0 0.0 copy-start.4
  110.0 0.9 add.18
  110.9 5.1 %all-to-all-start.5 = ((bf16[4,64,896]{2,1,0:T(8,128)(2,1)}), bf16[4,64,896]{2,1,0:T(8,128)(2,1)S(1)}, u32[]{:S(2)}, u32[]{:S(2)}) async-start(bf16[4,64,896]{2,1,0:T(8,128)(2,1)} %add.18), calls=%async_computation.5 | async-start | bytes 917504 | tf_op jit(solution)/shard_map/all_to_all | solution.py:358
  116.1 0.0 copy-done.3
  116.1 0.0 copy-done.4
  116.1 0.6 slots.1
  116.7 11.4 %all-to-all-done.5.arrived = bf16[4,64,896]{2,1,0:T(8,128)(2,1)S(1)} async-done(((bf16[4,64,896]{2,1,0:T(8,128)(2,1)}), bf16[4,64,896]{2,1,0:T(8,128)(2,1)S(1)}, u32[]{:S(2)}, u32[]{:S(2)}) %all-to-all-start.5) | async-done | bytes 458784 | tf_op jit(solution)/shard_map/all_to_all | solution.py:358
  128.1 1.0 dispatch.1
  129.1 4.5 %all-to-all-start.6 = ((bf16[8,24,896]{2,1,0:T(8,128)(2,1)}), bf16[8,24,896]{2,1,0:T(8,128)(2,1)S(1)}, u32[]{:S(2)}, u32[]{:S(2)}) async-start(bf16[8,24,896]{2,1,0:T(8,128)(2,1)} %bitcast.8), calls=%async_computation.6 | async-start | bytes 688128 | tf_op jit(solution)/shard_map/all_to_all | solution.py:358
  133.6 0.0 copy-done.6
  133.7 0.1 dynamic-slice_reduce_fusion
  133.8 0.1 reshape.31
  133.9 0.7 copy.12
  134.5 6.6 %all-to-all-done.6.arrived = bf16[8,24,896]{2,1,0:T(8,128)(2,1)S(1)} async-done(((bf16[8,24,896]{2,1,0:T(8,128)(2,1)}), bf16[8,24,896]{2,1,0:T(8,128)(2,1)S(1)}, u32[]{:S(2)}, u32[]{:S(2)}) %all-to-all-start.6) | async-done | bytes 344096 | tf_op jit(solution)/shard_map/all_to_all | solution.py:358
  141.2 1.1 norm.1
  (4 shorter events, 0.1 us)
Async XLA Ops:
  0.6 19.3 %copy-start.7 = (s32[16]{0:T(128)S(1)}, s32[16]{0:T(128)}, u32[]{:S(2)}) copy-start(s32[16]{0:T(128)} %param.10) | copy-start | bytes 196
  0.6 15.1 %all-to-all-start = ((bf16[8,24,576]{2,1,0:T(8,128)(2,1)}), bf16[8,24,576]{2,1,0:T(8,128)(2,1)S(1)}, u32[]{:S(2)}, u32[]{:S(2)}) async-start(bf16[8,24,576]{2,1,0:T(8,128)(2,1)} %bitcast.15), calls=%async_computation | async-start | bytes 491520 | tf_op jit(solution)/shard_map/all_to_all | solution.py:358
  9.2 0.9 copy-start.2
  15.8 12.4 %all-to-all-start.1 = ((bf16[4,576,128]{2,1,0:T(8,128)(2,1)}), bf16[4,576,128]{2,1,0:T(8,128)(2,1)S(1)}, u32[]{:S(2)}, u32[]{:S(2)}) async-start(bf16[4,576,128]{2,1,0:T(8,128)(2,1)} %get-tuple-element.14), calls=%async_computation.1 | async-start | bytes 1179648 | tf_op jit(solution)/shard_map/all_to_all | solution.py:358
  20.1 3.4 %collective-permute-start = (bf16[8,24,576]{2,1,0:T(8,128)(2,1)S(1)}, bf16[8,24,576]{2,1,0:T(8,128)(2,1)S(1)}, u32[]{:S(2)}, u32[]{:S(2)}) collective-permute-start(bf16[8,24,576]{2,1,0:T(8,128)(2,1)S(1)} %all-to-all-done.mine), channel_id=1, source_target_pairs={{0,32},{32,0},{1,33},{33,1},{2,34},{34,2},{3,35},{35,3},{4,36},{36... | collective-permute-start | bytes 663560 | tf_op jit(solution)/shard_map/ppermute | solution.py:382
  28.2 12.6 %all-to-all-start.2 = ((bf16[8,24,576]{2,1,0:T(8,128)(2,1)}), bf16[8,24,576]{2,1,0:T(8,128)(2,1)S(1)}, u32[]{:S(2)}, u32[]{:S(2)}) async-start(bf16[8,24,576]{2,1,0:T(8,128)(2,1)} %pick.1), calls=%async_computation.2 | async-start | bytes 491520 | tf_op jit(solution)/shard_map/all_to_all | solution.py:358
  34.0 33.1 %collective-permute-start.1 = (bf16[4,576,128]{2,1,0:T(8,128)(2,1)S(1)}, bf16[4,576,128]{2,1,0:T(8,128)(2,1)S(1)}, u32[]{:S(2)}, u32[]{:S(2)}) collective-permute-start(bf16[4,576,128]{2,1,0:T(8,128)(2,1)S(1)} %all-to-all-done.1.mine), channel_id=1, source_target_pairs={{0,2},{2,0},{1,3},{3,1},{4,6},{6,4},{5,7},{7,5},{8,10},{10,8},{9,1... | collective-permute-start | bytes 1769480 | tf_op jit(solution)/shard_map/ppermute | solution.py:386
  70.7 5.3 %copy-start.5 = (bf16[1,16,4,576]{3,2,1,0:T(4,128)(2,1)S(1)}, bf16[1,16,4,576]{3,2,1,0:T(4,128)(2,1)}, u32[]{:S(2)}) copy-start(bf16[1,16,4,576]{3,2,1,0:T(4,128)(2,1)} %param.12) | copy-start | bytes 221188
  70.7 18.5 %copy-start.1 = (bf16[2,512,128]{2,1,0:T(8,128)(2,1)S(1)}, bf16[2,512,128]{2,1,0:T(8,128)(2,1)}, u32[]{:S(2)}) copy-start(bf16[2,512,128]{2,1,0:T(8,128)(2,1)} %value_up.1) | copy-start | bytes 786436
  70.7 18.5 %all-to-all-start.3 = ((bf16[8,528,128]{2,1,0:T(8,128)(2,1)}), bf16[8,528,128]{2,1,0:T(8,128)(2,1)S(1)}, u32[]{:S(2)}, u32[]{:S(2)}) async-start(bf16[8,528,128]{2,1,0:T(8,128)(2,1)} %prompt_attention.1), calls=%async_computation.3 | async-start | bytes 2162688 | tf_op jit(solution)/shard_map/all_to_all | solution.py:358
  89.8 2.1 %copy-start = (bf16[256,7168]{1,0:T(8,128)(2,1)S(1)}, bf16[256,7168]{1,0:T(8,128)(2,1)}, u32[]{:S(2)}) copy-start(bf16[256,7168]{1,0:T(8,128)(2,1)} %weight.1) | copy-start | bytes 11010052
  110.0 6.0 %copy-start.3 = (s32[64,8]{0,1:T(8,128)S(1)}, s32[64,8]{0,1:T(8,128)}, u32[]{:S(2)}) copy-start(s32[64,8]{0,1:T(8,128)} %param.16) | copy-start | bytes 6148
  110.0 6.0 %copy-start.4 = (f32[64,8]{0,1:T(8,128)S(1)}, f32[64,8]{0,1:T(8,128)}, u32[]{:S(2)}) copy-start(f32[64,8]{0,1:T(8,128)} %param.17) | copy-start | bytes 6148
  110.9 17.2 %all-to-all-start.5 = ((bf16[4,64,896]{2,1,0:T(8,128)(2,1)}), bf16[4,64,896]{2,1,0:T(8,128)(2,1)S(1)}, u32[]{:S(2)}, u32[]{:S(2)}) async-start(bf16[4,64,896]{2,1,0:T(8,128)(2,1)} %add.18), calls=%async_computation.5 | async-start | bytes 917504 | tf_op jit(solution)/shard_map/all_to_all | solution.py:358
  116.1 17.6 %copy-start.6 = (bf16[7168]{0:T(1024)(128)(2,1)S(1)}, bf16[7168]{0:T(1024)(128)(2,1)}, u32[]{:S(2)}) copy-start(bf16[7168]{0:T(1024)(128)(2,1)} %param.15) | copy-start | bytes 43012
  129.1 12.1 %all-to-all-start.6 = ((bf16[8,24,896]{2,1,0:T(8,128)(2,1)}), bf16[8,24,896]{2,1,0:T(8,128)(2,1)S(1)}, u32[]{:S(2)}, u32[]{:S(2)}) async-start(bf16[8,24,896]{2,1,0:T(8,128)(2,1)} %bitcast.8), calls=%async_computation.6 | async-start | bytes 688128 | tf_op jit(solution)/shard_map/all_to_all | solution.py:358
